TPU v7x, 128 devices: a whole 4x4x4 slice. The times are simulated.
128 devices in a mesh: pop: 16 (over y_lo, x, core), tp: 8 (over z, y_hi).
Axes of the slice: x: 4, y: 4 (y_hi: 2, y_lo: 2; y = y_hi * 2 + y_lo), z: 4, core: 2. Of those that a mesh axis runs over, the one named last changes fastest.
Arguments:
- hidden_units: bfloat16 [16, 128, 18944], P('pop', None, 'tp'), may hold values from -6 to 6
- residual: bfloat16 [16, 128, 3584], P('pop'), may hold values from -6 to 6
- down_weight: bfloat16 [18944, 3584], P('tp'), may hold values from -0.046875 to 0.046875
- norm_gain: float32 [3584], replicated, may hold values from 0.5 to 1.5
- head: bfloat16 [3584, 98304], P(None, ('pop', 'tp')), may hold values from -16 to 16
- labels: int32 [16, 128], P('pop'), may hold values from 0 to 98303
- answer_start: int32 [16], replicated, may hold values from 32 to 96
- seeds: int32 [16], replicated, may hold values from 0 to 1073741823
- signs: int32 [32], replicated, may hold values from -1 to 1, as said below
Outputs:
- fitness: float32 [32], replicated
- update_direction: float32 [18944, 3584], P(('pop', 'tp'))
Inputs may be any that keep to these rules, and one draw needn't show every extreme that they name: Members 2 p and 2 p + 1 carry opposite signs.
All inputs are finite; a program needn't handle non-finite values.
Results may differ from a plain program's by a relative error of at most 0.007.
The roundings to bfloat16 on the way count: a program that leaves them out, or rounds other values in their place, can miss the bound.
Values may be sent and summed in bfloat16 or wider, within the bound.
No kernel may reach another device: no remote copies, remote signals or barrier semaphores. Data moves between devices by JAX's collectives and lax.ppermute only.
A program may use at most 192 MiB of HBM per device.

v0:
```python
import jax
import jax.numpy as jnp
from jax import lax
from jax.sharding import PartitionSpec as P

FF = 18944


root_three = 1.7320508075688772


def merged(array, axis, combine):
    everything = jax.tree.map(lambda part: lax.all_gather(part, axis), array)
    leading = jax.tree.map(lambda part: part[0], everything)

    def turn(k, so_far):
        return combine(so_far, jax.tree.map(lambda part: part[k], everything))

    return lax.fori_loop(1, lax.axis_size(axis), turn, leading)


def mix_bits(hashed):
    hashed = jnp.bitwise_xor(hashed, lax.shift_right_logical(hashed, jnp.full_like(hashed, 15)))
    hashed = hashed * jnp.int32(739982445)
    hashed = jnp.bitwise_xor(hashed, lax.shift_right_logical(hashed, jnp.full_like(hashed, 12)))
    hashed = hashed * jnp.int32(695872825)
    hashed = jnp.bitwise_xor(hashed, lax.shift_right_logical(hashed, jnp.full_like(hashed, 15)))
    return hashed


def noise_block(pair_seed, first_row, row_count, col_count):
    row_ids = (first_row + jnp.arange(row_count, dtype=jnp.int32))[:, None]
    col_ids = jnp.arange(col_count, dtype=jnp.int32)[None, :]
    hashed = row_ids * jnp.int32(col_count) + col_ids + pair_seed * jnp.int32(1540483477)
    hashed = mix_bits(jnp.bitwise_xor(mix_bits(hashed), jnp.int32(1013904223)))
    uniform_bits = jnp.bitwise_and(hashed, jnp.int32(16777215)).astype(jnp.float32)
    return (((uniform_bits + 0.5) * (2.0 / 16777216.0) - 1.0) * root_three).astype(jnp.bfloat16)


def combine_stats(first_stats, second_stats):
    joint_max = jnp.maximum(first_stats[0], second_stats[0])
    joint_total = first_stats[1] * jnp.exp(first_stats[0] - joint_max) + second_stats[1] * jnp.exp(
        second_stats[0] - joint_max
    )
    return (joint_max, joint_total, first_stats[2] + second_stats[2])


def local(hidden_units, residual, down_weight, norm_gain, head, labels, answer_start, seeds, signs):
    pop_count = lax.axis_size("pop")
    tp_count = lax.axis_size("tp")
    pop_at = lax.axis_index("pop")
    tp_at = lax.axis_index("tp")
    tokens_here = hidden_units.shape[1]
    model_width = residual.shape[2]
    local_units = down_weight.shape[0]
    vocab_local = head.shape[1]
    noise_scale = 0.25 * FF ** (-0.5)
    pair_seed = lax.dynamic_index_in_dim(seeds, pop_at, 0, keepdims=False)
    noise_rows = noise_block(pair_seed, tp_at * local_units, local_units, model_width)
    hidden_rows = hidden_units[0]
    pair_signs = lax.dynamic_slice_in_dim(signs, pop_at * 2, 2).astype(jnp.float32)
    vocab_ids = (pop_at * tp_count + tp_at) * vocab_local + jnp.arange(vocab_local, dtype=jnp.int32)
    positions = jnp.arange(tokens_here, dtype=jnp.int32)
    base_out = jnp.dot(hidden_rows, down_weight, preferred_element_type=jnp.float32)
    probe_out = jnp.dot(hidden_rows, noise_rows, preferred_element_type=jnp.float32)
    summed = lax.psum(jnp.concatenate([base_out, probe_out], axis=1), "tp")
    base_out = summed[:, :model_width]
    probe_out = summed[:, model_width:]
    layer_out = (
        residual[0].astype(jnp.float32)[None]
        + base_out[None]
        + pair_signs[:, None, None] * noise_scale * probe_out[None]
    )
    mean_square = jnp.mean(layer_out * layer_out, axis=2, keepdims=True)
    normed = (layer_out * lax.rsqrt(mean_square + 1e-06) * norm_gain).astype(jnp.bfloat16)
    normed = normed.reshape(2 * summed.shape[0], model_width)
    row_states = lax.all_gather(normed, "pop", axis=0, tiled=True)
    row_labels = lax.all_gather(jnp.concatenate([labels[0], labels[0]]), "pop", axis=0, tiled=True)
    logits = jnp.dot(row_states, head, preferred_element_type=jnp.float32)
    row_max = jnp.max(logits, axis=1)
    row_total = jnp.sum(jnp.exp(logits - row_max[:, None]), axis=1)
    target = jnp.sum(jnp.where(row_labels[:, None] == vocab_ids[None, :], logits, 0.0), axis=1)
    row_stats = tuple((updated for updated in (row_max, row_total, target)))
    sources = (
        lax.all_to_all(
            row_stats[0].reshape(pop_count, 2 * tokens_here),
            "pop",
            split_axis=0,
            concat_axis=0,
            tiled=True,
        ),
        lax.all_to_all(
            row_stats[1].reshape(pop_count, 2 * tokens_here),
            "pop",
            split_axis=0,
            concat_axis=0,
            tiled=True,
        ),
        lax.all_to_all(
            row_stats[2].reshape(pop_count, 2 * tokens_here),
            "pop",
            split_axis=0,
            concat_axis=0,
            tiled=True,
        ),
    )
    column_max = jnp.max(sources[0], axis=0)
    column_total = jnp.sum(sources[1] * jnp.exp(sources[0] - column_max[None, :]), axis=0)
    column_target = jnp.sum(sources[2], axis=0)
    own_stats = merged((column_max, column_total, column_target), "tp", combine_stats)
    log_prob = (own_stats[2] - own_stats[0] - jnp.log(own_stats[1])).reshape(1, 2, tokens_here)[0]
    own_start = lax.dynamic_index_in_dim(answer_start, pop_at, 0, keepdims=False)
    answer_mask = (positions >= own_start).astype(jnp.float32)
    fitness_own = jnp.sum(log_prob * answer_mask[None, :], axis=1) / (
        tokens_here - own_start
    ).astype(jnp.float32)
    fitness = lax.all_gather(fitness_own, "pop", axis=0, tiled=True)
    fitness_gap = jnp.sum((fitness * signs.astype(jnp.float32)).reshape(pop_count, 2), axis=1)
    out_rows = FF // (pop_count * tp_count)
    out_first = (pop_at * tp_count + tp_at) * out_rows

    def add_pair(pair_index, running):
        term = noise_block(seeds[pair_index], out_first, out_rows, model_width).astype(jnp.float32)
        return running + fitness_gap[pair_index] * term

    update_direction = lax.fori_loop(
        0, pop_count, add_pair, jnp.zeros((out_rows, model_width), jnp.float32)
    )
    return (fitness, update_direction)


def solution(mesh):
    return jax.shard_map(
        local,
        mesh=mesh,
        in_specs=(
            P("pop", None, "tp"),
            P("pop", None, None),
            P("tp", None),
            P(),
            P(None, ("pop", "tp")),
            P("pop", None),
            P(),
            P(),
            P(),
        ),
        out_specs=(P(), P(("pop", "tp"), None)),
        check_vma=False,
    )
```

profile of v0, /device:TPU:1, one launch (start us, length us, event | category | flops | bytes accessed | tf_op | source)
XLA Modules:
  0.0 609.7 jit_solution(17183387149484159719)
XLA Ops:
  9.2 8.4 %fusion.34 = f32[128,3584]{1,0:T(8,128)S(1)} fusion(bf16[2368,3584]{1,0:T(8,128)(2,1)} %param.15, bf16[1,128,2368]{1,2,0:T(8,128)(2,1)S(1)} %copy-done), kind=kOutput, calls=%fused_computation.55 | convolution fusion | flops 2172649472 | bytes 19415040 | tf_op jit(solution)/shard_map/dot_general | solution.py:64
  17.6 31.0 %fusion.26 = f32[128,3584]{1,0:T(8,128)S(1)} fusion(s32[]{:T(128)} %bitcast.5, s32[2368]{0:T(1024)S(1)} %add_multiply_fusion.1, bf16[1,128,2368]{1,2,0:T(8,128)(2,1)S(1)} %copy-done), kind=kOutput, calls=%fused_computation.45 | convolution fusion | flops 2393309184 | bytes 2450692 | tf_op jit(solution)/shard_map/dot_general | solution.py:65
  51.5 168.0 %all-reduce.3.cloned.1.call-done = f32[128,7168]{1,0:T(8,128)} async-done(((f32[128,7168]{1,0:T(8,128)}), f32[128,7168]{1,0:T(8,128)}) %all-reduce.3.cloned.1.call-update) | async-done | bytes 3670032 | tf_op jit(solution)/shard_map/psum | solution.py:66
  225.3 19.4 %all-gather.5 = s32[16,1,256]{2,1,0:T(1,128)S(1)} all-gather(s32[1,1,256]{2,1,0:T(1,128)S(1)} %bitcast.95), channel_id=1, replica_groups=mesh['pop'=16,'tp'=8] {'pop'}, dimensions={0}, use_global_device_ids=true | all-gather | bytes 17408 | tf_op jit(solution)/shard_map/all_gather | solution.py:78
  244.7 130.4 %all-gather.9.cloned.1.call-done = bf16[4096,3584]{1,0:T(8,128)(2,1)} async-done(((bf16[256,3584]{1,0:T(8,128)(2,1)}), bf16[4096,3584]{1,0:T(8,128)(2,1)}) %all-gather.9.cloned.1.call-update) | async-done | bytes 29360144 | tf_op jit(solution)/shard_map/all_gather | solution.py:77
  375.2 30.5 %fusion.50 = (f32[4096]{0:T(1024)}, f32[4096,768]{0,1:T(8,128)}) fusion(bf16[4096,3584]{1,0:T(8,128)(2,1)} %all-gather.9.cloned.1.call-done, bf16[3584,768]{1,0:T(8,128)(2,1)} %param.17), kind=kOutput, calls=%fused_computation.85 | convolution fusion | flops 22551719936 | bytes 47464448 | tf_op jit(solution)/shard_map/dot_general | solution.py:79
  405.7 5.1 all-to-all-start
  410.8 7.2 %select_reduce_fusion = (f32[4096]{0:T(1024)}, f32[4096]{0:T(1024)}) fusion(f32[4096,768]{0,1:T(8,128)} %get-tuple-element.367, s32[4096]{0:T(1024)S(1)} %bitcast.85, s32[768]{0:T(1024)S(1)} %iota_add_fusion, f32[4096]{0:T(1024)} %get-tuple-element.366), kind=kLoop, calls=%fused_computation.43 | loop fusion | flops 15720448 | bytes 12651520 | tf_op jit(solution)/shard_map/reduce_sum | solution.py:82
  418.0 5.7 all-to-all-start.1
  426.3 3.2 all-to-all-done.1
  429.5 3.7 all-to-all-start.2
  433.2 19.4 %all-gather.4 = f32[8,1,256]{2,1,0:T(1,128)S(1)} all-gather(f32[1,1,256]{2,1,0:T(1,128)S(1)} %bitcast.93), channel_id=3, replica_groups=mesh['pop'=16,'tp'=8] {'tp'}, dimensions={0}, use_global_device_ids=true | all-gather | bytes 9216 | tf_op jit(solution)/shard_map/all_gather | solution.py:13
  452.7 14.6 %all-gather.6 = f32[8,1,256]{2,1,0:T(1,128)S(1)} all-gather(f32[1,1,256]{2,1,0:T(1,128)S(1)} %bitcast.94), channel_id=4, replica_groups=mesh['pop'=16,'tp'=8] {'tp'}, dimensions={0}, use_global_device_ids=true | all-gather | bytes 9216 | tf_op jit(solution)/shard_map/all_gather | solution.py:13
  467.3 17.9 %all-gather.3 = f32[8,1,256]{2,1,0:T(1,128)S(1)} all-gather(f32[1,1,256]{2,1,0:T(1,128)S(1)} %bitcast.92), channel_id=2, replica_groups=mesh['pop'=16,'tp'=8] {'tp'}, dimensions={0}, use_global_device_ids=true | all-gather | bytes 9216 | tf_op jit(solution)/shard_map/all_gather | solution.py:13
  486.1 37.7 %all-reduce = f32[32]{0:T(128)S(1)} all-reduce(f32[32]{0:T(128)S(1)} %divide_dynamic-update-slice_fusion), channel_id=1, replica_groups=mesh['pop'=16,'tp'=8] {'pop'}, use_global_device_ids=true, to_apply=%add | all-reduce | flops 32 | bytes 256
  524.2 77.1 %while.36 = (s32[]{:T(128)}, f32[148,3584]{1,0:T(8,128)S(1)}, f32[16]{0:T(128)S(1)}, s32[]{:T(128)}, s32[16]{0:T(128)S(1)}, /*index=5*/s32[]{:T(128)}, s32[1]{0:T(128)}, s32[]{:T(128)}) while((s32[]{:T(128)}, f32[148,3584]{1,0:T(8,128)S(1)}, f32[16]{0:T(128)S(1)}, s32[]{:T(128)}, s32[16]{0:T(128)S(1)}, /*index=5*/s32[]{:T(128)}, ...), condition=%wide.region_13.14_spmd.clone, body=%wide.region_12.13_spmd.clone.sunk | while | flops 15913260 | bytes 4244783 | solution.py:126
  526.2 2.9 select_add_fusion.2
  531.0 2.9 select_add_fusion.2
  535.8 2.9 select_add_fusion.2
  540.6 2.9 select_add_fusion.2
  545.4 2.9 select_add_fusion.2
  550.2 2.9 select_add_fusion.2
  555.1 2.9 select_add_fusion.2
  559.9 2.9 select_add_fusion.2
  564.7 2.9 select_add_fusion.2
  569.5 2.9 select_add_fusion.2
  574.3 2.9 select_add_fusion.2
  579.2 2.9 select_add_fusion.2
  584.0 2.9 select_add_fusion.2
  588.8 2.9 select_add_fusion.2
  593.6 2.9 select_add_fusion.2
  598.4 2.9 select_add_fusion.2
  (135 shorter events, 34.7 us)
Async XLA Ops:
  7.2 2.0 copy-start
  7.2 212.3 %all-reduce.3.cloned.1.call-start = ((), (), s32[]{:S(2)}) async-start(), calls=%async_computation.3 | async-start | bytes 7340032 | tf_op jit(solution)/shard_map/psum | solution.py:66
  50.7 0.7 copy-start.7
  50.7 168.8 %copy-start.3 = (bf16[1,128,3584]{2,1,0:T(8,128)(2,1)S(1)}, bf16[1,128,3584]{2,1,0:T(8,128)(2,1)}, u32[]{:S(2)}) copy-start(bf16[1,128,3584]{2,1,0:T(8,128)(2,1)} %param.14) | copy-start | bytes 2752516
  50.8 324.4 %all-gather.9.cloned.1.call-start = ((), (), s32[]{:S(2)}) async-start(), calls=%async_computation.4 | async-start | bytes 31195136 | tf_op jit(solution)/shard_map/all_gather | solution.py:77
  221.8 0.7 copy-start.4
  222.6 2.2 copy-start.5
  222.6 2.8 copy-start.6
  405.7 12.3 %all-to-all-start = ((f32[16,1,256]{2,1,0:T(1,128)}), f32[16,1,256]{2,1,0:T(1,128)S(1)}, u32[]{:S(2)}, u32[]{:S(2)}) async-start(f32[16,1,256]{2,1,0:T(1,128)} %bitcast.11), calls=%async_computation | async-start | bytes 32768 | tf_op jit(solution)/shard_map/all_to_all | solution.py:85
  410.8 14.3 %copy-start.9 = (u32[128]{0:T(128)S(1)}, u32[128]{0:T(128)}, u32[]{:S(2)}) copy-start(u32[128]{0:T(128)} %constant.251) | copy-start | bytes 1540
  410.8 113.2 %copy-start.8 = (s32[16]{0:T(128)S(1)}, s32[16]{0:T(128)}, u32[]{:S(2)}) copy-start(s32[16]{0:T(128)} %param.20) | copy-start | bytes 196
  418.0 11.5 %all-to-all-start.1 = ((f32[16,1,256]{2,1,0:T(1,128)}), f32[16,1,256]{2,1,0:T(1,128)S(1)}, u32[]{:S(2)}, u32[]{:S(2)}) async-start(f32[16,1,256]{2,1,0:T(1,128)} %bitcast.14), calls=%async_computation.1 | async-start | bytes 32768 | tf_op jit(solution)/shard_map/all_to_all | solution.py:92
  429.5 23.2 %all-to-all-start.2 = ((f32[16,1,256]{2,1,0:T(1,128)}), f32[16,1,256]{2,1,0:T(1,128)S(1)}, u32[]{:S(2)}, u32[]{:S(2)}) async-start(f32[16,1,256]{2,1,0:T(1,128)} %bitcast.20), calls=%async_computation.2 | async-start | bytes 32768 | tf_op jit(solution)/shard_map/all_to_all | solution.py:99
  523.7 0.5 copy-start.10
  601.3 1.3 copy-start.2
  601.4 1.5 copy-start.1
Sparse Core Ops, SparseCore 0:
  50.9 168.5 all-reduce.2
  224.8 150.2 all-gather.8
where the time goes:
time: 611 us; the launch traced here: 610 us
  waiting for transfers between devices  302 us (49%)
  blocking collectives  109 us (18%)
  matrix products  70 us (11%)
  other arithmetic  62 us (10%)
  local copies, waits for them, and re-layouts  25.3 us (4%)
  between operations  16.2 us (3%)
  starting transfers between devices  14.6 us (2%)
  loops' own time  11 us (2%)
    psum x1, waiting for transfers between devices, local(): summed = lax.psum(jnp.concatenate([base_out, probe_out], axis=1), 'tp')  168 us
    all_gather x1, waiting for transfers between devices, local(): row_states = lax.all_gather(normed, 'pop', axis=0, tiled=True)  130 us
    all_gather x3, blocking collectives, merged(): everything = jax.tree.map(lambda part: lax.all_gather(part, axis), array)  52 us
    add x16, other arithmetic, add_pair(): return running + fitness_gap[pair_index] * term  46.2 us
    unnamed x1, blocking collectives  37.7 us
    dot_general x1, matrix products, local(): jnp.dot(hidden_rows, noise_rows, preferred_element_type=jnp.float32)  31 us
    dot_general x1, matrix products, local(): logits = jnp.dot(row_states, head, preferred_element_type=jnp.float32)  30.5 us
    all_gather x1, blocking collectives, local(): lax.all_gather(jnp.concatenate([labels[0], labels[0]]), 'pop', axis=0, ti...  19.4 us
  transfers between devices with their start and end apart: 5, of which 3 were waited for; matrix products, arithmetic and copies ran while one was open for 2% of the time, Pallas kernels for 0%

commit v1 on v0

v1 whole, which is shorter than its diff:
```python
import functools

import jax
import jax.numpy as jnp
from jax import lax
from jax.experimental import pallas as pl
from jax.experimental.pallas import tpu as pltpu
from jax.sharding import Mesh, PartitionSpec as P

FF = 18944
D = 3584
SKIP = 32
EXTRA = 128

MUL_A = 739982445
MUL_B = 695872825
SALT = 1013904223
SALT_MIXED = SALT ^ (SALT >> 15)
root_three = 1.7320508075688772

TP = ("z", "y_hi")
SAME_CORE = ("z", "y_hi", "y_lo", "x")


def shifted(hashed, places):
    return lax.shift_right_logical(hashed, jnp.full_like(hashed, places))


def noise_of(index):
    h = index ^ shifted(index, 15)
    h = h * jnp.int32(MUL_A)
    h = h ^ shifted(h, 12)
    h = h * jnp.int32(MUL_B)
    h = h ^ shifted(h, 30) ^ jnp.int32(SALT_MIXED)
    h = h * jnp.int32(MUL_A)
    h = h ^ shifted(h, 12)
    h = h * jnp.int32(MUL_B)
    bits = (h ^ shifted(h, 15)) & jnp.int32(16777215)
    return ((bits.astype(jnp.float32) - 8388607.5) * jnp.float32(root_three / 8388608.0)).astype(jnp.bfloat16)


def flat_index(rows, cols, width):
    return lax.broadcasted_iota(jnp.int32, (rows, cols), 0) * width + lax.broadcasted_iota(jnp.int32, (rows, cols), 1)


def probe_kernel(start_ref, hidden_ref, weight_ref, probe_ref, base_ref, *, first_col, tile):
    units = hidden_ref.shape[1]
    at = start_ref[0] + first_col + pl.program_id(0) * tile
    total = None
    for k in range(0, units, 256):
        depth = min(256, units - k)
        noise = noise_of(flat_index(depth, tile, D) + (at + k * D))
        part = jnp.dot(hidden_ref[SKIP:, k : k + depth], noise, preferred_element_type=jnp.float32)
        total = part if total is None else total + part
    probe_ref[...] = total.astype(probe_ref.dtype)
    if base_ref is not None:
        base_ref[...] = jnp.dot(
            hidden_ref[SKIP:, :], weight_ref[...], preferred_element_type=jnp.float32
        ).astype(base_ref.dtype)


def probe_call(start, hidden, weight, first_col, cols, tile, probe_type, base_type):
    tokens, units = hidden.shape
    steps = cols // tile
    rows = tokens - SKIP
    in_specs = [
        pl.BlockSpec(memory_space=pltpu.SMEM),
        pl.BlockSpec((tokens, units), lambda i: (0, 0)),
    ]
    out_specs = [pl.BlockSpec((rows, tile), lambda i: (0, i))]
    out_shape = [jax.ShapeDtypeStruct((rows, cols), probe_type)]
    kernel = functools.partial(probe_kernel, first_col=first_col, tile=tile)
    args = [start, hidden]
    if weight is not None:
        wide = D // steps
        in_specs.append(pl.BlockSpec((units, wide), lambda i: (0, i)))
        out_specs.append(pl.BlockSpec((rows, wide), lambda i: (0, i)))
        out_shape.append(jax.ShapeDtypeStruct((rows, D), base_type))
        args.append(weight)
    else:

        def kernel(start_ref, hidden_ref, probe_ref):
            probe_kernel(start_ref, hidden_ref, None, probe_ref, None, first_col=first_col, tile=tile)

    return pl.pallas_call(
        kernel,
        grid=(steps,),
        in_specs=in_specs,
        out_specs=out_specs,
        out_shape=out_shape,
        cost_estimate=pl.CostEstimate(
            flops=units * cols * 2000, bytes_accessed=units * cols, transcendentals=0
        ),
        compiler_params=pltpu.CompilerParams(vmem_limit_bytes=44 << 20),
        name="probe",
    )(*args)


def regenerate_kernel(start_ref, out_ref, *, width):
    at = start_ref[pl.program_id(0)]

    def rows16(r, _):
        first = pl.multiple_of(r * 16, 16)
        for c in range(0, D, width):
            out_ref[0, pl.ds(first, 16), c : c + width] = noise_of(flat_index(16, width, D) + (at + r * (16 * D) + c))
        return 0

    lax.fori_loop(0, out_ref.shape[1] // 16, rows16, 0)


def regenerate(starts, rows):
    pairs = starts.shape[0]
    padded = -(-rows // 16) * 16
    return pl.pallas_call(
        functools.partial(regenerate_kernel, width=512),
        grid=(pairs,),
        in_specs=[pl.BlockSpec(memory_space=pltpu.SMEM)],
        out_specs=pl.BlockSpec((1, padded, D), lambda p: (p, 0, 0)),
        out_shape=jax.ShapeDtypeStruct((pairs, padded, D), jnp.bfloat16),
        cost_estimate=pl.CostEstimate(
            flops=pairs * padded * D * 2000, bytes_accessed=pairs * padded * D * 2, transcendentals=0
        ),
        compiler_params=pltpu.CompilerParams(vmem_limit_bytes=44 << 20),
        name="regenerate",
    )(starts)


def logits_kernel(first_ref, rows_ref, own_ref, other_ref, out_ref, top_ref, sum_ref, hit_ref, *, steps_each):
    v = pl.program_id(1)
    tile = own_ref.shape[1]

    @pl.when(v == 0)
    def _():
        top_ref[...] = jnp.full_like(top_ref, -jnp.inf)
        sum_ref[...] = jnp.zeros_like(sum_ref)
        hit_ref[...] = jnp.zeros_like(hit_ref)

    def visit(head_ref, first):
        digits = rows_ref[:, D : D + EXTRA].astype(jnp.float32)
        label = digits[:, 0:1] * 65536.0 + digits[:, 1:2] * 256.0 + digits[:, 2:3]
        logits = jnp.dot(rows_ref[:, :D], head_ref[...], preferred_element_type=jnp.float32)
        lanes = lax.broadcasted_iota(jnp.int32, (1, 128), 1).astype(jnp.float32)
        label = label - first.astype(jnp.float32)
        slabs = [logits[:, c : c + 128] for c in range(0, tile, 128)]
        top = top_ref[...]
        high = functools.reduce(jnp.maximum, slabs, top)
        total = sum_ref[...] * jnp.exp(top - high)
        hit = hit_ref[...]
        for c, slab in enumerate(slabs):
            total = total + jnp.exp(slab - high)
            hit = hit + jnp.where(lanes + float(c * 128) == label, slab, 0.0)
        top_ref[...] = high
        sum_ref[...] = total
        hit_ref[...] = hit

    @pl.when(v < steps_each)
    def _():
        visit(own_ref, first_ref[0] + v * tile)

    @pl.when(v >= steps_each)
    def _():
        visit(other_ref, first_ref[1] + (v - steps_each) * tile)

    @pl.when(v == pl.num_programs(1) - 1)
    def _():
        top = top_ref[...]
        high = jnp.max(top, axis=1, keepdims=True)
        total = jnp.sum(sum_ref[...] * jnp.exp(top - high), axis=1, keepdims=True)
        hit = jnp.sum(hit_ref[...], axis=1, keepdims=True)
        lane = lax.broadcasted_iota(jnp.int32, top.shape, 1)
        both = jnp.where(lane == 0, high + jnp.log(total), hit)
        out_ref[...] = both.T[:8, :]


def vocabulary_stats(rows, own_head, other_head, firsts, tile_rows=512, tile=256):
    count = rows.shape[0]
    tile_rows = min(tile_rows, count)
    steps_each = own_head.shape[1] // tile
    return pl.pallas_call(
        functools.partial(logits_kernel, steps_each=steps_each),
        grid=(count // tile_rows, 2 * steps_each),
        in_specs=[
            pl.BlockSpec(memory_space=pltpu.SMEM),
            pl.BlockSpec((tile_rows, D + EXTRA), lambda r, v: (r, 0)),
            pl.BlockSpec((D, tile), lambda r, v: (0, jnp.minimum(v, steps_each - 1))),
            pl.BlockSpec((D, tile), lambda r, v: (0, jnp.maximum(v - steps_each, 0))),
        ],
        out_specs=pl.BlockSpec((8, tile_rows), lambda r, v: (0, r)),
        out_shape=jax.ShapeDtypeStruct((8, count), jnp.float32),
        scratch_shapes=[pltpu.VMEM((tile_rows, 128), jnp.float32)] * 3,
        cost_estimate=pl.CostEstimate(
            flops=2 * count * D * 2 * own_head.shape[1], bytes_accessed=count * D * 2, transcendentals=0
        ),
        compiler_params=pltpu.CompilerParams(vmem_limit_bytes=44 << 20),
        name="vocabulary_stats",
    )(firsts, rows, own_head, other_head)


def update_kernel(gap_ref, noise_ref, out_ref):
    rows = out_ref.shape[0]
    pairs = noise_ref.shape[0]
    for r in range(0, rows, 16):
        deep = min(16, rows - r)
        total = None
        for p in range(pairs):
            term = gap_ref[p] * noise_ref[p, r : r + 16, :].astype(jnp.float32)
            total = term if total is None else total + term
        out_ref[r : r + deep, :] = total[:deep]


def update(gap, noise, rows, tile=512):
    pairs, padded, _ = noise.shape
    return pl.pallas_call(
        update_kernel,
        grid=(D // tile,),
        in_specs=[
            pl.BlockSpec(memory_space=pltpu.SMEM),
            pl.BlockSpec((pairs, padded, tile), lambda c: (0, 0, c)),
        ],
        out_specs=pl.BlockSpec((rows, tile), lambda c: (0, c)),
        out_shape=jax.ShapeDtypeStruct((rows, D), jnp.float32),
        cost_estimate=pl.CostEstimate(
            flops=2 * pairs * rows * D, bytes_accessed=2 * pairs * padded * D, transcendentals=0
        ),
        compiler_params=pltpu.CompilerParams(vmem_limit_bytes=44 << 20),
        name="update",
    )(gap, noise)


def scattered_sum(partial, axes, shares):
    rows = partial.shape[0] // shares
    pieces = lax.all_to_all(partial.reshape(shares, rows, partial.shape[1]), axes, 0, 0)
    return jnp.sum(pieces.astype(jnp.float32), axis=0)


def joined(stats, axes, count):
    everyone = lax.all_to_all(jnp.broadcast_to(stats[None], (count,) + stats.shape), axes, 0, 0)
    level = everyone[:, 0]
    top = jnp.max(level, axis=0)
    level = top + jnp.log(jnp.sum(jnp.exp(level - top[None]), axis=0))
    return jnp.stack([level, jnp.sum(everyone[:, 1], axis=0)])


def local(hidden_units, residual, down_weight, norm_gain, head, labels, answer_start, seeds, signs):
    y_lo, x, core = lax.axis_index("y_lo"), lax.axis_index("x"), lax.axis_index("core")
    pop_at = (y_lo * lax.axis_size("x") + x) * 2 + core
    tp_at = lax.axis_index("z") * 2 + lax.axis_index("y_hi")
    tp_count = lax.axis_size("z") * 2
    pop_count = seeds.shape[0]
    chip_pairs = pop_count // 2
    tokens = hidden_units.shape[1]
    scored = tokens - SKIP
    share = scored // tp_count
    units = down_weight.shape[0]
    vocab = head.shape[1]
    noise_scale = 0.25 * FF ** (-0.5)
    swap = [(0, 1), (1, 0)]

    other_head = lax.ppermute(head, "core", swap)
    seed_terms = seeds * jnp.int32(1540483477)
    own_seed = lax.dynamic_index_in_dim(seed_terms, pop_at, 0, keepdims=False)
    start = (own_seed + tp_at * jnp.int32(units * D)).reshape(1)

    first_cols = 1024
    probe_a, base = probe_call(
        start, hidden_units[0], down_weight, 0, first_cols, 256, jnp.bfloat16, jnp.float32
    )
    (probe_b,) = probe_call(start, hidden_units[0], None, first_cols, D - first_cols, 256, jnp.bfloat16, None)
    base = scattered_sum(base, TP, tp_count)
    probe = jnp.concatenate([probe_a, probe_b], axis=1)
    probe = scattered_sum(probe, TP, tp_count)

    token_at = SKIP + tp_at * share
    pair_signs = lax.dynamic_slice_in_dim(signs, pop_at * 2, 2).astype(jnp.float32)
    own_residual = lax.dynamic_slice_in_dim(residual[0], token_at, share, 0).astype(jnp.float32)
    layer = (own_residual + base)[None] + pair_signs[:, None, None] * noise_scale * probe[None]
    mean_square = jnp.mean(layer * layer, axis=2, keepdims=True)
    normed = (layer * lax.rsqrt(mean_square + 1e-06) * norm_gain).astype(jnp.bfloat16)
    own_labels = lax.dynamic_slice_in_dim(labels[0], token_at, share, 0)
    places = jnp.arange(EXTRA, dtype=jnp.int32)[None, :]
    digits = (own_labels[:, None] >> jnp.clip(16 - 8 * places, 0, 16)) & 255
    digits = jnp.where(places < 3, digits, 0).astype(jnp.bfloat16)
    normed = jnp.concatenate([normed, jnp.broadcast_to(digits[None], (2, share, EXTRA))], axis=2)
    rows = lax.all_gather(normed.reshape(2 * share, D + EXTRA), SAME_CORE, axis=0, tiled=True)

    out_rows = FF // (pop_count * tp_count)
    own_first = (pop_at * tp_count + tp_at) * jnp.int32(out_rows * D)
    noise = regenerate(seed_terms + own_first, out_rows)

    own_vocab = (pop_at * tp_count + tp_at) * vocab
    other_vocab = ((pop_at + 1 - 2 * core) * tp_count + tp_at) * vocab
    stats = vocabulary_stats(rows, head, other_head, jnp.stack([own_vocab, other_vocab]))[:2]
    stats = joined(stats, TP, tp_count)
    stats = joined(stats, ("y_lo", "x"), chip_pairs)
    log_prob = (stats[1] - stats[0]).reshape(tp_count, chip_pairs, 2, share)
    positions = SKIP + jnp.arange(scored, dtype=jnp.int32).reshape(tp_count, 1, share)
    own_starts = lax.dynamic_index_in_dim(answer_start.reshape(chip_pairs, 2), core, 1, keepdims=False)
    mask = (positions >= own_starts[None, :, None]).astype(jnp.float32)
    own_fitness = jnp.sum(log_prob * mask[:, :, None, :], axis=(0, 3)) / (tokens - own_starts).astype(jnp.float32)[:, None]
    other_fitness = lax.ppermute(own_fitness, "core", swap)
    ordered = jnp.where(
        core == 0,
        jnp.stack([own_fitness, other_fitness], axis=1),
        jnp.stack([other_fitness, own_fitness], axis=1),
    )
    fitness = ordered.reshape(2 * pop_count)
    gap = jnp.sum((fitness * signs.astype(jnp.float32)).reshape(pop_count, 2), axis=1)
    return fitness, update(gap, noise, out_rows)


def solution(mesh):
    fine = Mesh(mesh.devices.reshape(2, 4, 2, 4, 2), ("y_lo", "x", "core", "z", "y_hi"))
    pop = ("y_lo", "x", "core")
    return jax.shard_map(
        local,
        mesh=fine,
        in_specs=(
            P(pop, None, TP),
            P(pop, None, None),
            P(TP, None),
            P(),
            P(None, pop + TP),
            P(pop, None),
            P(),
            P(),
            P(),
        ),
        out_specs=(P(), P(pop + TP, None)),
        check_vma=False,
    )
```

time: 611 us -> 260 us (0.43)
  waiting for transfers between devices: 302 us -> 105 us
  blocking collectives: 109 us -> 0 us
  Pallas kernels: 0 us -> 98 us
  matrix products: 70 us -> 0 us
  other arithmetic: 62 us -> 4.08 us
  local copies, waits for them, and re-layouts: 25.3 us -> 9.62 us
  starting transfers between devices: 14.6 us -> 28.2 us
  loops' own time: 11 us -> 0 us
    psum x1 -> x0, waiting for transfers between devices: 168 us -> none  [local(): summed = lax.psum(jnp.concatenate([base_out, probe_out], axis=1), 'tp')]
    pallas_call x0 -> x5, Pallas kernels: none -> 98 us  [the longest x1 29.6 us: vocabulary_stats(): pl.pallas_call(functools.partial(logits_kernel, steps_each=steps_each), g...]
    all_gather x1, waiting for transfers between devices: 130 us -> 55.4 us  [local(): lax.all_gather(normed.reshape(2 * share, D + EXTRA), SAME_CORE, axis=0, t...]
    all_gather x4 -> x0, blocking collectives: 71.3 us -> none  [the longest x3 52 us: merged(): everything = jax.tree.map(lambda part: lax.all_gather(part, axis), array)]
    dot_general x3 -> x0, matrix products: 70 us -> none  [the longest x1 31 us: local(): jnp.dot(hidden_rows, noise_rows, preferred_element_type=jnp.float32)]
    add x32 -> x4, other arithmetic: 48.7 us -> 1.64 us  [the longest x1 0.97 us: local(): (own_residual + base)[None]]
    all_to_all x3 -> x4, waiting for transfers between devices: 3.18 us -> 48.3 us  [the longest x2 36.4 us: scattered_sum(): lax.all_to_all(partial.reshape(shares, rows, partial.shape[1]), axes, 0, 0)]
    unnamed x1 -> x0, blocking collectives: 37.7 us -> none
  transfers between devices with their start and end apart: 5 -> 7, of which waited for: 3 -> 6; matrix products, arithmetic and copies ran while one was open for 2% -> 1% of each run, Pallas kernels for 0% -> 11%
where the time goes in v1:
time: 260 us; the launch traced here: 259 us
  waiting for transfers between devices  105 us (40%)
  Pallas kernels  98 us (38%)
  starting transfers between devices  28.2 us (11%)
  between operations  15 us (6%)
  local copies, waits for them, and re-layouts  9.62 us (4%)
  other arithmetic  4.08 us (2%)
    all_gather x1, waiting for transfers between devices, local(): lax.all_gather(normed.reshape(2 * share, D + EXTRA), SAME_CORE, axis=0, t...  55.4 us
    all_to_all x2, waiting for transfers between devices, scattered_sum(): lax.all_to_all(partial.reshape(shares, rows, partial.shape[1]), axes, 0, 0)  36.4 us
    pallas_call x1, Pallas kernels, vocabulary_stats(): pl.pallas_call(functools.partial(logits_kernel, steps_each=steps_each), g...  29.6 us
    pallas_call x2, Pallas kernels, probe_call(): pl.pallas_call(kernel, grid=(steps,), in_specs=in_specs, out_specs=out_sp...  29.5 us
    pallas_call x1, Pallas kernels, regenerate(): pl.pallas_call(functools.partial(regenerate_kernel, width=512), grid=(pai...  28.2 us
    all_to_all x2, starting transfers between devices, scattered_sum(): lax.all_to_all(partial.reshape(shares, rows, partial.shape[1]), axes, 0, 0)  12.5 us
    all_to_all x2, waiting for transfers between devices, joined(): lax.all_to_all(jnp.broadcast_to(stats[None], (count,) + stats.shape), axe...  11.9 us
    pallas_call x1, Pallas kernels, update(): pl.pallas_call(update_kernel, grid=(D // tile,), in_specs=[pl.BlockSpec(m...  10.6 us
  transfers between devices with their start and end apart: 7, of which 6 were waited for; matrix products, arithmetic and copies ran while one was open for 1% of the time, Pallas kernels for 11%

profile of v1, /device:TPU:1, one launch (start us, length us, event | category | flops | bytes accessed | tf_op | source)
XLA Modules:
  0.0 259.4 jit_solution(17944610059454248190)
XLA Ops:
  7.2 1.4 copy.20
  8.6 0.7 broadcast_add_fusion
  9.2 0.6 dynamic_slice.18
  10.5 18.0 %probe.3 = bf16[96,2560]{1,0:T(8,128)(2,1)S(1)} custom-call(s32[1]{0:T(128)} %bitcast.3.start_ref, bf16[128,2368]{1,0:T(8,128)(2,1)S(1)} %bitcast.28), custom_call_target="tpu_custom_call" | custom-call | flops 12124160000 | bytes 6062080 | tf_op jit(solution)/shard_map/probe/pallas_call | solution.py:85
  28.5 11.5 %probe.2 = (bf16[96,1024]{1,0:T(8,128)(2,1)S(1)}, f32[96,3584]{1,0:T(8,128)S(1)}) custom-call(s32[1]{0:T(128)} %bitcast.3.start_ref, bf16[128,2368]{1,0:T(8,128)(2,1)S(1)} %bitcast.29, bf16[2368,3584]{1,0:T(8,128)(2,1)} %weight_ref.1), custom_call_target="tpu_custom_call" | custom-call | flops 4849664000 | bytes 2424832 | tf_op jit(solution)/shard_map/probe/pallas_call | solution.py:85
  40.1 1.1 reshape.199
  41.1 8.5 %all-to-all-start.1 = ((bf16[8,12,3584]{2,1,0:T(8,128)(2,1)}), bf16[8,12,3584]{2,1,0:T(8,128)(2,1)S(1)}, u32[]{:S(2)}, u32[]{:S(2)}) async-start(bf16[8,12,3584]{2,1,0:T(8,128)(2,1)} %reshape.199), calls=%async_computation.1 | async-start | bytes 1835008 | tf_op jit(solution)/shard_map/all_to_all | solution.py:232
  49.6 1.4 reshape.198
  51.0 13.2 %all-to-all-done.1 = bf16[8,12,3584]{2,1,0:T(8,128)(2,1)S(1)} async-done(((bf16[8,12,3584]{2,1,0:T(8,128)(2,1)}), bf16[8,12,3584]{2,1,0:T(8,128)(2,1)S(1)}, u32[]{:S(2)}, u32[]{:S(2)}) %all-to-all-start.1) | async-done | bytes 688160 | tf_op jit(solution)/shard_map/all_to_all | solution.py:232
  64.2 4.0 %all-to-all-start = ((f32[8,12,3584]{2,1,0:T(8,128)}), f32[8,12,3584]{2,1,0:T(8,128)S(1)}, u32[]{:S(2)}, u32[]{:S(2)}) async-start(f32[8,12,3584]{2,1,0:T(8,128)} %reshape.198), calls=%async_computation | async-start | bytes 3670016 | tf_op jit(solution)/shard_map/all_to_all | solution.py:232
  68.8 0.2 convert_reduce_fusion
  69.0 23.2 %all-to-all-done = f32[8,12,3584]{2,1,0:T(8,128)S(1)} async-done(((f32[8,12,3584]{2,1,0:T(8,128)}), f32[8,12,3584]{2,1,0:T(8,128)S(1)}, u32[]{:S(2)}, u32[]{:S(2)}) %all-to-all-start) | async-done | bytes 1376288 | tf_op jit(solution)/shard_map/all_to_all | solution.py:232
  92.4 1.0 fusion
  93.4 0.2 multiply_reduce_fusion
  93.9 0.7 pad_maximum_fusion.1
  94.6 2.7 %collective-permute-start = (bf16[3584,768]{1,0:T(8,128)(2,1)}, bf16[3584,768]{1,0:T(8,128)(2,1)}, u32[]{:S(2)}, u32[]{:S(2)}) collective-permute-start(bf16[3584,768]{1,0:T(8,128)(2,1)} %own_ref.1), channel_id=1, source_target_pairs={{0,8},{8,0},{1,9},{9,1},{2,10},{10,2},{3,11},{11,3},{4,12},{12,4},... | collective-permute-start | bytes 16515080 | tf_op jit(solution)/shard_map/ppermute | solution.py:259
  97.4 0.2 dynamic-slice_reduce_fusion
  97.7 28.2 %regenerate.1.noise_ref = bf16[16,160,3584]{2,1,0:T(8,128)(2,1)} custom-call(s32[16]{0:T(128)S(1)} %get-tuple-element.12.start_ref), custom_call_target="tpu_custom_call" | custom-call | flops 18350080000 | bytes 18350080 | tf_op jit(solution)/shard_map/regenerate/pallas_call | solution.py:114
  125.9 55.4 %all-gather.2.cloned.1.call-done.rows_ref = bf16[1536,3712]{1,0:T(8,128)(2,1)} async-done(((bf16[24,3712]{1,0:T(8,128)(2,1)}), bf16[1536,3712]{1,0:T(8,128)(2,1)}) %all-gather.2.cloned.1.call-update) | async-done | bytes 11403280 | tf_op jit(solution)/shard_map/all_gather | solution.py:284
  181.4 2.6 copy-done.2
  183.9 29.6 %vocabulary_stats.1 = f32[8,1536]{1,0:T(8,128)S(1)} custom-call(s32[2]{0:T(128)S(1)} %pad_add_fusion.first_ref, bf16[1536,3712]{1,0:T(8,128)(2,1)} %all-gather.2.cloned.1.call-done.rows_ref, bf16[3584,768]{1,0:T(8,128)(2,1)S(1)} %copy-done.2, bf16[3584,768]{1,0:T(8,128)(2,1)} %collective-permute-done.other_ref), custom_call_target="tpu_custom_call" | custom-call | flops 16911433728 | bytes 11010048 | tf_op jit(solution)/shard_map/vocabulary_stats/pallas_call | solution.py:179
  213.5 0.7 broadcast_in_dim.21
  214.2 6.3 %all-to-all-start.2 = ((f32[8,2,1536]{2,1,0:T(2,128)}), f32[8,2,1536]{2,1,0:T(2,128)S(1)}, u32[]{:S(2)}, u32[]{:S(2)}) async-start(f32[8,2,1536]{2,1,0:T(2,128)} %broadcast_in_dim.21), calls=%async_computation.2 | async-start | bytes 196608 | tf_op jit(solution)/shard_map/all_to_all | solution.py:237
  220.5 6.9 %all-to-all-done.2 = f32[8,2,1536]{2,1,0:T(2,128)S(1)} async-done(((f32[8,2,1536]{2,1,0:T(2,128)}), f32[8,2,1536]{2,1,0:T(2,128)S(1)}, u32[]{:S(2)}, u32[]{:S(2)}) %all-to-all-start.2) | async-done | bytes 98336 | tf_op jit(solution)/shard_map/all_to_all | solution.py:237
  227.6 0.7 broadcast_in_dim.22
  228.3 3.4 %all-to-all-start.3 = ((f32[8,2,1536]{2,1,0:T(2,128)}), f32[8,2,1536]{2,1,0:T(2,128)S(1)}, u32[]{:S(2)}, u32[]{:S(2)}) async-start(f32[8,2,1536]{2,1,0:T(2,128)} %broadcast_in_dim.22), calls=%async_computation.3 | async-start | bytes 196608 | tf_op jit(solution)/shard_map/all_to_all | solution.py:237
  231.8 0.2 convert_reduce_fusion.1
  231.9 5.0 %all-to-all-done.3 = f32[8,2,1536]{2,1,0:T(2,128)S(1)} async-done(((f32[8,2,1536]{2,1,0:T(2,128)}), f32[8,2,1536]{2,1,0:T(2,128)S(1)}, u32[]{:S(2)}, u32[]{:S(2)}) %all-to-all-start.3) | async-done | bytes 98336 | tf_op jit(solution)/shard_map/all_to_all | solution.py:237
  237.1 0.1 sub.46
  237.4 3.2 %collective-permute-start.1 = (f32[8,2]{0,1:T(2,128)S(1)}, f32[8,2]{0,1:T(2,128)S(1)}, u32[]{:S(2)}, u32[]{:S(2)}) collective-permute-start(f32[8,2]{0,1:T(2,128)S(1)} %broadcast_divide_fusion), channel_id=1, source_target_pairs={{0,8},{8,0},{1,9},{9,1},{2,10},{10,2},{3,11},{11,3},{4,12},{12,4},... | collective-permute-start | bytes 200 | tf_op jit(solution)/shard_map/ppermute | solution.py:300
  240.7 0.8 collective-permute-done.1
  241.9 10.6 %update.1 = f32[148,3584]{1,0:T(8,128)} custom-call(f32[16]{0:T(128)S(1)} %reduce_sum.95.gap_ref, bf16[16,160,3584]{2,1,0:T(8,128)(2,1)} %regenerate.1.noise_ref), custom_call_target="tpu_custom_call" | custom-call | flops 16973824 | bytes 18350080 | tf_op jit(solution)/shard_map/update/pallas_call | solution.py:213
  (58 shorter events, 2.2 us)
Async XLA Ops:
  7.2 61.4 %copy-start = (s32[1,128]{1,0:T(1,128)S(1)}, s32[1,128]{1,0:T(1,128)}, u32[]{:S(2)}) copy-start(s32[1,128]{1,0:T(1,128)} %param.14) | copy-start | bytes 1540
  41.1 23.1 %all-to-all-start.1 = ((bf16[8,12,3584]{2,1,0:T(8,128)(2,1)}), bf16[8,12,3584]{2,1,0:T(8,128)(2,1)S(1)}, u32[]{:S(2)}, u32[]{:S(2)}) async-start(bf16[8,12,3584]{2,1,0:T(8,128)(2,1)} %reshape.199), calls=%async_computation.1 | async-start | bytes 1835008 | tf_op jit(solution)/shard_map/all_to_all | solution.py:232
  51.0 17.3 %copy-start.6 = (s32[32]{0:T(128)S(1)}, s32[32]{0:T(128)}, u32[]{:S(2)}) copy-start(s32[32]{0:T(128)} %param.17) | copy-start | bytes 388
  64.2 28.0 %all-to-all-start = ((f32[8,12,3584]{2,1,0:T(8,128)}), f32[8,12,3584]{2,1,0:T(8,128)S(1)}, u32[]{:S(2)}, u32[]{:S(2)}) async-start(f32[8,12,3584]{2,1,0:T(8,128)} %reshape.198), calls=%async_computation | async-start | bytes 3670016 | tf_op jit(solution)/shard_map/all_to_all | solution.py:232
  68.3 113.1 %all-gather.2.cloned.1.call-start = ((), (), s32[]{:S(2)}) async-start(), calls=%async_computation.4 | async-start | bytes 11581440 | tf_op jit(solution)/shard_map/all_gather | solution.py:284
  69.0 24.8 %copy-start.3 = (f32[3584]{0:T(1024)S(1)}, f32[3584]{0:T(1024)}, u32[]{:S(2)}) copy-start(f32[3584]{0:T(1024)} %param.12) | copy-start | bytes 43012
  93.3 4.0 %copy-start.4 = (s32[16]{0:T(128)S(1)}, s32[16]{0:T(128)}, u32[]{:S(2)}) copy-start(s32[16]{0:T(128)} %param.15) | copy-start | bytes 196
  94.6 31.3 %collective-permute-start = (bf16[3584,768]{1,0:T(8,128)(2,1)}, bf16[3584,768]{1,0:T(8,128)(2,1)}, u32[]{:S(2)}, u32[]{:S(2)}) collective-permute-start(bf16[3584,768]{1,0:T(8,128)(2,1)} %own_ref.1), channel_id=1, source_target_pairs={{0,8},{8,0},{1,9},{9,1},{2,10},{10,2},{3,11},{11,3},{4,12},{12,4},... | collective-permute-start | bytes 16515080 | tf_op jit(solution)/shard_map/ppermute | solution.py:259
  181.4 2.6 copy-start.2
  214.2 13.2 %all-to-all-start.2 = ((f32[8,2,1536]{2,1,0:T(2,128)}), f32[8,2,1536]{2,1,0:T(2,128)S(1)}, u32[]{:S(2)}, u32[]{:S(2)}) async-start(f32[8,2,1536]{2,1,0:T(2,128)} %broadcast_in_dim.21), calls=%async_computation.2 | async-start | bytes 196608 | tf_op jit(solution)/shard_map/all_to_all | solution.py:237
  228.3 8.6 %all-to-all-start.3 = ((f32[8,2,1536]{2,1,0:T(2,128)}), f32[8,2,1536]{2,1,0:T(2,128)S(1)}, u32[]{:S(2)}, u32[]{:S(2)}) async-start(f32[8,2,1536]{2,1,0:T(2,128)} %broadcast_in_dim.22), calls=%async_computation.3 | async-start | bytes 196608 | tf_op jit(solution)/shard_map/all_to_all | solution.py:237
  237.4 4.1 %collective-permute-start.1 = (f32[8,2]{0,1:T(2,128)S(1)}, f32[8,2]{0,1:T(2,128)S(1)}, u32[]{:S(2)}, u32[]{:S(2)}) collective-permute-start(f32[8,2]{0,1:T(2,128)S(1)} %broadcast_divide_fusion), channel_id=1, source_target_pairs={{0,8},{8,0},{1,9},{9,1},{2,10},{10,2},{3,11},{11,3},{4,12},{12,4},... | collective-permute-start | bytes 200 | tf_op jit(solution)/shard_map/ppermute | solution.py:300
  241.7 10.9 %copy-start.5 = (f32[32]{0:T(128)}, f32[32]{0:T(128)S(1)}, u32[]{:S(2)}) copy-start(f32[32]{0:T(128)S(1)} %select_n.42) | copy-start | bytes 388
  241.9 10.7 %copy-start.1 = (s32[1,128]{1,0:T(1,128)S(1)}, s32[1,128]{1,0:T(1,128)}, u32[]{:S(2)}) copy-start(s32[1,128]{1,0:T(1,128)} %param.14) | copy-start | bytes 1540
Sparse Core Ops, SparseCore 0:
  94.7 86.5 all-gather.1

commit v2 on v1

--- a/solution.py
+++ b/solution.py
@@ -43,57 +43,78 @@
     return lax.broadcasted_iota(jnp.int32, (rows, cols), 0) * width + lax.broadcasted_iota(jnp.int32, (rows, cols), 1)
 
 
-def probe_kernel(start_ref, hidden_ref, weight_ref, probe_ref, base_ref, *, first_col, tile):
+def probe_kernel(start_ref, hidden_ref, *refs, first_step, share, with_base):
+    if with_base:
+        left_ref, right_ref, probe_ref, base_ref = refs
+    else:
+        _, probe_ref = refs
     units = hidden_ref.shape[1]
-    at = start_ref[0] + first_col + pl.program_id(0) * tile
+    half = D // 2
+    step = pl.program_id(0) + first_step
+    lane = lax.broadcasted_iota(jnp.int32, (256, 256), 1)
+    index = lax.broadcasted_iota(jnp.int32, (256, 256), 0) * D + jnp.where(lane < 128, lane, lane + (half - 128))
+    at = start_ref[0] + step * 128
     total = None
     for k in range(0, units, 256):
         depth = min(256, units - k)
-        noise = noise_of(flat_index(depth, tile, D) + (at + k * D))
+        noise = noise_of(index[:depth] + (at + k * D))
         part = jnp.dot(hidden_ref[SKIP:, k : k + depth], noise, preferred_element_type=jnp.float32)
         total = part if total is None else total + part
-    probe_ref[...] = total.astype(probe_ref.dtype)
-    if base_ref is not None:
-        base_ref[...] = jnp.dot(
-            hidden_ref[SKIP:, :], weight_ref[...], preferred_element_type=jnp.float32
-        ).astype(base_ref.dtype)
-
-
-def probe_call(start, hidden, weight, first_col, cols, tile, probe_type, base_type):
+    for t in range(probe_ref.shape[0]):
+        rows = slice(t * share, (t + 1) * share)
+        probe_ref[t] = jnp.concatenate([total[rows, :128], total[rows, 128:]], axis=0).astype(probe_ref.dtype)
+    if with_base:
+        left = jnp.dot(hidden_ref[SKIP:, :], left_ref[...], preferred_element_type=jnp.float32)
+        right = jnp.dot(hidden_ref[SKIP:, :], right_ref[...], preferred_element_type=jnp.float32)
+        for t in range(base_ref.shape[0]):
+            rows = slice(t * share, (t + 1) * share)
+            base_ref[t] = jnp.concatenate([left[rows], right[rows]], axis=0).astype(base_ref.dtype)
+
+
+def products(start, hidden, weight, shares, first_steps=2):
     tokens, units = hidden.shape
-    steps = cols // tile
-    rows = tokens - SKIP
-    in_specs = [
-        pl.BlockSpec(memory_space=pltpu.SMEM),
-        pl.BlockSpec((tokens, units), lambda i: (0, 0)),
-    ]
-    out_specs = [pl.BlockSpec((rows, tile), lambda i: (0, i))]
-    out_shape = [jax.ShapeDtypeStruct((rows, cols), probe_type)]
-    kernel = functools.partial(probe_kernel, first_col=first_col, tile=tile)
-    args = [start, hidden]
-    if weight is not None:
-        wide = D // steps
-        in_specs.append(pl.BlockSpec((units, wide), lambda i: (0, i)))
-        out_specs.append(pl.BlockSpec((rows, wide), lambda i: (0, i)))
-        out_shape.append(jax.ShapeDtypeStruct((rows, D), base_type))
-        args.append(weight)
-    else:
-
-        def kernel(start_ref, hidden_ref, probe_ref):
-            probe_kernel(start_ref, hidden_ref, None, probe_ref, None, first_col=first_col, tile=tile)
-
-    return pl.pallas_call(
-        kernel,
-        grid=(steps,),
-        in_specs=in_specs,
-        out_specs=out_specs,
-        out_shape=out_shape,
-        cost_estimate=pl.CostEstimate(
-            flops=units * cols * 2000, bytes_accessed=units * cols, transcendentals=0
-        ),
-        compiler_params=pltpu.CompilerParams(vmem_limit_bytes=44 << 20),
+    share = (tokens - SKIP) // shares
+    half = D // 2
+    steps = half // 128
+    probe_shape = jax.ShapeDtypeStruct((shares, 2 * share, half), jnp.bfloat16)
+    scalar = pl.BlockSpec(memory_space=pltpu.SMEM)
+    whole = pl.BlockSpec((tokens, units), lambda i: (0, 0))
+    params = pltpu.CompilerParams(vmem_limit_bytes=56 << 20)
+
+    def cost(count):
+        return pl.CostEstimate(flops=units * count * 256 * 2000, bytes_accessed=units * count * 256, transcendentals=0)
+
+    wide = half // first_steps
+    probe, base = pl.pallas_call(
+        functools.partial(probe_kernel, first_step=0, share=share, with_base=True),
+        grid=(first_steps,),
+        in_specs=[
+            scalar,
+            whole,
+            pl.BlockSpec((units, wide), lambda i: (0, i)),
+            pl.BlockSpec((units, wide), lambda i: (0, i + first_steps)),
+        ],
+        out_specs=[
+            pl.BlockSpec((shares, 2 * share, 128), lambda i: (0, 0, i)),
+            pl.BlockSpec((shares, 2 * share, wide), lambda i: (0, 0, i)),
+        ],
+        out_shape=[probe_shape, jax.ShapeDtypeStruct((shares, 2 * share, half), jnp.float32)],
+        cost_estimate=cost(first_steps),
+        compiler_params=params,
+        name="base_and_probe",
+    )(start, hidden, weight, weight)
+    probe = pl.pallas_call(
+        functools.partial(probe_kernel, first_step=first_steps, share=share, with_base=False),
+        grid=(steps - first_steps,),
+        in_specs=[scalar, whole, pl.BlockSpec(memory_space=pl.ANY)],
+        out_specs=pl.BlockSpec((shares, 2 * share, 128), lambda i: (0, 0, i + first_steps)),
+        out_shape=probe_shape,
+        input_output_aliases={2: 0},
+        cost_estimate=cost(steps - first_steps),
+        compiler_params=params,
         name="probe",
-    )(*args)
+    )(start, hidden, probe)
+    return probe, base
 
 
 def regenerate_kernel(start_ref, out_ref, *, width):
@@ -125,44 +146,49 @@
     )(starts)
 
 
-def logits_kernel(first_ref, rows_ref, own_ref, other_ref, out_ref, top_ref, sum_ref, hit_ref, *, steps_each):
+LOWEST = -1e30
+
+
+def logits_kernel(first_ref, rows_ref, own_ref, other_ref, out_ref, top_ref, sum_ref, hit_ref, held_ref, *, chunk):
     v = pl.program_id(1)
-    tile = own_ref.shape[1]
-
-    @pl.when(v == 0)
-    def _():
-        top_ref[...] = jnp.full_like(top_ref, -jnp.inf)
-        sum_ref[...] = jnp.zeros_like(sum_ref)
-        hit_ref[...] = jnp.zeros_like(hit_ref)
-
-    def visit(head_ref, first):
-        digits = rows_ref[:, D : D + EXTRA].astype(jnp.float32)
-        label = digits[:, 0:1] * 65536.0 + digits[:, 1:2] * 256.0 + digits[:, 2:3]
-        logits = jnp.dot(rows_ref[:, :D], head_ref[...], preferred_element_type=jnp.float32)
-        lanes = lax.broadcasted_iota(jnp.int32, (1, 128), 1).astype(jnp.float32)
-        label = label - first.astype(jnp.float32)
-        slabs = [logits[:, c : c + 128] for c in range(0, tile, 128)]
-        top = top_ref[...]
+    count, vocab = rows_ref.shape[0], own_ref.shape[1]
+    lanes = lax.broadcasted_iota(jnp.int32, (1, 128), 1).astype(jnp.float32)
+
+    def absorb(slot, r, first):
+        some = pl.ds(r, chunk)
+        digits = rows_ref[some, D : D + EXTRA].astype(jnp.float32)
+        label = digits[:, 0:1] * 65536.0 + digits[:, 1:2] * 256.0 + digits[:, 2:3] - first.astype(jnp.float32)
+        slabs = [held_ref[slot, some, c : c + 128] for c in range(0, vocab, 128)]
+        top = top_ref[some, :]
         high = functools.reduce(jnp.maximum, slabs, top)
-        total = sum_ref[...] * jnp.exp(top - high)
-        hit = hit_ref[...]
+        total = sum_ref[some, :] * jnp.exp(top - high)
+        hit = hit_ref[some, :]
         for c, slab in enumerate(slabs):
             total = total + jnp.exp(slab - high)
             hit = hit + jnp.where(lanes + float(c * 128) == label, slab, 0.0)
-        top_ref[...] = high
-        sum_ref[...] = total
-        hit_ref[...] = hit
-
-    @pl.when(v < steps_each)
+        top_ref[some, :] = high
+        sum_ref[some, :] = total
+        hit_ref[some, :] = hit
+
+    def multiply(slot, r, head_ref):
+        some = pl.ds(r, chunk)
+        held_ref[slot, some, :] = jnp.dot(rows_ref[some, :D], head_ref[...], preferred_element_type=jnp.float32)
+
+    @pl.when(v == 0)
     def _():
-        visit(own_ref, first_ref[0] + v * tile)
-
-    @pl.when(v >= steps_each)
+        top_ref[...] = jnp.full_like(top_ref, LOWEST)
+        sum_ref[...] = jnp.zeros_like(sum_ref)
+        hit_ref[...] = jnp.zeros_like(hit_ref)
+        for r in range(0, count, chunk):
+            multiply(0, r, own_ref)
+
+    @pl.when(v == 1)
     def _():
-        visit(other_ref, first_ref[1] + (v - steps_each) * tile)
-
-    @pl.when(v == pl.num_programs(1) - 1)
-    def _():
+        for r in range(0, count, chunk):
+            multiply(1, r, other_ref)
+            absorb(0, r, first_ref[0])
+        for r in range(0, count, chunk):
+            absorb(1, r, first_ref[1])
         top = top_ref[...]
         high = jnp.max(top, axis=1, keepdims=True)
         total = jnp.sum(sum_ref[...] * jnp.exp(top - high), axis=1, keepdims=True)
@@ -172,26 +198,28 @@
         out_ref[...] = both.T[:8, :]
 
 
-def vocabulary_stats(rows, own_head, other_head, firsts, tile_rows=512, tile=256):
+def vocabulary_stats(rows, own_head, other_head, firsts, tile_rows=512, chunk=256):
     count = rows.shape[0]
     tile_rows = min(tile_rows, count)
-    steps_each = own_head.shape[1] // tile
+    vocab = own_head.shape[1]
+    head_spec = pl.BlockSpec((D, vocab), lambda r, v: (0, 0), pipeline_mode=pl.Buffered(1))
     return pl.pallas_call(
-        functools.partial(logits_kernel, steps_each=steps_each),
-        grid=(count // tile_rows, 2 * steps_each),
+        functools.partial(logits_kernel, chunk=min(chunk, tile_rows)),
+        grid=(count // tile_rows, 2),
         in_specs=[
             pl.BlockSpec(memory_space=pltpu.SMEM),
             pl.BlockSpec((tile_rows, D + EXTRA), lambda r, v: (r, 0)),
-            pl.BlockSpec((D, tile), lambda r, v: (0, jnp.minimum(v, steps_each - 1))),
-            pl.BlockSpec((D, tile), lambda r, v: (0, jnp.maximum(v - steps_each, 0))),
+            head_spec,
+            head_spec,
         ],
         out_specs=pl.BlockSpec((8, tile_rows), lambda r, v: (0, r)),
         out_shape=jax.ShapeDtypeStruct((8, count), jnp.float32),
-        scratch_shapes=[pltpu.VMEM((tile_rows, 128), jnp.float32)] * 3,
+        scratch_shapes=[pltpu.VMEM((tile_rows, 128), jnp.float32)] * 3
+        + [pltpu.VMEM((2, tile_rows, vocab), jnp.float32)],
         cost_estimate=pl.CostEstimate(
-            flops=2 * count * D * 2 * own_head.shape[1], bytes_accessed=count * D * 2, transcendentals=0
+            flops=2 * count * D * 2 * vocab, bytes_accessed=count * D * 2, transcendentals=0
         ),
-        compiler_params=pltpu.CompilerParams(vmem_limit_bytes=44 << 20),
+        compiler_params=pltpu.CompilerParams(vmem_limit_bytes=56 << 20),
         name="vocabulary_stats",
     )(firsts, rows, own_head, other_head)
 
@@ -208,7 +236,7 @@
         out_ref[r : r + deep, :] = total[:deep]
 
 
-def update(gap, noise, rows, tile=512):
+def update(gap, noise, rows, tile=896):
     pairs, padded, _ = noise.shape
     return pl.pallas_call(
         update_kernel,
@@ -227,10 +255,11 @@
     )(gap, noise)
 
 
-def scattered_sum(partial, axes, shares):
-    rows = partial.shape[0] // shares
-    pieces = lax.all_to_all(partial.reshape(shares, rows, partial.shape[1]), axes, 0, 0)
-    return jnp.sum(pieces.astype(jnp.float32), axis=0)
+def scattered_sum(partial, axes):
+    pieces = lax.all_to_all(partial, axes, 0, 0)
+    total = jnp.sum(pieces.astype(jnp.float32), axis=0)
+    share = total.shape[0] // 2
+    return jnp.concatenate([total[:share], total[share:]], axis=1)
 
 
 def joined(stats, axes, count):
@@ -261,14 +290,9 @@
     own_seed = lax.dynamic_index_in_dim(seed_terms, pop_at, 0, keepdims=False)
     start = (own_seed + tp_at * jnp.int32(units * D)).reshape(1)
 
-    first_cols = 1024
-    probe_a, base = probe_call(
-        start, hidden_units[0], down_weight, 0, first_cols, 256, jnp.bfloat16, jnp.float32
-    )
-    (probe_b,) = probe_call(start, hidden_units[0], None, first_cols, D - first_cols, 256, jnp.bfloat16, None)
-    base = scattered_sum(base, TP, tp_count)
-    probe = jnp.concatenate([probe_a, probe_b], axis=1)
-    probe = scattered_sum(probe, TP, tp_count)
+    probe, base = products(start, hidden_units[0], down_weight, tp_count)
+    base = scattered_sum(base, TP)
+    probe = scattered_sum(probe, TP)
 
     token_at = SKIP + tp_at * share
     pair_signs = lax.dynamic_slice_in_dim(signs, pop_at * 2, 2).astype(jnp.float32)

time: 260 us -> 249 us (0.958)
  waiting for transfers between devices: 105 us -> 97.2 us
  local copies, waits for them, and re-layouts: 9.62 us -> 6.21 us
    all_to_all x2, waiting for transfers between devices: 36.4 us -> 29.9 us  [scattered_sum(): pieces = lax.all_to_all(partial, axes, 0, 0)]
where the time goes in v2:
time: 249 us
  Pallas kernels  97.2 us (39%)
  waiting for transfers between devices  97.2 us (39%)
  starting transfers between devices  28.8 us (12%)
  between operations  14.9 us (6%)
  local copies, waits for them, and re-layouts  6.21 us (2%)
  other arithmetic  4.54 us (2%)
    all_gather x1, waiting for transfers between devices, local(): lax.all_gather(normed.reshape(2 * share, D + EXTRA), SAME_CORE, axis=0, t...  54.7 us
    all_to_all x2, waiting for transfers between devices, scattered_sum(): pieces = lax.all_to_all(partial, axes, 0, 0)  29.9 us
    pallas_call x1, Pallas kernels, regenerate(): pl.pallas_call(functools.partial(regenerate_kernel, width=512), grid=(pai...  28.2 us
    pallas_call x1, Pallas kernels, vocabulary_stats(): pl.pallas_call(functools.partial(logits_kernel, chunk=min(chunk, tile_row...  26.1 us
    pallas_call x1, Pallas kernels, products(): pl.pallas_call(functools.partial(probe_kernel, first_step=first_steps, sh...  23.3 us
    all_to_all x2, starting transfers between devices, scattered_sum(): pieces = lax.all_to_all(partial, axes, 0, 0)  12.3 us
    all_to_all x2, waiting for transfers between devices, joined(): lax.all_to_all(jnp.broadcast_to(stats[None], (count,) + stats.shape), axe...  11.9 us
    pallas_call x1, Pallas kernels, products(): pl.pallas_call(functools.partial(probe_kernel, first_step=0, share=share,...  10.4 us
  transfers between devices with their start and end apart: 7, of which 6 were waited for; matrix products, arithmetic and copies ran while one was open for 1% of the time, Pallas kernels for 11%

profile of v2, /device:TPU:1, one launch (start us, length us, event | category | flops | bytes accessed | tf_op | source)
XLA Modules:
  0.0 248.8 jit_solution(9848046751468109336)
XLA Ops:
  7.2 2.1 copy.21
  9.3 0.7 broadcast_add_fusion
  10.0 0.6 dynamic_slice.18
  11.2 10.4 %base_and_probe.1 = (bf16[8,24,1792]{2,1,0:T(8,128)(2,1)}, f32[8,24,1792]{2,1,0:T(8,128)}) custom-call(s32[1]{0:T(128)} %bitcast.3.start_ref, bf16[128,2368]{1,0:T(8,128)(2,1)} %bitcast.28, bf16[2368,3584]{1,0:T(8,128)(2,1)} %refs_1_.1, bf16[2368,3584]{1,0:T(8,128)(2,1)} %refs_1_.1), custom_call_target="tpu_custom_call" | custom-call | flops 2424832000 | bytes 1212416 | tf_op jit(solution)/shard_map/base_and_probe/pallas_call | solution.py:88
  21.7 23.3 %probe.1 = bf16[8,24,1792]{2,1,0:T(8,128)(2,1)} custom-call(s32[1]{0:T(128)} %bitcast.3.start_ref, bf16[128,2368]{1,0:T(8,128)(2,1)} %bitcast.29, bf16[8,24,1792]{2,1,0:T(8,128)(2,1)} %get-tuple-element.5.refs_0_), custom_call_target="tpu_custom_call", output_to_operand_aliasing={{}: (2, {})} | custom-call | flops 14548992000 | bytes 7274496 | tf_op jit(solution)/shard_map/probe/pallas_call | solution.py:106
  45.0 8.5 %all-to-all-start.1 = ((bf16[8,24,1792]{2,1,0:T(8,128)(2,1)}), bf16[8,24,1792]{2,1,0:T(8,128)(2,1)S(1)}, u32[]{:S(2)}, u32[]{:S(2)}) async-start(bf16[8,24,1792]{2,1,0:T(8,128)(2,1)} %probe.1), calls=%async_computation.1 | async-start | bytes 1376256 | tf_op jit(solution)/shard_map/all_to_all | solution.py:259
  53.9 11.8 %all-to-all-done.1 = bf16[8,24,1792]{2,1,0:T(8,128)(2,1)S(1)} async-done(((bf16[8,24,1792]{2,1,0:T(8,128)(2,1)}), bf16[8,24,1792]{2,1,0:T(8,128)(2,1)S(1)}, u32[]{:S(2)}, u32[]{:S(2)}) %all-to-all-start.1) | async-done | bytes 688160 | tf_op jit(solution)/shard_map/all_to_all | solution.py:259
  65.7 3.8 %all-to-all-start = ((f32[8,24,1792]{2,1,0:T(8,128)}), f32[8,24,1792]{2,1,0:T(8,128)S(1)}, u32[]{:S(2)}, u32[]{:S(2)}) async-start(f32[8,24,1792]{2,1,0:T(8,128)} %get-tuple-element.4), calls=%async_computation | async-start | bytes 2752512 | tf_op jit(solution)/shard_map/all_to_all | solution.py:259
  69.8 18.1 %all-to-all-done = f32[8,24,1792]{2,1,0:T(8,128)S(1)} async-done(((f32[8,24,1792]{2,1,0:T(8,128)}), f32[8,24,1792]{2,1,0:T(8,128)S(1)}, u32[]{:S(2)}, u32[]{:S(2)}) %all-to-all-start) | async-done | bytes 1376288 | tf_op jit(solution)/shard_map/all_to_all | solution.py:259
  88.0 1.0 fusion
  89.0 0.2 multiply_reduce_fusion
  89.4 0.1 multiply_convert_fusion
  89.6 0.7 pad_maximum_fusion.1
  90.3 3.5 %collective-permute-start = (bf16[3584,768]{1,0:T(8,128)(2,1)}, bf16[3584,768]{1,0:T(8,128)(2,1)}, u32[]{:S(2)}, u32[]{:S(2)}) collective-permute-start(bf16[3584,768]{1,0:T(8,128)(2,1)} %own_ref.1), channel_id=1, source_target_pairs={{0,8},{8,0},{1,9},{9,1},{2,10},{10,2},{3,11},{11,3},{4,12},{12,4},... | collective-permute-start | bytes 16515080 | tf_op jit(solution)/shard_map/ppermute | solution.py:288
  93.8 0.2 dynamic-slice_reduce_fusion
  94.0 0.7 pad_add_fusion.first_ref
  94.7 28.2 %regenerate.1.noise_ref = bf16[16,160,3584]{2,1,0:T(8,128)(2,1)} custom-call(s32[16]{0:T(128)S(1)} %get-tuple-element.16.start_ref), custom_call_target="tpu_custom_call" | custom-call | flops 18350080000 | bytes 18350080 | tf_op jit(solution)/shard_map/regenerate/pallas_call | solution.py:135
  122.9 54.7 %all-gather.2.cloned.1.call-done.rows_ref = bf16[1536,3712]{1,0:T(8,128)(2,1)} async-done(((bf16[24,3712]{1,0:T(8,128)(2,1)}), bf16[1536,3712]{1,0:T(8,128)(2,1)}) %all-gather.2.cloned.1.call-update) | async-done | bytes 11403280 | tf_op jit(solution)/shard_map/all_gather | solution.py:308
  177.6 26.1 %vocabulary_stats.1 = f32[8,1536]{1,0:T(8,128)} custom-call(s32[2]{0:T(128)} %pad_add_fusion.first_ref, bf16[1536,3712]{1,0:T(8,128)(2,1)} %all-gather.2.cloned.1.call-done.rows_ref, bf16[3584,768]{1,0:T(8,128)(2,1)} %own_ref.1, bf16[3584,768]{1,0:T(8,128)(2,1)} %collective-permute-done.other_ref), custom_call_target="tpu_custom_call" | custom-call | flops 16911433728 | bytes 11010048 | tf_op jit(solution)/shard_map/vocabulary_stats/pallas_call | solution.py:206
  203.7 0.8 slice.40
  204.5 0.7 broadcast_in_dim.21
  205.1 6.3 %all-to-all-start.2 = ((f32[8,2,1536]{2,1,0:T(2,128)}), f32[8,2,1536]{2,1,0:T(2,128)S(1)}, u32[]{:S(2)}, u32[]{:S(2)}) async-start(f32[8,2,1536]{2,1,0:T(2,128)} %broadcast_in_dim.21), calls=%async_computation.2 | async-start | bytes 196608 | tf_op jit(solution)/shard_map/all_to_all | solution.py:266
  211.5 6.9 %all-to-all-done.2 = f32[8,2,1536]{2,1,0:T(2,128)S(1)} async-done(((f32[8,2,1536]{2,1,0:T(2,128)}), f32[8,2,1536]{2,1,0:T(2,128)S(1)}, u32[]{:S(2)}, u32[]{:S(2)}) %all-to-all-start.2) | async-done | bytes 98336 | tf_op jit(solution)/shard_map/all_to_all | solution.py:266
  218.6 0.7 broadcast_in_dim.22
  219.3 3.4 %all-to-all-start.3 = ((f32[8,2,1536]{2,1,0:T(2,128)}), f32[8,2,1536]{2,1,0:T(2,128)S(1)}, u32[]{:S(2)}, u32[]{:S(2)}) async-start(f32[8,2,1536]{2,1,0:T(2,128)} %broadcast_in_dim.22), calls=%async_computation.3 | async-start | bytes 196608 | tf_op jit(solution)/shard_map/all_to_all | solution.py:266
  222.7 0.2 convert_reduce_fusion.1
  222.9 5.0 %all-to-all-done.3 = f32[8,2,1536]{2,1,0:T(2,128)S(1)} async-done(((f32[8,2,1536]{2,1,0:T(2,128)}), f32[8,2,1536]{2,1,0:T(2,128)S(1)}, u32[]{:S(2)}, u32[]{:S(2)}) %all-to-all-start.3) | async-done | bytes 98336 | tf_op jit(solution)/shard_map/all_to_all | solution.py:266
  228.0 0.1 sub.46
  228.2 0.1 multiply_reduce_fusion.1
  228.4 3.2 %collective-permute-start.1 = (f32[8,2]{0,1:T(2,128)S(1)}, f32[8,2]{0,1:T(2,128)S(1)}, u32[]{:S(2)}, u32[]{:S(2)}) collective-permute-start(f32[8,2]{0,1:T(2,128)S(1)} %broadcast_divide_fusion), channel_id=1, source_target_pairs={{0,8},{8,0},{1,9},{9,1},{2,10},{10,2},{3,11},{11,3},{4,12},{12,4},... | collective-permute-start | bytes 200 | tf_op jit(solution)/shard_map/ppermute | solution.py:324
  231.7 0.8 collective-permute-done.1
  232.9 9.1 %update.1 = f32[148,3584]{1,0:T(8,128)} custom-call(f32[16]{0:T(128)S(1)} %reduce_sum.92.gap_ref, bf16[16,160,3584]{2,1,0:T(8,128)(2,1)} %regenerate.1.noise_ref), custom_call_target="tpu_custom_call" | custom-call | flops 16973824 | bytes 18350080 | tf_op jit(solution)/shard_map/update/pallas_call | solution.py:241
  (56 shorter events, 2.0 us)
Async XLA Ops:
  7.2 46.6 %copy-start = (s32[1,128]{1,0:T(1,128)S(1)}, s32[1,128]{1,0:T(1,128)}, u32[]{:S(2)}) copy-start(s32[1,128]{1,0:T(1,128)} %param.14) | copy-start | bytes 1540
  21.7 31.9 %copy-start.5 = (s32[32]{0:T(128)S(1)}, s32[32]{0:T(128)}, u32[]{:S(2)}) copy-start(s32[32]{0:T(128)} %param.17) | copy-start | bytes 388
  45.0 20.6 %all-to-all-start.1 = ((bf16[8,24,1792]{2,1,0:T(8,128)(2,1)}), bf16[8,24,1792]{2,1,0:T(8,128)(2,1)S(1)}, u32[]{:S(2)}, u32[]{:S(2)}) async-start(bf16[8,24,1792]{2,1,0:T(8,128)(2,1)} %probe.1), calls=%async_computation.1 | async-start | bytes 1376256 | tf_op jit(solution)/shard_map/all_to_all | solution.py:259
  53.5 35.9 %copy-start.2 = (f32[3584]{0:T(1024)S(1)}, f32[3584]{0:T(1024)}, u32[]{:S(2)}) copy-start(f32[3584]{0:T(1024)} %param.12) | copy-start | bytes 43012
  65.7 28.1 %copy-start.3 = (s32[16]{0:T(128)S(1)}, s32[16]{0:T(128)}, u32[]{:S(2)}) copy-start(s32[16]{0:T(128)} %param.15) | copy-start | bytes 196
  65.7 22.3 %all-to-all-start = ((f32[8,24,1792]{2,1,0:T(8,128)}), f32[8,24,1792]{2,1,0:T(8,128)S(1)}, u32[]{:S(2)}, u32[]{:S(2)}) async-start(f32[8,24,1792]{2,1,0:T(8,128)} %get-tuple-element.4), calls=%async_computation | async-start | bytes 2752512 | tf_op jit(solution)/shard_map/all_to_all | solution.py:259
  69.5 108.1 %all-gather.2.cloned.1.call-start = ((), (), s32[]{:S(2)}) async-start(), calls=%async_computation.4 | async-start | bytes 11581440 | tf_op jit(solution)/shard_map/all_gather | solution.py:308
  90.3 32.7 %collective-permute-start = (bf16[3584,768]{1,0:T(8,128)(2,1)}, bf16[3584,768]{1,0:T(8,128)(2,1)}, u32[]{:S(2)}, u32[]{:S(2)}) collective-permute-start(bf16[3584,768]{1,0:T(8,128)(2,1)} %own_ref.1), channel_id=1, source_target_pairs={{0,8},{8,0},{1,9},{9,1},{2,10},{10,2},{3,11},{11,3},{4,12},{12,4},... | collective-permute-start | bytes 16515080 | tf_op jit(solution)/shard_map/ppermute | solution.py:288
  205.1 13.2 %all-to-all-start.2 = ((f32[8,2,1536]{2,1,0:T(2,128)}), f32[8,2,1536]{2,1,0:T(2,128)S(1)}, u32[]{:S(2)}, u32[]{:S(2)}) async-start(f32[8,2,1536]{2,1,0:T(2,128)} %broadcast_in_dim.21), calls=%async_computation.2 | async-start | bytes 196608 | tf_op jit(solution)/shard_map/all_to_all | solution.py:266
  219.3 8.6 %all-to-all-start.3 = ((f32[8,2,1536]{2,1,0:T(2,128)}), f32[8,2,1536]{2,1,0:T(2,128)S(1)}, u32[]{:S(2)}, u32[]{:S(2)}) async-start(f32[8,2,1536]{2,1,0:T(2,128)} %broadcast_in_dim.22), calls=%async_computation.3 | async-start | bytes 196608 | tf_op jit(solution)/shard_map/all_to_all | solution.py:266
  228.4 4.1 %collective-permute-start.1 = (f32[8,2]{0,1:T(2,128)S(1)}, f32[8,2]{0,1:T(2,128)S(1)}, u32[]{:S(2)}, u32[]{:S(2)}) collective-permute-start(f32[8,2]{0,1:T(2,128)S(1)} %broadcast_divide_fusion), channel_id=1, source_target_pairs={{0,8},{8,0},{1,9},{9,1},{2,10},{10,2},{3,11},{11,3},{4,12},{12,4},... | collective-permute-start | bytes 200 | tf_op jit(solution)/shard_map/ppermute | solution.py:324
  232.7 9.3 %copy-start.4 = (f32[32]{0:T(128)}, f32[32]{0:T(128)S(1)}, u32[]{:S(2)}) copy-start(f32[32]{0:T(128)S(1)} %select_n.42) | copy-start | bytes 388
  232.8 9.2 %copy-start.1 = (s32[1,128]{1,0:T(1,128)S(1)}, s32[1,128]{1,0:T(1,128)}, u32[]{:S(2)}) copy-start(s32[1,128]{1,0:T(1,128)} %param.14) | copy-start | bytes 1540
Sparse Core Ops, SparseCore 0:
  90.4 87.1 all-gather.1

commit v3 on v2

v3 whole, which is shorter than its diff:
```python
import functools

import jax
import jax.numpy as jnp
from jax import lax
from jax.experimental import pallas as pl
from jax.experimental.pallas import tpu as pltpu
from jax.sharding import Mesh, PartitionSpec as P

FF = 18944
D = 3584
SKIP = 32
EXTRA = 128

MUL_A = 739982445
MUL_B = 695872825
SALT = 1013904223
SALT_MIXED = SALT ^ (SALT >> 15)
root_three = 1.7320508075688772

TP = ("z", "y_hi")
SAME_CORE = ("z", "y_hi", "y_lo", "x")


def shifted(hashed, places):
    return lax.shift_right_logical(hashed, jnp.full_like(hashed, places))


def noise_of(index):
    h = index ^ shifted(index, 15)
    h = h * jnp.int32(MUL_A)
    h = h ^ shifted(h, 12)
    h = h * jnp.int32(MUL_B)
    h = h ^ shifted(h, 30) ^ jnp.int32(SALT_MIXED)
    h = h * jnp.int32(MUL_A)
    h = h ^ shifted(h, 12)
    h = h * jnp.int32(MUL_B)
    bits = (h ^ shifted(h, 15)) & jnp.int32(16777215)
    return ((bits.astype(jnp.float32) - 8388607.5) * jnp.float32(root_three / 8388608.0)).astype(jnp.bfloat16)


def flat_index(rows, cols, width):
    return lax.broadcasted_iota(jnp.int32, (rows, cols), 0) * width + lax.broadcasted_iota(jnp.int32, (rows, cols), 1)


def places():
    pop_at = (lax.axis_index("y_lo") * lax.axis_size("x") + lax.axis_index("x")) * 2 + lax.axis_index("core")
    return pop_at, lax.axis_index("z") * 2 + lax.axis_index("y_hi")


def probe_step(seeds_ref, hidden_ref, step):
    units = hidden_ref.shape[1]
    half = D // 2
    lane = lax.broadcasted_iota(jnp.int32, (256, 256), 1)
    index = lax.broadcasted_iota(jnp.int32, (256, 256), 0) * D + jnp.where(lane < 128, lane, lane + (half - 128))
    pop_at, tp_at = places()
    at = seeds_ref[pop_at] * jnp.int32(1540483477) + tp_at * jnp.int32(units * D) + step * 128
    total = None
    for k in range(0, units, 256):
        depth = min(256, units - k)
        noise = noise_of(index[:depth] + (at + k * D))
        part = jnp.dot(hidden_ref[SKIP:, k : k + depth], noise, preferred_element_type=jnp.float32)
        total = part if total is None else total + part
    return total[:, :128], total[:, 128:]


def put_shares(ref, cols, left, right):
    share = ref.shape[1] // 2
    for t in range(ref.shape[0]):
        rows = slice(t * share, (t + 1) * share)
        ref[t, :, cols] = jnp.concatenate([left[rows], right[rows]], axis=0).astype(ref.dtype)


def first_kernel(seeds_ref, hidden_ref, weight_hbm, probe_ref, base_ref, weight_ref, sems, *, steps):
    half = D // 2
    wide = half // 2
    copies = []
    for c in range(4):
        cols = slice((c % 2) * half + (c // 2) * wide, (c % 2) * half + (c // 2 + 1) * wide)
        copies.append(pltpu.make_async_copy(weight_hbm.at[:, cols], weight_ref.at[c], sems.at[c]))
        copies[-1].start()
    for step in range(steps):
        put_shares(probe_ref, slice(step * 128, step * 128 + 128), *probe_step(seeds_ref, hidden_ref, step))
        if step + 2 < steps:
            continue
        c = 2 * (step + 2 - steps)
        sides = []
        for side in (c, c + 1):
            copies[side].wait()
            sides.append(jnp.dot(hidden_ref[SKIP:, :], weight_ref[side], preferred_element_type=jnp.float32))
        put_shares(base_ref, slice((c // 2) * wide, (c // 2 + 1) * wide), *sides)


def rest_kernel(seeds_ref, hidden_ref, _, probe_ref, *, first_step):
    put_shares(probe_ref, slice(None), *probe_step(seeds_ref, hidden_ref, pl.program_id(0) + first_step))


def products(seeds, hidden, weight, shares, first_steps=2):
    tokens, units = hidden.shape
    share = (tokens - SKIP) // shares
    half = D // 2
    steps = half // 128
    probe_shape = jax.ShapeDtypeStruct((shares, 2 * share, half), jnp.bfloat16)
    base_shape = jax.ShapeDtypeStruct((shares, 2 * share, half), jnp.float32)
    scalar = pl.BlockSpec(memory_space=pltpu.SMEM)
    whole = pl.BlockSpec((tokens, units), lambda i: (0, 0))
    params = pltpu.CompilerParams(vmem_limit_bytes=44 << 20)

    def cost(count):
        return pl.CostEstimate(flops=units * count * 256 * 2000, bytes_accessed=units * count * 256, transcendentals=0)

    probe, base = pl.pallas_call(
        functools.partial(first_kernel, steps=first_steps),
        grid=(1,),
        in_specs=[scalar, whole, pl.BlockSpec(memory_space=pl.ANY)],
        out_specs=[
            pl.BlockSpec((shares, 2 * share, first_steps * 128), lambda i: (0, 0, 0)),
            pl.BlockSpec((shares, 2 * share, half), lambda i: (0, 0, 0)),
        ],
        out_shape=[probe_shape, base_shape],
        scratch_shapes=[pltpu.VMEM((4, units, half // 2), jnp.bfloat16), pltpu.SemaphoreType.DMA((4,))],
        cost_estimate=cost(first_steps),
        compiler_params=params,
        name="base_and_probe",
    )(seeds, hidden, weight)
    probe = pl.pallas_call(
        functools.partial(rest_kernel, first_step=first_steps),
        grid=(steps - first_steps,),
        in_specs=[scalar, whole, pl.BlockSpec(memory_space=pl.ANY)],
        out_specs=pl.BlockSpec((shares, 2 * share, 128), lambda i: (0, 0, i + first_steps)),
        out_shape=probe_shape,
        input_output_aliases={2: 0},
        cost_estimate=cost(steps - first_steps),
        compiler_params=params,
        name="probe",
    )(seeds, hidden, probe)
    return probe, base


def regenerate_kernel(seeds_ref, out_ref, *, width, out_rows):
    pop_at, tp_at = places()
    pair = pl.program_id(0)
    at = seeds_ref[pair] * jnp.int32(1540483477) + (pop_at * lax.axis_size("z") * 2 + tp_at) * jnp.int32(out_rows * D)

    def rows16(r, _):
        first = pl.multiple_of(r * 16, 16)
        for c in range(0, D, width):
            out_ref[0, pl.ds(first, 16), c : c + width] = noise_of(
                flat_index(16, width, D) + (at + r * (16 * D) + c)
            )
        return 0

    lax.fori_loop(0, out_ref.shape[1] // 16, rows16, 0)


def regenerate(seeds, rows):
    pairs = seeds.shape[0]
    padded = -(-rows // 16) * 16
    return pl.pallas_call(
        functools.partial(regenerate_kernel, width=512, out_rows=rows),
        grid=(pairs,),
        in_specs=[pl.BlockSpec(memory_space=pltpu.SMEM)],
        out_specs=pl.BlockSpec((1, padded, D), lambda p: (p, 0, 0)),
        out_shape=jax.ShapeDtypeStruct((pairs, padded, D), jnp.bfloat16),
        cost_estimate=pl.CostEstimate(
            flops=pairs * padded * D * 2000, bytes_accessed=pairs * padded * D * 2, transcendentals=0
        ),
        compiler_params=pltpu.CompilerParams(vmem_limit_bytes=50 << 20),
        name="regenerate",
    )(seeds)


def logits_kernel(
    first_ref, rows_hbm, own_hbm, other_ref, out_ref, rows_ref, own_ref, held_ref, stats_ref, sems, own_sem
):
    slots, chunk, _ = rows_ref.shape
    chunks = rows_hbm.shape[0] // chunk
    vocab = own_ref.shape[1]
    lanes = lax.broadcasted_iota(jnp.int32, (1, 128), 1).astype(jnp.float32)

    def fetch(i):
        return pltpu.make_async_copy(
            rows_hbm.at[pl.ds(i * chunk, chunk), :], rows_ref.at[i % slots], sems.at[i % slots]
        )

    def multiply(i):
        rows = rows_ref[i % slots, :, :D]
        held_ref[i % 2, :, vocab:] = jnp.dot(rows, other_ref[...], preferred_element_type=jnp.float32)
        if i == 0:
            own.wait()
        held_ref[i % 2, :, :vocab] = jnp.dot(rows, own_ref[...], preferred_element_type=jnp.float32)

    def absorb(i):
        slot = i % 2
        high = held_ref[slot, :, :128]
        for c in range(128, 2 * vocab, 128):
            high = jnp.maximum(high, held_ref[slot, :, c : c + 128])
        high = jnp.broadcast_to(jnp.max(high, axis=1, keepdims=True), (chunk, 128))
        digits = rows_ref[i % slots, :, D : D + EXTRA].astype(jnp.float32)
        label = digits[:, 0:1] * 65536.0 + digits[:, 1:2] * 256.0 + digits[:, 2:3]
        label = [jnp.broadcast_to(label - first_ref[h].astype(jnp.float32), (chunk, 128)) for h in range(2)]
        total = jnp.zeros((chunk, 128), jnp.float32)
        hit = jnp.zeros((chunk, 128), jnp.float32)
        for c in range(0, 2 * vocab, 128):
            slab = held_ref[slot, :, c : c + 128]
            total = total + jnp.exp(slab - high)
            hit = jnp.where(lanes + float(c % vocab) == label[c // vocab], slab, hit)
        total = jnp.sum(total, axis=1, keepdims=True)
        hit = jnp.sum(hit, axis=1, keepdims=True)
        lane = lax.broadcasted_iota(jnp.int32, (chunk, 128), 1)
        stats_ref[i * chunk : (i + 1) * chunk, :] = jnp.where(lane == 0, high + jnp.log(total), hit)

    fetch(0).start()
    own = pltpu.make_async_copy(own_hbm, own_ref, own_sem)
    own.start()
    for i in range(1, min(slots - 1, chunks)):
        fetch(i).start()
    for i in range(chunks):
        fetch(i).wait()
        multiply(i)
        if i:
            absorb(i - 1)
        if i + slots - 1 < chunks:
            fetch(i + slots - 1).start()
    absorb(chunks - 1)
    out_ref[...] = stats_ref[...].T[:8, :]


def vocabulary_stats(rows, own_head, other_head, firsts, chunk=256, slots=4):
    count = rows.shape[0]
    vocab = own_head.shape[1]
    return pl.pallas_call(
        logits_kernel,
        in_specs=[
            pl.BlockSpec(memory_space=pltpu.SMEM),
            pl.BlockSpec(memory_space=pl.ANY),
            pl.BlockSpec(memory_space=pl.ANY),
            pl.BlockSpec(memory_space=pltpu.VMEM),
        ],
        out_specs=pl.BlockSpec(memory_space=pltpu.VMEM),
        out_shape=jax.ShapeDtypeStruct((8, count), jnp.float32),
        scratch_shapes=[
            pltpu.VMEM((slots, chunk, D + EXTRA), jnp.bfloat16),
            pltpu.VMEM((D, vocab), jnp.bfloat16),
            pltpu.VMEM((2, chunk, 2 * vocab), jnp.float32),
            pltpu.VMEM((count, 128), jnp.float32),
            pltpu.SemaphoreType.DMA((slots,)),
            pltpu.SemaphoreType.DMA,
        ],
        cost_estimate=pl.CostEstimate(
            flops=2 * count * D * 2 * vocab, bytes_accessed=count * D * 2, transcendentals=0
        ),
        compiler_params=pltpu.CompilerParams(vmem_limit_bytes=54 << 20),
        name="vocabulary_stats",
    )(firsts, rows, own_head, other_head)


def update_kernel(gap_ref, noise_ref, out_ref):
    rows = out_ref.shape[0]
    pairs = noise_ref.shape[0]
    for r in range(0, rows, 16):
        deep = min(16, rows - r)
        total = None
        for p in range(pairs):
            term = gap_ref[p] * noise_ref[p, r : r + 16, :].astype(jnp.float32)
            total = term if total is None else total + term
        out_ref[r : r + deep, :] = total[:deep]


def update(gap, noise, rows, tile=896):
    pairs, padded, _ = noise.shape
    return pl.pallas_call(
        update_kernel,
        grid=(D // tile,),
        in_specs=[
            pl.BlockSpec(memory_space=pltpu.SMEM),
            pl.BlockSpec((pairs, padded, tile), lambda c: (0, 0, c)),
        ],
        out_specs=pl.BlockSpec((rows, tile), lambda c: (0, c)),
        out_shape=jax.ShapeDtypeStruct((rows, D), jnp.float32),
        cost_estimate=pl.CostEstimate(
            flops=2 * pairs * rows * D, bytes_accessed=2 * pairs * padded * D, transcendentals=0
        ),
        compiler_params=pltpu.CompilerParams(vmem_limit_bytes=44 << 20),
        name="update",
    )(gap, noise)


def scattered_sum(partial, axes):
    pieces = lax.all_to_all(partial, axes, 0, 0)
    total = jnp.sum(pieces.astype(jnp.float32), axis=0)
    share = total.shape[0] // 2
    return jnp.concatenate([total[:share], total[share:]], axis=1)


def joined(stats, axes, count):
    everyone = lax.all_to_all(jnp.broadcast_to(stats[None], (count,) + stats.shape), axes, 0, 0)
    level = everyone[:, 0]
    top = jnp.max(level, axis=0)
    level = top + jnp.log(jnp.sum(jnp.exp(level - top[None]), axis=0))
    return jnp.stack([level, jnp.sum(everyone[:, 1], axis=0)])


def local(hidden_units, residual, down_weight, norm_gain, head, labels, answer_start, seeds, signs):
    core = lax.axis_index("core")
    pop_at, tp_at = places()
    tp_count = lax.axis_size("z") * 2
    pop_count = seeds.shape[0]
    chip_pairs = pop_count // 2
    tokens = hidden_units.shape[1]
    scored = tokens - SKIP
    share = scored // tp_count
    vocab = head.shape[1]
    noise_scale = 0.25 * FF ** (-0.5)
    swap = [(0, 1), (1, 0)]

    other_head = lax.ppermute(head, "core", swap)

    probe, base = products(seeds, hidden_units[0], down_weight, tp_count)
    base = scattered_sum(base, TP)
    probe, base = lax.optimization_barrier((probe, base))
    probe = scattered_sum(probe, TP)

    token_at = SKIP + tp_at * share
    pair_signs = lax.dynamic_slice_in_dim(signs, pop_at * 2, 2).astype(jnp.float32)
    own_residual = lax.dynamic_slice_in_dim(residual[0], token_at, share, 0).astype(jnp.float32)
    layer = (own_residual + base)[None] + pair_signs[:, None, None] * noise_scale * probe[None]
    mean_square = jnp.mean(layer * layer, axis=2, keepdims=True)
    normed = (layer * lax.rsqrt(mean_square + 1e-06) * norm_gain).astype(jnp.bfloat16)
    own_labels = lax.dynamic_slice_in_dim(labels[0], token_at, share, 0)
    slots = jnp.arange(EXTRA, dtype=jnp.int32)[None, :]
    digits = (own_labels[:, None] >> jnp.clip(16 - 8 * slots, 0, 16)) & 255
    digits = jnp.where(slots < 3, digits, 0).astype(jnp.bfloat16)
    normed = jnp.concatenate([normed, jnp.broadcast_to(digits[None], (2, share, EXTRA))], axis=2)

    out_rows = FF // (pop_count * tp_count)
    later_seeds, normed = lax.optimization_barrier((seeds, normed))
    rows = lax.all_gather(normed.reshape(2 * share, D + EXTRA), SAME_CORE, axis=0, tiled=True)
    noise = regenerate(later_seeds, out_rows)

    own_vocab = (pop_at * tp_count + tp_at) * vocab
    other_vocab = ((pop_at + 1 - 2 * core) * tp_count + tp_at) * vocab
    firsts, noise = lax.optimization_barrier((jnp.stack([own_vocab, other_vocab]), noise))
    stats = vocabulary_stats(rows, head, other_head, firsts)[:2]
    stats = joined(stats, TP, tp_count)
    stats = joined(stats, ("y_lo", "x"), chip_pairs)
    log_prob = (stats[1] - stats[0]).reshape(tp_count, chip_pairs, 2, share)
    positions = SKIP + jnp.arange(scored, dtype=jnp.int32).reshape(tp_count, 1, share)
    own_starts = lax.dynamic_index_in_dim(answer_start.reshape(chip_pairs, 2), core, 1, keepdims=False)
    mask = (positions >= own_starts[None, :, None]).astype(jnp.float32)
    own_fitness = jnp.sum(log_prob * mask[:, :, None, :], axis=(0, 3)) / (tokens - own_starts).astype(jnp.float32)[:, None]
    other_fitness = lax.ppermute(own_fitness, "core", swap)
    ordered = jnp.where(
        core == 0,
        jnp.stack([own_fitness, other_fitness], axis=1),
        jnp.stack([other_fitness, own_fitness], axis=1),
    )
    fitness = ordered.reshape(2 * pop_count)
    gap = jnp.sum((fitness * signs.astype(jnp.float32)).reshape(pop_count, 2), axis=1)
    return fitness, update(gap, noise, out_rows)


def solution(mesh):
    fine = Mesh(mesh.devices.reshape(2, 4, 2, 4, 2), ("y_lo", "x", "core", "z", "y_hi"))
    pop = ("y_lo", "x", "core")
    return jax.shard_map(
        local,
        mesh=fine,
        in_specs=(
            P(pop, None, TP),
            P(pop, None, None),
            P(TP, None),
            P(),
            P(None, pop + TP),
            P(pop, None),
            P(),
            P(),
            P(),
        ),
        out_specs=(P(), P(pop + TP, None)),
        check_vma=False,
    )
```

time: 249 us -> 229 us (0.920)
  waiting for transfers between devices: 97.2 us -> 78.2 us
    all_to_all x2, waiting for transfers between devices: 29.9 us -> 10.9 us  [scattered_sum(): pieces = lax.all_to_all(partial, axes, 0, 0)]
    all_to_all x2, starting transfers between devices: 12.3 us -> 15.2 us  [scattered_sum(): pieces = lax.all_to_all(partial, axes, 0, 0)]
  transfers between devices with their start and end apart: 7 -> 7, of which waited for: 6 -> 5; matrix products, arithmetic and copies ran while one was open for 1% -> 1% of each run, Pallas kernels for 11% -> 23%
where the time goes in v3:
time: 229 us
  Pallas kernels  96.7 us (42%)
  waiting for transfers between devices  78.2 us (34%)
  starting transfers between devices  30.6 us (13%)
  between operations  14.3 us (6%)
  local copies, waits for them, and re-layouts  5.8 us (3%)
  other arithmetic  3.26 us (1%)
    all_gather x1, waiting for transfers between devices, local(): lax.all_gather(normed.reshape(2 * share, D + EXTRA), SAME_CORE, axis=0, t...  54.6 us
    pallas_call x1, Pallas kernels, regenerate(): pl.pallas_call(functools.partial(regenerate_kernel, width=512, out_rows=r...  28.6 us
    pallas_call x1, Pallas kernels, vocabulary_stats(): pl.pallas_call(logits_kernel, in_specs=[pl.BlockSpec(memory_space=pltpu.S...  25.6 us
    pallas_call x1, Pallas kernels, products(): pl.pallas_call(functools.partial(rest_kernel, first_step=first_steps), gr...  23 us
    all_to_all x2, starting transfers between devices, scattered_sum(): pieces = lax.all_to_all(partial, axes, 0, 0)  15.2 us
    all_to_all x2, waiting for transfers between devices, joined(): lax.all_to_all(jnp.broadcast_to(stats[None], (count,) + stats.shape), axe...  11.9 us
    all_to_all x2, waiting for transfers between devices, scattered_sum(): pieces = lax.all_to_all(partial, axes, 0, 0)  10.9 us
    pallas_call x1, Pallas kernels, products(): pl.pallas_call(functools.partial(first_kernel, steps=first_steps), grid=(...  10.4 us
  transfers between devices with their start and end apart: 7, of which 5 were waited for; matrix products, arithmetic and copies ran while one was open for 1% of the time, Pallas kernels for 23%

profile of v3, /device:TPU:1, one launch (start us, length us, event | category | flops | bytes accessed | tf_op | source)
XLA Modules:
  0.0 228.8 jit_solution(4062008517884257444)
XLA Ops:
  7.2 1.4 copy.21
  8.6 0.6 copy-done.2
  9.2 10.4 %base_and_probe.1 = (bf16[8,24,1792]{2,1,0:T(8,128)(2,1)}, f32[8,24,1792]{2,1,0:T(8,128)}) custom-call(s32[16]{0:T(128)S(1)} %copy-done.2, bf16[128,2368]{1,0:T(8,128)(2,1)S(1)} %bitcast.23, bf16[2368,3584]{1,0:T(8,128)(2,1)} %weight_hbm.1), custom_call_target="tpu_custom_call" | custom-call | flops 2424832000 | bytes 1212416 | tf_op jit(solution)/shard_map/base_and_probe/pallas_call | solution.py:112
  19.6 8.5 %all-to-all-start = ((f32[8,24,1792]{2,1,0:T(8,128)}), f32[8,24,1792]{2,1,0:T(8,128)S(1)}, u32[]{:S(2)}, u32[]{:S(2)}) async-start(f32[8,24,1792]{2,1,0:T(8,128)} %get-tuple-element.11), calls=%async_computation | async-start | bytes 2752512 | tf_op jit(solution)/shard_map/all_to_all | solution.py:290
  28.4 23.0 %probe.1 = bf16[8,24,1792]{2,1,0:T(8,128)(2,1)} custom-call(s32[16]{0:T(128)S(1)} %copy-done.3, bf16[128,2368]{1,0:T(8,128)(2,1)S(1)} %bitcast.24, bf16[8,24,1792]{2,1,0:T(8,128)(2,1)} %get-tuple-element.10._), custom_call_target="tpu_custom_call", output_to_operand_aliasing={{}: (2, {})} | custom-call | flops 14548992000 | bytes 7274496 | tf_op jit(solution)/shard_map/probe/pallas_call | solution.py:126
  51.6 6.7 %all-to-all-start.1 = ((bf16[8,24,1792]{2,1,0:T(8,128)(2,1)}), bf16[8,24,1792]{2,1,0:T(8,128)(2,1)S(1)}, u32[]{:S(2)}, u32[]{:S(2)}) async-start(bf16[8,24,1792]{2,1,0:T(8,128)(2,1)} %probe.1), calls=%async_computation.1 | async-start | bytes 1376256 | tf_op jit(solution)/shard_map/all_to_all | solution.py:290
  58.3 1.0 convert_add_fusion
  59.3 10.9 %all-to-all-done.1 = bf16[8,24,1792]{2,1,0:T(8,128)(2,1)S(1)} async-done(((bf16[8,24,1792]{2,1,0:T(8,128)(2,1)}), bf16[8,24,1792]{2,1,0:T(8,128)(2,1)S(1)}, u32[]{:S(2)}, u32[]{:S(2)}) %all-to-all-start.1) | async-done | bytes 688160 | tf_op jit(solution)/shard_map/all_to_all | solution.py:290
  70.3 0.2 multiply_reduce_fusion
  70.5 0.1 multiply_convert_fusion
  70.7 0.7 reshape.179
  71.4 2.5 %collective-permute-start = (bf16[3584,768]{1,0:T(8,128)(2,1)}, bf16[3584,768]{1,0:T(8,128)(2,1)}, u32[]{:S(2)}, u32[]{:S(2)}) collective-permute-start(bf16[3584,768]{1,0:T(8,128)(2,1)} %own_hbm.1), channel_id=1, source_target_pairs={{0,8},{8,0},{1,9},{9,1},{2,10},{10,2},{3,11},{11,3},{4,12},{12,4},... | collective-permute-start | bytes 16515080 | tf_op jit(solution)/shard_map/ppermute | solution.py:317
  74.0 0.2 dynamic-slice_reduce_fusion
  74.2 0.7 pad_add_fusion.first_ref
  74.9 28.6 %regenerate.1.noise_ref = bf16[16,160,3584]{2,1,0:T(8,128)(2,1)} custom-call(s32[16]{0:T(128)S(1)} %copy-done.3), custom_call_target="tpu_custom_call" | custom-call | flops 18350080000 | bytes 18350080 | tf_op jit(solution)/shard_map/regenerate/pallas_call | solution.py:159
  103.5 54.6 %all-gather.2.cloned.1.call-done.rows_hbm = bf16[1536,3712]{1,0:T(8,128)(2,1)} async-done(((bf16[24,3712]{1,0:T(8,128)(2,1)}), bf16[1536,3712]{1,0:T(8,128)(2,1)}) %all-gather.2.cloned.1.call-update) | async-done | bytes 11403280 | tf_op jit(solution)/shard_map/all_gather | solution.py:338
  158.1 25.6 %vocabulary_stats.1 = f32[8,1536]{1,0:T(8,128)} custom-call(s32[2]{0:T(128)} %pad_add_fusion.first_ref, bf16[1536,3712]{1,0:T(8,128)(2,1)} %all-gather.2.cloned.1.call-done.rows_hbm, bf16[3584,768]{1,0:T(8,128)(2,1)} %own_hbm.1, bf16[3584,768]{1,0:T(8,128)(2,1)} %collective-permute-done.other_ref), custom_call_target="tpu_custom_call" | custom-call | flops 16911433728 | bytes 11010048 | tf_op jit(solution)/shard_map/vocabulary_stats/pallas_call | solution.py:232
  183.7 0.8 slice.40
  184.5 0.7 broadcast_in_dim.21
  185.2 6.3 %all-to-all-start.2 = ((f32[8,2,1536]{2,1,0:T(2,128)}), f32[8,2,1536]{2,1,0:T(2,128)S(1)}, u32[]{:S(2)}, u32[]{:S(2)}) async-start(f32[8,2,1536]{2,1,0:T(2,128)} %broadcast_in_dim.21), calls=%async_computation.2 | async-start | bytes 196608 | tf_op jit(solution)/shard_map/all_to_all | solution.py:297
  191.5 6.9 %all-to-all-done.2 = f32[8,2,1536]{2,1,0:T(2,128)S(1)} async-done(((f32[8,2,1536]{2,1,0:T(2,128)}), f32[8,2,1536]{2,1,0:T(2,128)S(1)}, u32[]{:S(2)}, u32[]{:S(2)}) %all-to-all-start.2) | async-done | bytes 98336 | tf_op jit(solution)/shard_map/all_to_all | solution.py:297
  198.4 0.1 slice_reduce_fusion.3
  198.6 0.7 broadcast_in_dim.22
  199.3 3.4 %all-to-all-start.3 = ((f32[8,2,1536]{2,1,0:T(2,128)}), f32[8,2,1536]{2,1,0:T(2,128)S(1)}, u32[]{:S(2)}, u32[]{:S(2)}) async-start(f32[8,2,1536]{2,1,0:T(2,128)} %broadcast_in_dim.22), calls=%async_computation.3 | async-start | bytes 196608 | tf_op jit(solution)/shard_map/all_to_all | solution.py:297
  202.7 0.2 convert_reduce_fusion.1
  202.9 5.0 %all-to-all-done.3 = f32[8,2,1536]{2,1,0:T(2,128)S(1)} async-done(((f32[8,2,1536]{2,1,0:T(2,128)}), f32[8,2,1536]{2,1,0:T(2,128)S(1)}, u32[]{:S(2)}, u32[]{:S(2)}) %all-to-all-start.3) | async-done | bytes 98336 | tf_op jit(solution)/shard_map/all_to_all | solution.py:297
  208.0 0.1 sub.46
  208.2 0.1 multiply_reduce_fusion.1
  208.4 3.2 %collective-permute-start.1 = (f32[8,2]{0,1:T(2,128)S(1)}, f32[8,2]{0,1:T(2,128)S(1)}, u32[]{:S(2)}, u32[]{:S(2)}) collective-permute-start(f32[8,2]{0,1:T(2,128)S(1)} %broadcast_divide_fusion), channel_id=1, source_target_pairs={{0,8},{8,0},{1,9},{9,1},{2,10},{10,2},{3,11},{11,3},{4,12},{12,4},... | collective-permute-start | bytes 200 | tf_op jit(solution)/shard_map/ppermute | solution.py:352
  211.7 0.8 collective-permute-done.1
  212.8 0.1 reduce_sum.92.gap_ref
  212.9 9.1 %update.1 = f32[148,3584]{1,0:T(8,128)} custom-call(f32[16]{0:T(128)S(1)} %reduce_sum.92.gap_ref, bf16[16,160,3584]{2,1,0:T(8,128)(2,1)} %regenerate.1.noise_ref), custom_call_target="tpu_custom_call" | custom-call | flops 16973824 | bytes 18350080 | tf_op jit(solution)/shard_map/update/pallas_call | solution.py:272
  (52 shorter events, 1.4 us)
Async XLA Ops:
  7.2 21.1 %copy-start = (s32[1,128]{1,0:T(1,128)S(1)}, s32[1,128]{1,0:T(1,128)}, u32[]{:S(2)}) copy-start(s32[1,128]{1,0:T(1,128)} %param.14) | copy-start | bytes 1540
  8.6 0.7 copy-start.2
  9.2 19.0 %copy-start.7 = (s32[32]{0:T(128)S(1)}, s32[32]{0:T(128)}, u32[]{:S(2)}) copy-start(s32[32]{0:T(128)} %param.17) | copy-start | bytes 388
  9.2 19.2 %copy-start.3 = (s32[16]{0:T(128)S(1)}, s32[16]{0:T(128)}, u32[]{:S(2)}) copy-start(s32[16]{0:T(128)} %seeds_ref.4) | copy-start | bytes 196
  19.6 31.8 %all-to-all-start = ((f32[8,24,1792]{2,1,0:T(8,128)}), f32[8,24,1792]{2,1,0:T(8,128)S(1)}, u32[]{:S(2)}, u32[]{:S(2)}) async-start(f32[8,24,1792]{2,1,0:T(8,128)} %get-tuple-element.11), calls=%async_computation | async-start | bytes 2752512 | tf_op jit(solution)/shard_map/all_to_all | solution.py:290
  51.4 19.1 %copy-start.4 = (f32[3584]{0:T(1024)S(1)}, f32[3584]{0:T(1024)}, u32[]{:S(2)}) copy-start(f32[3584]{0:T(1024)} %param.12) | copy-start | bytes 43012
  51.5 22.5 %copy-start.5 = (s32[16]{0:T(128)S(1)}, s32[16]{0:T(128)}, u32[]{:S(2)}) copy-start(s32[16]{0:T(128)} %param.15) | copy-start | bytes 196
  51.6 18.5 %all-to-all-start.1 = ((bf16[8,24,1792]{2,1,0:T(8,128)(2,1)}), bf16[8,24,1792]{2,1,0:T(8,128)(2,1)S(1)}, u32[]{:S(2)}, u32[]{:S(2)}) async-start(bf16[8,24,1792]{2,1,0:T(8,128)(2,1)} %probe.1), calls=%async_computation.1 | async-start | bytes 1376256 | tf_op jit(solution)/shard_map/all_to_all | solution.py:290
  58.2 99.8 %all-gather.2.cloned.1.call-start = ((), (), s32[]{:S(2)}) async-start(), calls=%async_computation.4 | async-start | bytes 11581440 | tf_op jit(solution)/shard_map/all_gather | solution.py:338
  71.4 32.0 %collective-permute-start = (bf16[3584,768]{1,0:T(8,128)(2,1)}, bf16[3584,768]{1,0:T(8,128)(2,1)}, u32[]{:S(2)}, u32[]{:S(2)}) collective-permute-start(bf16[3584,768]{1,0:T(8,128)(2,1)} %own_hbm.1), channel_id=1, source_target_pairs={{0,8},{8,0},{1,9},{9,1},{2,10},{10,2},{3,11},{11,3},{4,12},{12,4},... | collective-permute-start | bytes 16515080 | tf_op jit(solution)/shard_map/ppermute | solution.py:317
  185.2 13.2 %all-to-all-start.2 = ((f32[8,2,1536]{2,1,0:T(2,128)}), f32[8,2,1536]{2,1,0:T(2,128)S(1)}, u32[]{:S(2)}, u32[]{:S(2)}) async-start(f32[8,2,1536]{2,1,0:T(2,128)} %broadcast_in_dim.21), calls=%async_computation.2 | async-start | bytes 196608 | tf_op jit(solution)/shard_map/all_to_all | solution.py:297
  199.3 8.6 %all-to-all-start.3 = ((f32[8,2,1536]{2,1,0:T(2,128)}), f32[8,2,1536]{2,1,0:T(2,128)S(1)}, u32[]{:S(2)}, u32[]{:S(2)}) async-start(f32[8,2,1536]{2,1,0:T(2,128)} %broadcast_in_dim.22), calls=%async_computation.3 | async-start | bytes 196608 | tf_op jit(solution)/shard_map/all_to_all | solution.py:297
  208.4 4.1 %collective-permute-start.1 = (f32[8,2]{0,1:T(2,128)S(1)}, f32[8,2]{0,1:T(2,128)S(1)}, u32[]{:S(2)}, u32[]{:S(2)}) collective-permute-start(f32[8,2]{0,1:T(2,128)S(1)} %broadcast_divide_fusion), channel_id=1, source_target_pairs={{0,8},{8,0},{1,9},{9,1},{2,10},{10,2},{3,11},{11,3},{4,12},{12,4},... | collective-permute-start | bytes 200 | tf_op jit(solution)/shard_map/ppermute | solution.py:352
  212.7 9.3 %copy-start.6 = (f32[32]{0:T(128)}, f32[32]{0:T(128)S(1)}, u32[]{:S(2)}) copy-start(f32[32]{0:T(128)S(1)} %select_n.37) | copy-start | bytes 388
  212.8 9.2 %copy-start.1 = (s32[1,128]{1,0:T(1,128)S(1)}, s32[1,128]{1,0:T(1,128)}, u32[]{:S(2)}) copy-start(s32[1,128]{1,0:T(1,128)} %param.14) | copy-start | bytes 1540
Sparse Core Ops, SparseCore 0:
  71.6 86.4 all-gather.1

commit v4 on v3

--- a/solution.py
+++ b/solution.py
@@ -80,22 +80,25 @@
         copies.append(pltpu.make_async_copy(weight_hbm.at[:, cols], weight_ref.at[c], sems.at[c]))
         copies[-1].start()
     for step in range(steps):
-        put_shares(probe_ref, slice(step * 128, step * 128 + 128), *probe_step(seeds_ref, hidden_ref, step))
-        if step + 2 < steps:
-            continue
         c = 2 * (step + 2 - steps)
-        sides = []
-        for side in (c, c + 1):
-            copies[side].wait()
-            sides.append(jnp.dot(hidden_ref[SKIP:, :], weight_ref[side], preferred_element_type=jnp.float32))
-        put_shares(base_ref, slice((c // 2) * wide, (c // 2 + 1) * wide), *sides)
+        if c >= 0:
+            copies[c].wait()
+            copies[c + 1].wait()
+        probe_sides = probe_step(seeds_ref, hidden_ref, step)
+        if c >= 0:
+            sides = [
+                jnp.dot(hidden_ref[SKIP:, :], weight_ref[side], preferred_element_type=jnp.float32)
+                for side in (c, c + 1)
+            ]
+            put_shares(base_ref, slice((c // 2) * wide, (c // 2 + 1) * wide), *sides)
+        put_shares(probe_ref, slice(step * 128, step * 128 + 128), *probe_sides)
 
 
 def rest_kernel(seeds_ref, hidden_ref, _, probe_ref, *, first_step):
     put_shares(probe_ref, slice(None), *probe_step(seeds_ref, hidden_ref, pl.program_id(0) + first_step))
 
 
-def products(seeds, hidden, weight, shares, first_steps=2):
+def products(seeds, hidden, weight, shares, first_steps=4):
     tokens, units = hidden.shape
     share = (tokens - SKIP) // shares
     half = D // 2
@@ -145,23 +148,23 @@
     def rows16(r, _):
         first = pl.multiple_of(r * 16, 16)
         for c in range(0, D, width):
-            out_ref[0, pl.ds(first, 16), c : c + width] = noise_of(
+            out_ref[c // width, 0, pl.ds(first, 16), :] = noise_of(
                 flat_index(16, width, D) + (at + r * (16 * D) + c)
             )
         return 0
 
-    lax.fori_loop(0, out_ref.shape[1] // 16, rows16, 0)
-
-
-def regenerate(seeds, rows):
+    lax.fori_loop(0, out_ref.shape[2] // 16, rows16, 0)
+
+
+def regenerate(seeds, rows, width=512):
     pairs = seeds.shape[0]
     padded = -(-rows // 16) * 16
     return pl.pallas_call(
-        functools.partial(regenerate_kernel, width=512, out_rows=rows),
+        functools.partial(regenerate_kernel, width=width, out_rows=rows),
         grid=(pairs,),
         in_specs=[pl.BlockSpec(memory_space=pltpu.SMEM)],
-        out_specs=pl.BlockSpec((1, padded, D), lambda p: (p, 0, 0)),
-        out_shape=jax.ShapeDtypeStruct((pairs, padded, D), jnp.bfloat16),
+        out_specs=pl.BlockSpec((D // width, 1, padded, width), lambda p: (0, p, 0, 0)),
+        out_shape=jax.ShapeDtypeStruct((D // width, pairs, padded, width), jnp.bfloat16),
         cost_estimate=pl.CostEstimate(
             flops=pairs * padded * D * 2000, bytes_accessed=pairs * padded * D * 2, transcendentals=0
         ),
@@ -171,7 +174,7 @@
 
 
 def logits_kernel(
-    first_ref, rows_hbm, own_hbm, other_ref, out_ref, rows_ref, own_ref, held_ref, stats_ref, sems, own_sem
+    first_ref, rows_hbm, own_hbm, other_hbm, out_ref, rows_ref, own_ref, other_ref, held_ref, stats_ref, sems, head_sems
 ):
     slots, chunk, _ = rows_ref.shape
     chunks = rows_hbm.shape[0] // chunk
@@ -183,12 +186,27 @@
             rows_hbm.at[pl.ds(i * chunk, chunk), :], rows_ref.at[i % slots], sems.at[i % slots]
         )
 
+    early = vocab // 3
+    heads = [
+        pltpu.make_async_copy(own_hbm.at[:, :early], own_ref.at[:, :early], head_sems.at[0]),
+        pltpu.make_async_copy(own_hbm.at[:, early:], own_ref.at[:, early:], head_sems.at[1]),
+        pltpu.make_async_copy(other_hbm, other_ref, head_sems.at[2]),
+    ]
+
     def multiply(i):
         rows = rows_ref[i % slots, :, :D]
-        held_ref[i % 2, :, vocab:] = jnp.dot(rows, other_ref[...], preferred_element_type=jnp.float32)
         if i == 0:
-            own.wait()
-        held_ref[i % 2, :, :vocab] = jnp.dot(rows, own_ref[...], preferred_element_type=jnp.float32)
+            for copy, ref, cols, at in (
+                (heads[0], own_ref, slice(0, early), 0),
+                (heads[1], own_ref, slice(early, vocab), early),
+                (heads[2], other_ref, slice(0, vocab), vocab),
+            ):
+                copy.wait()
+                made = jnp.dot(rows, ref[:, cols], preferred_element_type=jnp.float32)
+                held_ref[0, :, at : at + made.shape[1]] = made
+        else:
+            held_ref[i % 2, :, :vocab] = jnp.dot(rows, own_ref[...], preferred_element_type=jnp.float32)
+            held_ref[i % 2, :, vocab:] = jnp.dot(rows, other_ref[...], preferred_element_type=jnp.float32)
 
     def absorb(i):
         slot = i % 2
@@ -211,8 +229,8 @@
         stats_ref[i * chunk : (i + 1) * chunk, :] = jnp.where(lane == 0, high + jnp.log(total), hit)
 
     fetch(0).start()
-    own = pltpu.make_async_copy(own_hbm, own_ref, own_sem)
-    own.start()
+    for copy in heads:
+        copy.start()
     for i in range(1, min(slots - 1, chunks)):
         fetch(i).start()
     for i in range(chunks):
@@ -223,10 +241,12 @@
         if i + slots - 1 < chunks:
             fetch(i + slots - 1).start()
     absorb(chunks - 1)
-    out_ref[...] = stats_ref[...].T[:8, :]
-
-
-def vocabulary_stats(rows, own_head, other_head, firsts, chunk=256, slots=4):
+    both = stats_ref[...].T[:2, :]
+    for t in range(out_ref.shape[0]):
+        out_ref[t] = both
+
+
+def vocabulary_stats(rows, own_head, other_head, firsts, copies, chunk=256, slots=4):
     count = rows.shape[0]
     vocab = own_head.shape[1]
     return pl.pallas_call(
@@ -235,17 +255,18 @@
             pl.BlockSpec(memory_space=pltpu.SMEM),
             pl.BlockSpec(memory_space=pl.ANY),
             pl.BlockSpec(memory_space=pl.ANY),
-            pl.BlockSpec(memory_space=pltpu.VMEM),
+            pl.BlockSpec(memory_space=pl.ANY),
         ],
         out_specs=pl.BlockSpec(memory_space=pltpu.VMEM),
-        out_shape=jax.ShapeDtypeStruct((8, count), jnp.float32),
+        out_shape=jax.ShapeDtypeStruct((copies, 2, count), jnp.float32),
         scratch_shapes=[
             pltpu.VMEM((slots, chunk, D + EXTRA), jnp.bfloat16),
+            pltpu.VMEM((D, vocab), jnp.bfloat16),
             pltpu.VMEM((D, vocab), jnp.bfloat16),
             pltpu.VMEM((2, chunk, 2 * vocab), jnp.float32),
             pltpu.VMEM((count, 128), jnp.float32),
             pltpu.SemaphoreType.DMA((slots,)),
-            pltpu.SemaphoreType.DMA,
+            pltpu.SemaphoreType.DMA((3,)),
         ],
         cost_estimate=pl.CostEstimate(
             flops=2 * count * D * 2 * vocab, bytes_accessed=count * D * 2, transcendentals=0
@@ -257,27 +278,27 @@
 
 def update_kernel(gap_ref, noise_ref, out_ref):
     rows = out_ref.shape[0]
-    pairs = noise_ref.shape[0]
+    pairs = noise_ref.shape[1]
     for r in range(0, rows, 16):
         deep = min(16, rows - r)
         total = None
         for p in range(pairs):
-            term = gap_ref[p] * noise_ref[p, r : r + 16, :].astype(jnp.float32)
+            term = gap_ref[p] * noise_ref[0, p, r : r + 16, :].astype(jnp.float32)
             total = term if total is None else total + term
         out_ref[r : r + deep, :] = total[:deep]
 
 
-def update(gap, noise, rows, tile=896):
-    pairs, padded, _ = noise.shape
+def update(gap, noise, rows):
+    slabs, pairs, padded, width = noise.shape
     return pl.pallas_call(
         update_kernel,
-        grid=(D // tile,),
+        grid=(slabs,),
         in_specs=[
             pl.BlockSpec(memory_space=pltpu.SMEM),
-            pl.BlockSpec((pairs, padded, tile), lambda c: (0, 0, c)),
+            pl.BlockSpec((1, pairs, padded, width), lambda c: (c, 0, 0, 0)),
         ],
-        out_specs=pl.BlockSpec((rows, tile), lambda c: (0, c)),
-        out_shape=jax.ShapeDtypeStruct((rows, D), jnp.float32),
+        out_specs=pl.BlockSpec((rows, width), lambda c: (0, c)),
+        out_shape=jax.ShapeDtypeStruct((rows, slabs * width), jnp.float32),
         cost_estimate=pl.CostEstimate(
             flops=2 * pairs * rows * D, bytes_accessed=2 * pairs * padded * D, transcendentals=0
         ),
@@ -293,8 +314,8 @@
     return jnp.concatenate([total[:share], total[share:]], axis=1)
 
 
-def joined(stats, axes, count):
-    everyone = lax.all_to_all(jnp.broadcast_to(stats[None], (count,) + stats.shape), axes, 0, 0)
+def joined(stats, axes):
+    everyone = lax.all_to_all(stats, axes, 0, 0)
     level = everyone[:, 0]
     top = jnp.max(level, axis=0)
     level = top + jnp.log(jnp.sum(jnp.exp(level - top[None]), axis=0))
@@ -341,9 +362,8 @@
     own_vocab = (pop_at * tp_count + tp_at) * vocab
     other_vocab = ((pop_at + 1 - 2 * core) * tp_count + tp_at) * vocab
     firsts, noise = lax.optimization_barrier((jnp.stack([own_vocab, other_vocab]), noise))
-    stats = vocabulary_stats(rows, head, other_head, firsts)[:2]
-    stats = joined(stats, TP, tp_count)
-    stats = joined(stats, ("y_lo", "x"), chip_pairs)
+    stats = joined(vocabulary_stats(rows, head, other_head, firsts, tp_count), TP)
+    stats = joined(jnp.broadcast_to(stats[None], (chip_pairs,) + stats.shape), ("y_lo", "x"))
     log_prob = (stats[1] - stats[0]).reshape(tp_count, chip_pairs, 2, share)
     positions = SKIP + jnp.arange(scored, dtype=jnp.int32).reshape(tp_count, 1, share)
     own_starts = lax.dynamic_index_in_dim(answer_start.reshape(chip_pairs, 2), core, 1, keepdims=False)

time: 229 us -> 229 us (level)
    pallas_call x1, Pallas kernels: 23 us -> 19.4 us  [products(): pl.pallas_call(functools.partial(rest_kernel, first_step=first_steps), gr...]
    pallas_call x1, Pallas kernels: 10.4 us -> 14 us  [products(): pl.pallas_call(functools.partial(first_kernel, steps=first_steps), grid=(...]
  transfers between devices with their start and end apart: 7 -> 7, of which waited for: 5 -> 6; matrix products, arithmetic and copies ran while one was open for 1% -> 1% of each run, Pallas kernels for 23% -> 21%
where the time goes in v4:
time: 229 us
  Pallas kernels  98 us (43%)
  waiting for transfers between devices  78.2 us (34%)
  starting transfers between devices  30.5 us (13%)
  between operations  14.3 us (6%)
  local copies, waits for them, and re-layouts  4.33 us (2%)
  other arithmetic  3.25 us (1%)
    all_gather x1, waiting for transfers between devices, local(): lax.all_gather(normed.reshape(2 * share, D + EXTRA), SAME_CORE, axis=0, t...  54.5 us
    pallas_call x1, Pallas kernels, regenerate(): pl.pallas_call(functools.partial(regenerate_kernel, width=width, out_rows...  28.6 us
    pallas_call x1, Pallas kernels, vocabulary_stats(): pl.pallas_call(logits_kernel, in_specs=[pl.BlockSpec(memory_space=pltpu.S...  25.3 us
    pallas_call x1, Pallas kernels, products(): pl.pallas_call(functools.partial(rest_kernel, first_step=first_steps), gr...  19.4 us
    all_to_all x2, starting transfers between devices, scattered_sum(): pieces = lax.all_to_all(partial, axes, 0, 0)  15 us
    pallas_call x1, Pallas kernels, products(): pl.pallas_call(functools.partial(first_kernel, steps=first_steps), grid=(...  14 us
    all_to_all x2, waiting for transfers between devices, joined(): everyone = lax.all_to_all(stats, axes, 0, 0)  11.8 us
    all_to_all x2, waiting for transfers between devices, scattered_sum(): pieces = lax.all_to_all(partial, axes, 0, 0)  11 us
  transfers between devices with their start and end apart: 7, of which 6 were waited for; matrix products, arithmetic and copies ran while one was open for 1% of the time, Pallas kernels for 21%

profile of v4, /device:TPU:1, one launch (start us, length us, event | category | flops | bytes accessed | tf_op | source)
XLA Modules:
  0.0 228.6 jit_solution(2144346039147316193)
XLA Ops:
  7.2 1.4 copy.21
  8.6 0.6 copy-done.2
  9.2 14.0 %base_and_probe.1 = (bf16[8,24,1792]{2,1,0:T(8,128)(2,1)}, f32[8,24,1792]{2,1,0:T(8,128)}) custom-call(s32[16]{0:T(128)S(1)} %copy-done.2, bf16[128,2368]{1,0:T(8,128)(2,1)S(1)} %bitcast.23, bf16[2368,3584]{1,0:T(8,128)(2,1)} %weight_hbm.1), custom_call_target="tpu_custom_call" | custom-call | flops 4849664000 | bytes 2424832 | tf_op jit(solution)/shard_map/base_and_probe/pallas_call | solution.py:115
  23.3 8.5 %all-to-all-start = ((f32[8,24,1792]{2,1,0:T(8,128)}), f32[8,24,1792]{2,1,0:T(8,128)S(1)}, u32[]{:S(2)}, u32[]{:S(2)}) async-start(f32[8,24,1792]{2,1,0:T(8,128)} %get-tuple-element.11), calls=%async_computation | async-start | bytes 2752512 | tf_op jit(solution)/shard_map/all_to_all | solution.py:311
  32.0 19.4 %probe.1 = bf16[8,24,1792]{2,1,0:T(8,128)(2,1)} custom-call(s32[16]{0:T(128)S(1)} %copy-done.3, bf16[128,2368]{1,0:T(8,128)(2,1)S(1)} %bitcast.24, bf16[8,24,1792]{2,1,0:T(8,128)(2,1)} %get-tuple-element.10._), custom_call_target="tpu_custom_call", output_to_operand_aliasing={{}: (2, {})} | custom-call | flops 12124160000 | bytes 6062080 | tf_op jit(solution)/shard_map/probe/pallas_call | solution.py:129
  51.4 0.1 all-to-all-done
  51.7 6.5 %all-to-all-start.1 = ((bf16[8,24,1792]{2,1,0:T(8,128)(2,1)}), bf16[8,24,1792]{2,1,0:T(8,128)(2,1)S(1)}, u32[]{:S(2)}, u32[]{:S(2)}) async-start(bf16[8,24,1792]{2,1,0:T(8,128)(2,1)} %probe.1), calls=%async_computation.1 | async-start | bytes 1376256 | tf_op jit(solution)/shard_map/all_to_all | solution.py:311
  58.3 1.0 convert_add_fusion
  59.2 10.8 %all-to-all-done.1 = bf16[8,24,1792]{2,1,0:T(8,128)(2,1)S(1)} async-done(((bf16[8,24,1792]{2,1,0:T(8,128)(2,1)}), bf16[8,24,1792]{2,1,0:T(8,128)(2,1)S(1)}, u32[]{:S(2)}, u32[]{:S(2)}) %all-to-all-start.1) | async-done | bytes 688160 | tf_op jit(solution)/shard_map/all_to_all | solution.py:311
  70.2 0.2 multiply_reduce_fusion
  70.5 0.1 multiply_convert_fusion
  70.7 0.7 reshape.178
  71.4 2.5 %collective-permute-start = (bf16[3584,768]{1,0:T(8,128)(2,1)}, bf16[3584,768]{1,0:T(8,128)(2,1)}, u32[]{:S(2)}, u32[]{:S(2)}) collective-permute-start(bf16[3584,768]{1,0:T(8,128)(2,1)} %own_hbm.1), channel_id=1, source_target_pairs={{0,8},{8,0},{1,9},{9,1},{2,10},{10,2},{3,11},{11,3},{4,12},{12,4},... | collective-permute-start | bytes 16515080 | tf_op jit(solution)/shard_map/ppermute | solution.py:338
  74.0 0.2 dynamic-slice_reduce_fusion
  74.2 0.7 pad_add_fusion.first_ref
  74.9 28.6 %regenerate.1.noise_ref = bf16[7,16,160,512]{3,2,1,0:T(8,128)(2,1)} custom-call(s32[16]{0:T(128)S(1)} %copy-done.3), custom_call_target="tpu_custom_call" | custom-call | flops 18350080000 | bytes 18350080 | tf_op jit(solution)/shard_map/regenerate/pallas_call | solution.py:162
  103.5 54.5 %all-gather.2.cloned.1.call-done.rows_hbm = bf16[1536,3712]{1,0:T(8,128)(2,1)} async-done(((bf16[24,3712]{1,0:T(8,128)(2,1)}), bf16[1536,3712]{1,0:T(8,128)(2,1)}) %all-gather.2.cloned.1.call-update) | async-done | bytes 11403280 | tf_op jit(solution)/shard_map/all_gather | solution.py:359
  158.0 25.3 %vocabulary_stats.1 = f32[8,2,1536]{2,1,0:T(2,128)} custom-call(s32[2]{0:T(128)} %pad_add_fusion.first_ref, bf16[1536,3712]{1,0:T(8,128)(2,1)} %all-gather.2.cloned.1.call-done.rows_hbm, bf16[3584,768]{1,0:T(8,128)(2,1)} %own_hbm.1, bf16[3584,768]{1,0:T(8,128)(2,1)} %collective-permute-done.other_hbm), custom_call_target="tpu_custom_call" | custom-call | flops 16911433728 | bytes 11010048 | tf_op jit(solution)/shard_map/vocabulary_stats/pallas_call | solution.py:252
  183.4 6.3 %all-to-all-start.2 = ((f32[8,2,1536]{2,1,0:T(2,128)}), f32[8,2,1536]{2,1,0:T(2,128)S(1)}, u32[]{:S(2)}, u32[]{:S(2)}) async-start(f32[8,2,1536]{2,1,0:T(2,128)} %vocabulary_stats.1), calls=%async_computation.2 | async-start | bytes 196608 | tf_op jit(solution)/shard_map/all_to_all | solution.py:318
  189.7 6.9 %all-to-all-done.2 = f32[8,2,1536]{2,1,0:T(2,128)S(1)} async-done(((f32[8,2,1536]{2,1,0:T(2,128)}), f32[8,2,1536]{2,1,0:T(2,128)S(1)}, u32[]{:S(2)}, u32[]{:S(2)}) %all-to-all-start.2) | async-done | bytes 98336 | tf_op jit(solution)/shard_map/all_to_all | solution.py:318
  196.6 0.1 slice_reduce_fusion.3
  196.8 0.7 broadcast_in_dim.19
  197.5 3.4 %all-to-all-start.3 = ((f32[8,2,1536]{2,1,0:T(2,128)}), f32[8,2,1536]{2,1,0:T(2,128)S(1)}, u32[]{:S(2)}, u32[]{:S(2)}) async-start(f32[8,2,1536]{2,1,0:T(2,128)} %broadcast_in_dim.19), calls=%async_computation.3 | async-start | bytes 196608 | tf_op jit(solution)/shard_map/all_to_all | solution.py:318
  200.9 0.2 convert_reduce_fusion.1
  201.1 5.0 %all-to-all-done.3 = f32[8,2,1536]{2,1,0:T(2,128)S(1)} async-done(((f32[8,2,1536]{2,1,0:T(2,128)}), f32[8,2,1536]{2,1,0:T(2,128)S(1)}, u32[]{:S(2)}, u32[]{:S(2)}) %all-to-all-start.3) | async-done | bytes 98336 | tf_op jit(solution)/shard_map/all_to_all | solution.py:318
  206.1 0.1 slice_reduce_fusion.2
  206.2 0.1 sub.46
  206.4 0.1 multiply_reduce_fusion.1
  206.6 3.3 %collective-permute-start.1 = (f32[8,2]{0,1:T(2,128)S(1)}, f32[8,2]{0,1:T(2,128)S(1)}, u32[]{:S(2)}, u32[]{:S(2)}) collective-permute-start(f32[8,2]{0,1:T(2,128)S(1)} %broadcast_divide_fusion), channel_id=1, source_target_pairs={{0,8},{8,0},{1,9},{9,1},{2,10},{10,2},{3,11},{11,3},{4,12},{12,4},... | collective-permute-start | bytes 200 | tf_op jit(solution)/shard_map/ppermute | solution.py:372
  209.9 0.8 collective-permute-done.1
  211.0 0.1 reduce_sum.92.gap_ref
  211.1 10.6 %update.1 = f32[148,3584]{1,0:T(8,128)} custom-call(f32[16]{0:T(128)S(1)} %reduce_sum.92.gap_ref, bf16[7,16,160,512]{3,2,1,0:T(8,128)(2,1)} %regenerate.1.noise_ref), custom_call_target="tpu_custom_call" | custom-call | flops 16973824 | bytes 18350080 | tf_op jit(solution)/shard_map/update/pallas_call | solution.py:293
  (50 shorter events, 1.3 us)
Async XLA Ops:
  7.2 24.6 %copy-start = (s32[1,128]{1,0:T(1,128)S(1)}, s32[1,128]{1,0:T(1,128)}, u32[]{:S(2)}) copy-start(s32[1,128]{1,0:T(1,128)} %param.14) | copy-start | bytes 1540
  8.6 0.7 copy-start.2
  9.2 22.7 %copy-start.7 = (s32[32]{0:T(128)S(1)}, s32[32]{0:T(128)}, u32[]{:S(2)}) copy-start(s32[32]{0:T(128)} %param.17) | copy-start | bytes 388
  9.2 22.8 %copy-start.3 = (s32[16]{0:T(128)S(1)}, s32[16]{0:T(128)}, u32[]{:S(2)}) copy-start(s32[16]{0:T(128)} %seeds_ref.4) | copy-start | bytes 196
  23.3 28.3 %all-to-all-start = ((f32[8,24,1792]{2,1,0:T(8,128)}), f32[8,24,1792]{2,1,0:T(8,128)S(1)}, u32[]{:S(2)}, u32[]{:S(2)}) async-start(f32[8,24,1792]{2,1,0:T(8,128)} %get-tuple-element.11), calls=%async_computation | async-start | bytes 2752512 | tf_op jit(solution)/shard_map/all_to_all | solution.py:311
  51.4 19.0 %copy-start.4 = (f32[3584]{0:T(1024)S(1)}, f32[3584]{0:T(1024)}, u32[]{:S(2)}) copy-start(f32[3584]{0:T(1024)} %param.12) | copy-start | bytes 43012
  51.4 22.5 %copy-start.5 = (s32[16]{0:T(128)S(1)}, s32[16]{0:T(128)}, u32[]{:S(2)}) copy-start(s32[16]{0:T(128)} %param.15) | copy-start | bytes 196
  51.7 18.4 %all-to-all-start.1 = ((bf16[8,24,1792]{2,1,0:T(8,128)(2,1)}), bf16[8,24,1792]{2,1,0:T(8,128)(2,1)S(1)}, u32[]{:S(2)}, u32[]{:S(2)}) async-start(bf16[8,24,1792]{2,1,0:T(8,128)(2,1)} %probe.1), calls=%async_computation.1 | async-start | bytes 1376256 | tf_op jit(solution)/shard_map/all_to_all | solution.py:311
  58.2 99.8 %all-gather.2.cloned.1.call-start = ((), (), s32[]{:S(2)}) async-start(), calls=%async_computation.4 | async-start | bytes 11581440 | tf_op jit(solution)/shard_map/all_gather | solution.py:359
  71.4 32.1 %collective-permute-start = (bf16[3584,768]{1,0:T(8,128)(2,1)}, bf16[3584,768]{1,0:T(8,128)(2,1)}, u32[]{:S(2)}, u32[]{:S(2)}) collective-permute-start(bf16[3584,768]{1,0:T(8,128)(2,1)} %own_hbm.1), channel_id=1, source_target_pairs={{0,8},{8,0},{1,9},{9,1},{2,10},{10,2},{3,11},{11,3},{4,12},{12,4},... | collective-permute-start | bytes 16515080 | tf_op jit(solution)/shard_map/ppermute | solution.py:338
  183.4 13.2 %all-to-all-start.2 = ((f32[8,2,1536]{2,1,0:T(2,128)}), f32[8,2,1536]{2,1,0:T(2,128)S(1)}, u32[]{:S(2)}, u32[]{:S(2)}) async-start(f32[8,2,1536]{2,1,0:T(2,128)} %vocabulary_stats.1), calls=%async_computation.2 | async-start | bytes 196608 | tf_op jit(solution)/shard_map/all_to_all | solution.py:318
  197.5 8.6 %all-to-all-start.3 = ((f32[8,2,1536]{2,1,0:T(2,128)}), f32[8,2,1536]{2,1,0:T(2,128)S(1)}, u32[]{:S(2)}, u32[]{:S(2)}) async-start(f32[8,2,1536]{2,1,0:T(2,128)} %broadcast_in_dim.19), calls=%async_computation.3 | async-start | bytes 196608 | tf_op jit(solution)/shard_map/all_to_all | solution.py:318
  206.6 4.1 %collective-permute-start.1 = (f32[8,2]{0,1:T(2,128)S(1)}, f32[8,2]{0,1:T(2,128)S(1)}, u32[]{:S(2)}, u32[]{:S(2)}) collective-permute-start(f32[8,2]{0,1:T(2,128)S(1)} %broadcast_divide_fusion), channel_id=1, source_target_pairs={{0,8},{8,0},{1,9},{9,1},{2,10},{10,2},{3,11},{11,3},{4,12},{12,4},... | collective-permute-start | bytes 200 | tf_op jit(solution)/shard_map/ppermute | solution.py:372
  210.9 10.9 %copy-start.6 = (f32[32]{0:T(128)}, f32[32]{0:T(128)S(1)}, u32[]{:S(2)}) copy-start(f32[32]{0:T(128)S(1)} %select_n.37) | copy-start | bytes 388
  211.0 10.8 %copy-start.1 = (s32[1,128]{1,0:T(1,128)S(1)}, s32[1,128]{1,0:T(1,128)}, u32[]{:S(2)}) copy-start(s32[1,128]{1,0:T(1,128)} %param.14) | copy-start | bytes 1540
Sparse Core Ops, SparseCore 0:
  71.5 86.4 all-gather.1

commit v5 on v4

--- a/solution.py
+++ b/solution.py
@@ -37,10 +37,6 @@
     h = h * jnp.int32(MUL_B)
     bits = (h ^ shifted(h, 15)) & jnp.int32(16777215)
     return ((bits.astype(jnp.float32) - 8388607.5) * jnp.float32(root_three / 8388608.0)).astype(jnp.bfloat16)
-
-
-def flat_index(rows, cols, width):
-    return lax.broadcasted_iota(jnp.int32, (rows, cols), 0) * width + lax.broadcasted_iota(jnp.int32, (rows, cols), 1)
 
 
 def places():
@@ -80,25 +76,20 @@
         copies.append(pltpu.make_async_copy(weight_hbm.at[:, cols], weight_ref.at[c], sems.at[c]))
         copies[-1].start()
     for step in range(steps):
-        c = 2 * (step + 2 - steps)
-        if c >= 0:
-            copies[c].wait()
-            copies[c + 1].wait()
-        probe_sides = probe_step(seeds_ref, hidden_ref, step)
-        if c >= 0:
-            sides = [
-                jnp.dot(hidden_ref[SKIP:, :], weight_ref[side], preferred_element_type=jnp.float32)
-                for side in (c, c + 1)
-            ]
-            put_shares(base_ref, slice((c // 2) * wide, (c // 2 + 1) * wide), *sides)
-        put_shares(probe_ref, slice(step * 128, step * 128 + 128), *probe_sides)
+        put_shares(probe_ref, slice(step * 128, step * 128 + 128), *probe_step(seeds_ref, hidden_ref, step))
+    for c in range(0, 4, 2):
+        sides = []
+        for side in (c, c + 1):
+            copies[side].wait()
+            sides.append(jnp.dot(hidden_ref[SKIP:, :], weight_ref[side], preferred_element_type=jnp.float32))
+        put_shares(base_ref, slice((c // 2) * wide, (c // 2 + 1) * wide), *sides)
 
 
 def rest_kernel(seeds_ref, hidden_ref, _, probe_ref, *, first_step):
     put_shares(probe_ref, slice(None), *probe_step(seeds_ref, hidden_ref, pl.program_id(0) + first_step))
 
 
-def products(seeds, hidden, weight, shares, first_steps=4):
+def products(seeds, hidden, weight, shares, first_steps=2):
     tokens, units = hidden.shape
     share = (tokens - SKIP) // shares
     half = D // 2
@@ -140,37 +131,31 @@
     return probe, base
 
 
-def regenerate_kernel(seeds_ref, out_ref, *, width, out_rows):
+def regenerate_kernel(seeds_ref, out_ref, *, out_rows):
+    slabs, depth, width = out_ref.shape
+    pairs = seeds_ref.shape[0]
     pop_at, tp_at = places()
-    pair = pl.program_id(0)
-    at = seeds_ref[pair] * jnp.int32(1540483477) + (pop_at * lax.axis_size("z") * 2 + tp_at) * jnp.int32(out_rows * D)
-
-    def rows16(r, _):
-        first = pl.multiple_of(r * 16, 16)
-        for c in range(0, D, width):
-            out_ref[c // width, 0, pl.ds(first, 16), :] = noise_of(
-                flat_index(16, width, D) + (at + r * (16 * D) + c)
-            )
-        return 0
-
-    lax.fori_loop(0, out_ref.shape[2] // 16, rows16, 0)
-
-
-def regenerate(seeds, rows, width=512):
+    first = (pop_at * lax.axis_size("z") * 2 + tp_at) * out_rows + pl.program_id(0) * (depth // pairs)
+    index = seeds_ref[...] * jnp.int32(1540483477) + lax.broadcasted_iota(jnp.int32, (pairs, width), 1)
+    for r in range(depth // pairs):
+        for c in range(slabs):
+            out_ref[c, r * pairs : (r + 1) * pairs, :] = noise_of(index + ((first + r) * D + c * width))
+
+
+def regenerate(seeds, rows, width=512, rows_each=4):
     pairs = seeds.shape[0]
-    padded = -(-rows // 16) * 16
     return pl.pallas_call(
-        functools.partial(regenerate_kernel, width=width, out_rows=rows),
-        grid=(pairs,),
-        in_specs=[pl.BlockSpec(memory_space=pltpu.SMEM)],
-        out_specs=pl.BlockSpec((D // width, 1, padded, width), lambda p: (0, p, 0, 0)),
-        out_shape=jax.ShapeDtypeStruct((D // width, pairs, padded, width), jnp.bfloat16),
+        functools.partial(regenerate_kernel, out_rows=rows),
+        grid=(rows // rows_each,),
+        in_specs=[pl.BlockSpec((pairs, 1), lambda i: (0, 0))],
+        out_specs=pl.BlockSpec((D // width, rows_each * pairs, width), lambda i: (0, i, 0)),
+        out_shape=jax.ShapeDtypeStruct((D // width, rows * pairs, width), jnp.bfloat16),
         cost_estimate=pl.CostEstimate(
-            flops=pairs * padded * D * 2000, bytes_accessed=pairs * padded * D * 2, transcendentals=0
+            flops=pairs * rows * D * 2000, bytes_accessed=pairs * rows * D * 2, transcendentals=0
         ),
         compiler_params=pltpu.CompilerParams(vmem_limit_bytes=50 << 20),
         name="regenerate",
-    )(seeds)
+    )(seeds.reshape(pairs, 1))
 
 
 def logits_kernel(
@@ -276,35 +261,45 @@
     )(firsts, rows, own_head, other_head)
 
 
-def update_kernel(gap_ref, noise_ref, out_ref):
+def update_kernel(gap_ref, noise_ref, out_ref, *, pairs):
     rows = out_ref.shape[0]
-    pairs = noise_ref.shape[1]
+    gap = gap_ref[...]
+    high = gap.astype(jnp.bfloat16).astype(jnp.float32)
+    middle = (gap - high).astype(jnp.bfloat16).astype(jnp.float32)
+    low = gap - high - middle
+    at = (16, 16 * pairs)
+    own = lax.broadcasted_iota(jnp.int32, at, 0) * pairs
+    lane = lax.broadcasted_iota(jnp.int32, at, 1)
+    mine = (lane >= own) & (lane < own + pairs)
+    left = jnp.concatenate([jnp.where(mine, jnp.broadcast_to(part, at), 0.0) for part in (high, middle, low)], axis=0)
+    left = left.astype(jnp.bfloat16)
     for r in range(0, rows, 16):
         deep = min(16, rows - r)
-        total = None
-        for p in range(pairs):
-            term = gap_ref[p] * noise_ref[0, p, r : r + 16, :].astype(jnp.float32)
-            total = term if total is None else total + term
+        parts = jnp.dot(
+            left[:, : deep * pairs],
+            noise_ref[0, r * pairs : (r + deep) * pairs, :],
+            preferred_element_type=jnp.float32,
+        )
+        total = parts[:16] + parts[16:32] + parts[32:]
         out_ref[r : r + deep, :] = total[:deep]
 
 
 def update(gap, noise, rows):
-    slabs, pairs, padded, width = noise.shape
+    slabs, depth, width = noise.shape
+    pairs = gap.shape[0]
     return pl.pallas_call(
-        update_kernel,
+        functools.partial(update_kernel, pairs=pairs),
         grid=(slabs,),
         in_specs=[
-            pl.BlockSpec(memory_space=pltpu.SMEM),
-            pl.BlockSpec((1, pairs, padded, width), lambda c: (c, 0, 0, 0)),
+            pl.BlockSpec((1, 16 * pairs), lambda c: (0, 0)),
+            pl.BlockSpec((1, depth, width), lambda c: (c, 0, 0)),
         ],
         out_specs=pl.BlockSpec((rows, width), lambda c: (0, c)),
         out_shape=jax.ShapeDtypeStruct((rows, slabs * width), jnp.float32),
-        cost_estimate=pl.CostEstimate(
-            flops=2 * pairs * rows * D, bytes_accessed=2 * pairs * padded * D, transcendentals=0
-        ),
+        cost_estimate=pl.CostEstimate(flops=2 * depth * D, bytes_accessed=2 * depth * D, transcendentals=0),
         compiler_params=pltpu.CompilerParams(vmem_limit_bytes=44 << 20),
         name="update",
-    )(gap, noise)
+    )(jnp.tile(gap, 16).reshape(1, 16 * pairs), noise)
 
 
 def scattered_sum(partial, axes):

time: 229 us -> 228 us (level)
    pallas_call x1, Pallas kernels: 14 us -> 9.25 us  [products(): pl.pallas_call(functools.partial(first_kernel, steps=first_steps), grid=(...]
    pallas_call x1, Pallas kernels: 19.4 us -> 23 us  [products(): pl.pallas_call(functools.partial(rest_kernel, first_step=first_steps), gr...]
  transfers between devices with their start and end apart: 7 -> 7, of which waited for: 6 -> 5; matrix products, arithmetic and copies ran while one was open for 1% -> 1% of each run, Pallas kernels for 21% -> 22%
where the time goes in v5:
time: 228 us; the launch traced here: 227 us
  Pallas kernels  96 us (42%)
  waiting for transfers between devices  78.7 us (35%)
  starting transfers between devices  30.7 us (13%)
  between operations  14.3 us (6%)
  local copies, waits for them, and re-layouts  4.5 us (2%)
  other arithmetic  3.21 us (1%)
    all_gather x1, waiting for transfers between devices, local(): lax.all_gather(normed.reshape(2 * share, D + EXTRA), SAME_CORE, axis=0, t...  55.1 us
    pallas_call x1, Pallas kernels, regenerate(): pl.pallas_call(functools.partial(regenerate_kernel, out_rows=rows), grid=...  28.1 us
    pallas_call x1, Pallas kernels, vocabulary_stats(): pl.pallas_call(logits_kernel, in_specs=[pl.BlockSpec(memory_space=pltpu.S...  25.3 us
    pallas_call x1, Pallas kernels, products(): pl.pallas_call(functools.partial(rest_kernel, first_step=first_steps), gr...  23 us
    all_to_all x2, starting transfers between devices, scattered_sum(): pieces = lax.all_to_all(partial, axes, 0, 0)  15.2 us
    all_to_all x2, waiting for transfers between devices, joined(): everyone = lax.all_to_all(stats, axes, 0, 0)  11.9 us
    all_to_all x2, waiting for transfers between devices, scattered_sum(): pieces = lax.all_to_all(partial, axes, 0, 0)  10.8 us
    pallas_call x1, Pallas kernels, update(): pl.pallas_call(functools.partial(update_kernel, pairs=pairs), grid=(slabs...  10.3 us
  transfers between devices with their start and end apart: 7, of which 5 were waited for; matrix products, arithmetic and copies ran while one was open for 1% of the time, Pallas kernels for 22%

profile of v5, /device:TPU:1, one launch (start us, length us, event | category | flops | bytes accessed | tf_op | source)
XLA Modules:
  0.0 227.3 jit_solution(4611613509176876416)
XLA Ops:
  7.2 1.4 copy.25
  8.6 0.6 copy-done.2
  9.2 9.3 %base_and_probe.1 = (bf16[8,24,1792]{2,1,0:T(8,128)(2,1)}, f32[8,24,1792]{2,1,0:T(8,128)}) custom-call(s32[16]{0:T(128)S(1)} %copy-done.2, bf16[128,2368]{1,0:T(8,128)(2,1)S(1)} %bitcast.24, bf16[2368,3584]{1,0:T(8,128)(2,1)} %weight_hbm.1), custom_call_target="tpu_custom_call" | custom-call | flops 2424832000 | bytes 1212416 | tf_op jit(solution)/shard_map/base_and_probe/pallas_call | solution.py:106
  18.5 8.5 %all-to-all-start = ((f32[8,24,1792]{2,1,0:T(8,128)}), f32[8,24,1792]{2,1,0:T(8,128)S(1)}, u32[]{:S(2)}, u32[]{:S(2)}) async-start(f32[8,24,1792]{2,1,0:T(8,128)} %get-tuple-element.11), calls=%async_computation | async-start | bytes 2752512 | tf_op jit(solution)/shard_map/all_to_all | solution.py:306
  27.3 23.0 %probe.1 = bf16[8,24,1792]{2,1,0:T(8,128)(2,1)} custom-call(s32[16]{0:T(128)S(1)} %copy-done.3, bf16[128,2368]{1,0:T(8,128)(2,1)S(1)} %bitcast.25, bf16[8,24,1792]{2,1,0:T(8,128)(2,1)} %get-tuple-element.10._), custom_call_target="tpu_custom_call", output_to_operand_aliasing={{}: (2, {})} | custom-call | flops 14548992000 | bytes 7274496 | tf_op jit(solution)/shard_map/probe/pallas_call | solution.py:120
  50.5 6.7 %all-to-all-start.1 = ((bf16[8,24,1792]{2,1,0:T(8,128)(2,1)}), bf16[8,24,1792]{2,1,0:T(8,128)(2,1)S(1)}, u32[]{:S(2)}, u32[]{:S(2)}) async-start(bf16[8,24,1792]{2,1,0:T(8,128)(2,1)} %probe.1), calls=%async_computation.1 | async-start | bytes 1376256 | tf_op jit(solution)/shard_map/all_to_all | solution.py:306
  57.2 1.0 convert_add_fusion
  58.1 10.8 %all-to-all-done.1 = bf16[8,24,1792]{2,1,0:T(8,128)(2,1)S(1)} async-done(((bf16[8,24,1792]{2,1,0:T(8,128)(2,1)}), bf16[8,24,1792]{2,1,0:T(8,128)(2,1)S(1)}, u32[]{:S(2)}, u32[]{:S(2)}) %all-to-all-start.1) | async-done | bytes 688160 | tf_op jit(solution)/shard_map/all_to_all | solution.py:306
  69.0 0.1 convert_reduce_fusion
  69.1 0.2 multiply_reduce_fusion
  69.4 0.1 multiply_convert_fusion
  69.6 0.7 reshape.183
  70.3 2.5 %collective-permute-start = (bf16[3584,768]{1,0:T(8,128)(2,1)}, bf16[3584,768]{1,0:T(8,128)(2,1)}, u32[]{:S(2)}, u32[]{:S(2)}) collective-permute-start(bf16[3584,768]{1,0:T(8,128)(2,1)} %own_hbm.1), channel_id=1, source_target_pairs={{0,8},{8,0},{1,9},{9,1},{2,10},{10,2},{3,11},{11,3},{4,12},{12,4},... | collective-permute-start | bytes 16515080 | tf_op jit(solution)/shard_map/ppermute | solution.py:333
  72.9 0.2 dynamic-slice_reduce_fusion
  73.1 0.6 pad_add_fusion.first_ref
  73.8 28.1 %regenerate.1.noise_ref = bf16[7,2368,512]{2,1,0:T(8,128)(2,1)} custom-call(s32[16,1]{1,0:T(8,128)S(1)} %copy.26.seeds_ref), custom_call_target="tpu_custom_call" | custom-call | flops 16973824000 | bytes 16973824 | tf_op jit(solution)/shard_map/regenerate/pallas_call | solution.py:147
  101.9 55.1 %all-gather.2.cloned.1.call-done.rows_hbm = bf16[1536,3712]{1,0:T(8,128)(2,1)} async-done(((bf16[24,3712]{1,0:T(8,128)(2,1)}), bf16[1536,3712]{1,0:T(8,128)(2,1)}) %all-gather.2.cloned.1.call-update) | async-done | bytes 11403280 | tf_op jit(solution)/shard_map/all_gather | solution.py:354
  157.0 25.3 %vocabulary_stats.1 = f32[8,2,1536]{2,1,0:T(2,128)} custom-call(s32[2]{0:T(128)} %pad_add_fusion.first_ref, bf16[1536,3712]{1,0:T(8,128)(2,1)} %all-gather.2.cloned.1.call-done.rows_hbm, bf16[3584,768]{1,0:T(8,128)(2,1)} %own_hbm.1, bf16[3584,768]{1,0:T(8,128)(2,1)} %collective-permute-done.other_hbm), custom_call_target="tpu_custom_call" | custom-call | flops 16911433728 | bytes 11010048 | tf_op jit(solution)/shard_map/vocabulary_stats/pallas_call | solution.py:237
  182.3 6.3 %all-to-all-start.2 = ((f32[8,2,1536]{2,1,0:T(2,128)}), f32[8,2,1536]{2,1,0:T(2,128)S(1)}, u32[]{:S(2)}, u32[]{:S(2)}) async-start(f32[8,2,1536]{2,1,0:T(2,128)} %vocabulary_stats.1), calls=%async_computation.2 | async-start | bytes 196608 | tf_op jit(solution)/shard_map/all_to_all | solution.py:313
  188.7 6.9 %all-to-all-done.2 = f32[8,2,1536]{2,1,0:T(2,128)S(1)} async-done(((f32[8,2,1536]{2,1,0:T(2,128)}), f32[8,2,1536]{2,1,0:T(2,128)S(1)}, u32[]{:S(2)}, u32[]{:S(2)}) %all-to-all-start.2) | async-done | bytes 98336 | tf_op jit(solution)/shard_map/all_to_all | solution.py:313
  195.6 0.1 slice_reduce_fusion.3
  195.8 0.7 broadcast_in_dim.19
  196.5 3.4 %all-to-all-start.3 = ((f32[8,2,1536]{2,1,0:T(2,128)}), f32[8,2,1536]{2,1,0:T(2,128)S(1)}, u32[]{:S(2)}, u32[]{:S(2)}) async-start(f32[8,2,1536]{2,1,0:T(2,128)} %broadcast_in_dim.19), calls=%async_computation.3 | async-start | bytes 196608 | tf_op jit(solution)/shard_map/all_to_all | solution.py:313
  199.9 0.2 convert_reduce_fusion.1
  200.1 5.0 %all-to-all-done.3 = f32[8,2,1536]{2,1,0:T(2,128)S(1)} async-done(((f32[8,2,1536]{2,1,0:T(2,128)}), f32[8,2,1536]{2,1,0:T(2,128)S(1)}, u32[]{:S(2)}, u32[]{:S(2)}) %all-to-all-start.3) | async-done | bytes 98336 | tf_op jit(solution)/shard_map/all_to_all | solution.py:313
  205.0 0.1 slice_reduce_fusion.2
  205.2 0.1 sub.46
  205.4 0.1 multiply_reduce_fusion.1
  205.6 3.2 %collective-permute-start.1 = (f32[8,2]{0,1:T(2,128)S(1)}, f32[8,2]{0,1:T(2,128)S(1)}, u32[]{:S(2)}, u32[]{:S(2)}) collective-permute-start(f32[8,2]{0,1:T(2,128)S(1)} %broadcast_divide_fusion), channel_id=1, source_target_pairs={{0,8},{8,0},{1,9},{9,1},{2,10},{10,2},{3,11},{11,3},{4,12},{12,4},... | collective-permute-start | bytes 200 | tf_op jit(solution)/shard_map/ppermute | solution.py:367
  208.8 0.8 collective-permute-done.1
  210.0 0.1 reduce_sum.92
  210.2 10.3 %update.1 = f32[148,3584]{1,0:T(8,128)} custom-call(f32[1,256]{1,0:T(1,128)S(1)} %reshape_tile.3.gap_ref, bf16[7,2368,512]{2,1,0:T(8,128)(2,1)} %regenerate.1.noise_ref), custom_call_target="tpu_custom_call" | custom-call | flops 16973824 | bytes 16973824 | tf_op jit(solution)/shard_map/update/pallas_call | solution.py:290
  (53 shorter events, 1.3 us)
Async XLA Ops:
  7.2 19.9 %copy-start = (s32[1,128]{1,0:T(1,128)S(1)}, s32[1,128]{1,0:T(1,128)}, u32[]{:S(2)}) copy-start(s32[1,128]{1,0:T(1,128)} %param.14) | copy-start | bytes 1540
  8.6 0.7 copy-start.2
  9.2 17.8 %copy-start.7 = (s32[32]{0:T(128)S(1)}, s32[32]{0:T(128)}, u32[]{:S(2)}) copy-start(s32[32]{0:T(128)} %param.17) | copy-start | bytes 388
  9.2 18.1 %copy-start.3 = (s32[16]{0:T(128)S(1)}, s32[16]{0:T(128)}, u32[]{:S(2)}) copy-start(s32[16]{0:T(128)} %seeds_ref.3) | copy-start | bytes 196
  18.5 31.8 %all-to-all-start = ((f32[8,24,1792]{2,1,0:T(8,128)}), f32[8,24,1792]{2,1,0:T(8,128)S(1)}, u32[]{:S(2)}, u32[]{:S(2)}) async-start(f32[8,24,1792]{2,1,0:T(8,128)} %get-tuple-element.11), calls=%async_computation | async-start | bytes 2752512 | tf_op jit(solution)/shard_map/all_to_all | solution.py:306
  50.3 19.0 %copy-start.4 = (f32[3584]{0:T(1024)S(1)}, f32[3584]{0:T(1024)}, u32[]{:S(2)}) copy-start(f32[3584]{0:T(1024)} %param.12) | copy-start | bytes 43012
  50.3 22.5 %copy-start.5 = (s32[16]{0:T(128)S(1)}, s32[16]{0:T(128)}, u32[]{:S(2)}) copy-start(s32[16]{0:T(128)} %param.15) | copy-start | bytes 196
  50.5 18.5 %all-to-all-start.1 = ((bf16[8,24,1792]{2,1,0:T(8,128)(2,1)}), bf16[8,24,1792]{2,1,0:T(8,128)(2,1)S(1)}, u32[]{:S(2)}, u32[]{:S(2)}) async-start(bf16[8,24,1792]{2,1,0:T(8,128)(2,1)} %probe.1), calls=%async_computation.1 | async-start | bytes 1376256 | tf_op jit(solution)/shard_map/all_to_all | solution.py:306
  57.1 99.9 %all-gather.2.cloned.1.call-start = ((), (), s32[]{:S(2)}) async-start(), calls=%async_computation.4 | async-start | bytes 11581440 | tf_op jit(solution)/shard_map/all_gather | solution.py:354
  70.3 31.6 %collective-permute-start = (bf16[3584,768]{1,0:T(8,128)(2,1)}, bf16[3584,768]{1,0:T(8,128)(2,1)}, u32[]{:S(2)}, u32[]{:S(2)}) collective-permute-start(bf16[3584,768]{1,0:T(8,128)(2,1)} %own_hbm.1), channel_id=1, source_target_pairs={{0,8},{8,0},{1,9},{9,1},{2,10},{10,2},{3,11},{11,3},{4,12},{12,4},... | collective-permute-start | bytes 16515080 | tf_op jit(solution)/shard_map/ppermute | solution.py:333
  182.3 13.2 %all-to-all-start.2 = ((f32[8,2,1536]{2,1,0:T(2,128)}), f32[8,2,1536]{2,1,0:T(2,128)S(1)}, u32[]{:S(2)}, u32[]{:S(2)}) async-start(f32[8,2,1536]{2,1,0:T(2,128)} %vocabulary_stats.1), calls=%async_computation.2 | async-start | bytes 196608 | tf_op jit(solution)/shard_map/all_to_all | solution.py:313
  196.5 8.6 %all-to-all-start.3 = ((f32[8,2,1536]{2,1,0:T(2,128)}), f32[8,2,1536]{2,1,0:T(2,128)S(1)}, u32[]{:S(2)}, u32[]{:S(2)}) async-start(f32[8,2,1536]{2,1,0:T(2,128)} %broadcast_in_dim.19), calls=%async_computation.3 | async-start | bytes 196608 | tf_op jit(solution)/shard_map/all_to_all | solution.py:313
  205.6 4.1 %collective-permute-start.1 = (f32[8,2]{0,1:T(2,128)S(1)}, f32[8,2]{0,1:T(2,128)S(1)}, u32[]{:S(2)}, u32[]{:S(2)}) collective-permute-start(f32[8,2]{0,1:T(2,128)S(1)} %broadcast_divide_fusion), channel_id=1, source_target_pairs={{0,8},{8,0},{1,9},{9,1},{2,10},{10,2},{3,11},{11,3},{4,12},{12,4},... | collective-permute-start | bytes 200 | tf_op jit(solution)/shard_map/ppermute | solution.py:367
  209.8 10.6 %copy-start.6 = (f32[32]{0:T(128)}, f32[32]{0:T(128)S(1)}, u32[]{:S(2)}) copy-start(f32[32]{0:T(128)S(1)} %select_n.37) | copy-start | bytes 388
  210.1 10.4 %copy-start.1 = (s32[1,128]{1,0:T(1,128)S(1)}, s32[1,128]{1,0:T(1,128)}, u32[]{:S(2)}) copy-start(s32[1,128]{1,0:T(1,128)} %param.14) | copy-start | bytes 1540
Sparse Core Ops, SparseCore 0:
  70.4 86.5 all-gather.1

commit v6 on v5

--- a/solution.py
+++ b/solution.py
@@ -159,11 +159,11 @@
 
 
 def logits_kernel(
-    first_ref, rows_hbm, own_hbm, other_hbm, out_ref, rows_ref, own_ref, other_ref, held_ref, stats_ref, sems, head_sems
+    first_ref, rows_hbm, own_hbm, other_hbm, out_ref, rows_ref, heads_ref, held_ref, stats_ref, sems, head_sems
 ):
     slots, chunk, _ = rows_ref.shape
     chunks = rows_hbm.shape[0] // chunk
-    vocab = own_ref.shape[1]
+    vocab = own_hbm.shape[1]
     lanes = lax.broadcasted_iota(jnp.int32, (1, 128), 1).astype(jnp.float32)
 
     def fetch(i):
@@ -171,27 +171,23 @@
             rows_hbm.at[pl.ds(i * chunk, chunk), :], rows_ref.at[i % slots], sems.at[i % slots]
         )
 
-    early = vocab // 3
-    heads = [
-        pltpu.make_async_copy(own_hbm.at[:, :early], own_ref.at[:, :early], head_sems.at[0]),
-        pltpu.make_async_copy(own_hbm.at[:, early:], own_ref.at[:, early:], head_sems.at[1]),
-        pltpu.make_async_copy(other_hbm, other_ref, head_sems.at[2]),
-    ]
+    third = vocab // 3
+    pieces = []
+    for hbm, at, cuts in ((own_hbm, 0, (0, 2 * third, vocab)), (other_hbm, vocab, (0, third, vocab))):
+        for first, last in zip(cuts[:-1], cuts[1:]):
+            to = heads_ref.at[:, at + first : at + last]
+            pieces.append(pltpu.make_async_copy(hbm.at[:, first:last], to, head_sems.at[len(pieces)]))
 
     def multiply(i):
         rows = rows_ref[i % slots, :, :D]
         if i == 0:
-            for copy, ref, cols, at in (
-                (heads[0], own_ref, slice(0, early), 0),
-                (heads[1], own_ref, slice(early, vocab), early),
-                (heads[2], other_ref, slice(0, vocab), vocab),
-            ):
-                copy.wait()
-                made = jnp.dot(rows, ref[:, cols], preferred_element_type=jnp.float32)
-                held_ref[0, :, at : at + made.shape[1]] = made
+            for part, waits in enumerate((pieces[:1], pieces[1:3], pieces[3:])):
+                for piece in waits:
+                    piece.wait()
+                cols = slice(2 * part * third, 2 * (part + 1) * third)
+                held_ref[0, :, cols] = jnp.dot(rows, heads_ref[:, cols], preferred_element_type=jnp.float32)
         else:
-            held_ref[i % 2, :, :vocab] = jnp.dot(rows, own_ref[...], preferred_element_type=jnp.float32)
-            held_ref[i % 2, :, vocab:] = jnp.dot(rows, other_ref[...], preferred_element_type=jnp.float32)
+            held_ref[i % 2] = jnp.dot(rows, heads_ref[...], preferred_element_type=jnp.float32)
 
     def absorb(i):
         slot = i % 2
@@ -214,8 +210,8 @@
         stats_ref[i * chunk : (i + 1) * chunk, :] = jnp.where(lane == 0, high + jnp.log(total), hit)
 
     fetch(0).start()
-    for copy in heads:
-        copy.start()
+    for piece in pieces:
+        piece.start()
     for i in range(1, min(slots - 1, chunks)):
         fetch(i).start()
     for i in range(chunks):
@@ -246,12 +242,11 @@
         out_shape=jax.ShapeDtypeStruct((copies, 2, count), jnp.float32),
         scratch_shapes=[
             pltpu.VMEM((slots, chunk, D + EXTRA), jnp.bfloat16),
-            pltpu.VMEM((D, vocab), jnp.bfloat16),
-            pltpu.VMEM((D, vocab), jnp.bfloat16),
+            pltpu.VMEM((D, 2 * vocab), jnp.bfloat16),
             pltpu.VMEM((2, chunk, 2 * vocab), jnp.float32),
             pltpu.VMEM((count, 128), jnp.float32),
             pltpu.SemaphoreType.DMA((slots,)),
-            pltpu.SemaphoreType.DMA((3,)),
+            pltpu.SemaphoreType.DMA((4,)),
         ],
         cost_estimate=pl.CostEstimate(
             flops=2 * count * D * 2 * vocab, bytes_accessed=count * D * 2, transcendentals=0
@@ -261,8 +256,16 @@
     )(firsts, rows, own_head, other_head)
 
 
-def update_kernel(gap_ref, noise_ref, out_ref, *, pairs):
-    rows = out_ref.shape[0]
+def update_kernel(gap_ref, noise_hbm, out_hbm, noise_ref, out_ref, in_sems, out_sems, *, pairs):
+    slabs, _, width = noise_ref.shape
+    rows = out_ref.shape[1]
+    reads = [pltpu.make_async_copy(noise_hbm.at[c], noise_ref.at[c], in_sems.at[c]) for c in range(slabs)]
+    writes = [
+        pltpu.make_async_copy(out_ref.at[c], out_hbm.at[:, c * width : (c + 1) * width], out_sems.at[c])
+        for c in range(slabs)
+    ]
+    for read in reads:
+        read.start()
     gap = gap_ref[...]
     high = gap.astype(jnp.bfloat16).astype(jnp.float32)
     middle = (gap - high).astype(jnp.bfloat16).astype(jnp.float32)
@@ -273,15 +276,20 @@
     mine = (lane >= own) & (lane < own + pairs)
     left = jnp.concatenate([jnp.where(mine, jnp.broadcast_to(part, at), 0.0) for part in (high, middle, low)], axis=0)
     left = left.astype(jnp.bfloat16)
-    for r in range(0, rows, 16):
-        deep = min(16, rows - r)
-        parts = jnp.dot(
-            left[:, : deep * pairs],
-            noise_ref[0, r * pairs : (r + deep) * pairs, :],
-            preferred_element_type=jnp.float32,
-        )
-        total = parts[:16] + parts[16:32] + parts[32:]
-        out_ref[r : r + deep, :] = total[:deep]
+    for c in range(slabs):
+        reads[c].wait()
+        for r in range(0, rows, 16):
+            deep = min(16, rows - r)
+            parts = jnp.dot(
+                left[:, : deep * pairs],
+                noise_ref[c, r * pairs : (r + deep) * pairs, :],
+                preferred_element_type=jnp.float32,
+            )
+            total = parts[:16] + parts[16:32] + parts[32:]
+            out_ref[c, r : r + deep, :] = total[:deep]
+        writes[c].start()
+    for write in writes:
+        write.wait()
 
 
 def update(gap, noise, rows):
@@ -289,15 +297,17 @@
     pairs = gap.shape[0]
     return pl.pallas_call(
         functools.partial(update_kernel, pairs=pairs),
-        grid=(slabs,),
-        in_specs=[
-            pl.BlockSpec((1, 16 * pairs), lambda c: (0, 0)),
-            pl.BlockSpec((1, depth, width), lambda c: (c, 0, 0)),
+        in_specs=[pl.BlockSpec(memory_space=pltpu.VMEM), pl.BlockSpec(memory_space=pl.ANY)],
+        out_specs=pl.BlockSpec(memory_space=pl.ANY),
+        out_shape=jax.ShapeDtypeStruct((rows, slabs * width), jnp.float32),
+        scratch_shapes=[
+            pltpu.VMEM((slabs, depth, width), jnp.bfloat16),
+            pltpu.VMEM((slabs, rows, width), jnp.float32),
+            pltpu.SemaphoreType.DMA((slabs,)),
+            pltpu.SemaphoreType.DMA((slabs,)),
         ],
-        out_specs=pl.BlockSpec((rows, width), lambda c: (0, c)),
-        out_shape=jax.ShapeDtypeStruct((rows, slabs * width), jnp.float32),
         cost_estimate=pl.CostEstimate(flops=2 * depth * D, bytes_accessed=2 * depth * D, transcendentals=0),
-        compiler_params=pltpu.CompilerParams(vmem_limit_bytes=44 << 20),
+        compiler_params=pltpu.CompilerParams(vmem_limit_bytes=50 << 20),
         name="update",
     )(jnp.tile(gap, 16).reshape(1, 16 * pairs), noise)
 

time: 228 us -> 224 us (0.982)
  Pallas kernels: 96 us -> 92.5 us
    pallas_call x1, Pallas kernels: 10.3 us -> 7.72 us  [update(): pl.pallas_call(functools.partial(update_kernel, pairs=pairs), in_specs=[p...]
  transfers between devices with their start and end apart: 7 -> 7, of which waited for: 5 -> 5; matrix products, arithmetic and copies ran while one was open for 1% -> 1% of each run, Pallas kernels for 22% -> 23%
where the time goes in v6:
time: 224 us
  Pallas kernels  92.5 us (41%)
  waiting for transfers between devices  78.7 us (35%)
  starting transfers between devices  30.7 us (14%)
  between operations  14.3 us (6%)
  local copies, waits for them, and re-layouts  4.5 us (2%)
  other arithmetic  3.21 us (1%)
    all_gather x1, waiting for transfers between devices, local(): lax.all_gather(normed.reshape(2 * share, D + EXTRA), SAME_CORE, axis=0, t...  55.1 us
    pallas_call x1, Pallas kernels, regenerate(): pl.pallas_call(functools.partial(regenerate_kernel, out_rows=rows), grid=...  28.1 us
    pallas_call x1, Pallas kernels, vocabulary_stats(): pl.pallas_call(logits_kernel, in_specs=[pl.BlockSpec(memory_space=pltpu.S...  24.4 us
    pallas_call x1, Pallas kernels, products(): pl.pallas_call(functools.partial(rest_kernel, first_step=first_steps), gr...  23 us
    all_to_all x2, starting transfers between devices, scattered_sum(): pieces = lax.all_to_all(partial, axes, 0, 0)  15.2 us
    all_to_all x2, waiting for transfers between devices, joined(): everyone = lax.all_to_all(stats, axes, 0, 0)  11.9 us
    all_to_all x2, waiting for transfers between devices, scattered_sum(): pieces = lax.all_to_all(partial, axes, 0, 0)  10.8 us
    all_to_all x2, starting transfers between devices, joined(): everyone = lax.all_to_all(stats, axes, 0, 0)  9.7 us
  transfers between devices with their start and end apart: 7, of which 5 were waited for; matrix products, arithmetic and copies ran while one was open for 1% of the time, Pallas kernels for 23%

profile of v6, /device:TPU:1, one launch (start us, length us, event | category | flops | bytes accessed | tf_op | source)
XLA Modules:
  0.0 223.9 jit_solution(4422642341986251100)
XLA Ops:
  7.2 1.4 copy.25
  8.6 0.6 copy-done.2
  9.2 9.3 %base_and_probe.1 = (bf16[8,24,1792]{2,1,0:T(8,128)(2,1)}, f32[8,24,1792]{2,1,0:T(8,128)}) custom-call(s32[16]{0:T(128)S(1)} %copy-done.2, bf16[128,2368]{1,0:T(8,128)(2,1)S(1)} %bitcast.24, bf16[2368,3584]{1,0:T(8,128)(2,1)} %weight_hbm.1), custom_call_target="tpu_custom_call" | custom-call | flops 2424832000 | bytes 1212416 | tf_op jit(solution)/shard_map/base_and_probe/pallas_call | solution.py:106
  18.5 8.5 %all-to-all-start = ((f32[8,24,1792]{2,1,0:T(8,128)}), f32[8,24,1792]{2,1,0:T(8,128)S(1)}, u32[]{:S(2)}, u32[]{:S(2)}) async-start(f32[8,24,1792]{2,1,0:T(8,128)} %get-tuple-element.11), calls=%async_computation | async-start | bytes 2752512 | tf_op jit(solution)/shard_map/all_to_all | solution.py:316
  27.3 23.0 %probe.1 = bf16[8,24,1792]{2,1,0:T(8,128)(2,1)} custom-call(s32[16]{0:T(128)S(1)} %copy-done.3, bf16[128,2368]{1,0:T(8,128)(2,1)S(1)} %bitcast.25, bf16[8,24,1792]{2,1,0:T(8,128)(2,1)} %get-tuple-element.10._), custom_call_target="tpu_custom_call", output_to_operand_aliasing={{}: (2, {})} | custom-call | flops 14548992000 | bytes 7274496 | tf_op jit(solution)/shard_map/probe/pallas_call | solution.py:120
  50.5 6.7 %all-to-all-start.1 = ((bf16[8,24,1792]{2,1,0:T(8,128)(2,1)}), bf16[8,24,1792]{2,1,0:T(8,128)(2,1)S(1)}, u32[]{:S(2)}, u32[]{:S(2)}) async-start(bf16[8,24,1792]{2,1,0:T(8,128)(2,1)} %probe.1), calls=%async_computation.1 | async-start | bytes 1376256 | tf_op jit(solution)/shard_map/all_to_all | solution.py:316
  57.2 1.0 convert_add_fusion
  58.1 10.8 %all-to-all-done.1 = bf16[8,24,1792]{2,1,0:T(8,128)(2,1)S(1)} async-done(((bf16[8,24,1792]{2,1,0:T(8,128)(2,1)}), bf16[8,24,1792]{2,1,0:T(8,128)(2,1)S(1)}, u32[]{:S(2)}, u32[]{:S(2)}) %all-to-all-start.1) | async-done | bytes 688160 | tf_op jit(solution)/shard_map/all_to_all | solution.py:316
  69.0 0.1 convert_reduce_fusion
  69.1 0.2 multiply_reduce_fusion
  69.4 0.1 multiply_convert_fusion
  69.6 0.7 reshape.183
  70.3 2.5 %collective-permute-start = (bf16[3584,768]{1,0:T(8,128)(2,1)}, bf16[3584,768]{1,0:T(8,128)(2,1)}, u32[]{:S(2)}, u32[]{:S(2)}) collective-permute-start(bf16[3584,768]{1,0:T(8,128)(2,1)} %own_hbm.1), channel_id=1, source_target_pairs={{0,8},{8,0},{1,9},{9,1},{2,10},{10,2},{3,11},{11,3},{4,12},{12,4},... | collective-permute-start | bytes 16515080 | tf_op jit(solution)/shard_map/ppermute | solution.py:343
  72.9 0.2 dynamic-slice_reduce_fusion
  73.1 0.6 pad_add_fusion.first_ref
  73.8 28.1 %regenerate.1.noise_hbm = bf16[7,2368,512]{2,1,0:T(8,128)(2,1)} custom-call(s32[16,1]{1,0:T(8,128)S(1)} %copy.26.seeds_ref), custom_call_target="tpu_custom_call" | custom-call | flops 16973824000 | bytes 16973824 | tf_op jit(solution)/shard_map/regenerate/pallas_call | solution.py:147
  101.9 55.1 %all-gather.2.cloned.1.call-done.rows_hbm = bf16[1536,3712]{1,0:T(8,128)(2,1)} async-done(((bf16[24,3712]{1,0:T(8,128)(2,1)}), bf16[1536,3712]{1,0:T(8,128)(2,1)}) %all-gather.2.cloned.1.call-update) | async-done | bytes 11403280 | tf_op jit(solution)/shard_map/all_gather | solution.py:364
  157.0 24.4 %vocabulary_stats.1 = f32[8,2,1536]{2,1,0:T(2,128)} custom-call(s32[2]{0:T(128)} %pad_add_fusion.first_ref, bf16[1536,3712]{1,0:T(8,128)(2,1)} %all-gather.2.cloned.1.call-done.rows_hbm, bf16[3584,768]{1,0:T(8,128)(2,1)} %own_hbm.1, bf16[3584,768]{1,0:T(8,128)(2,1)} %collective-permute-done.other_hbm), custom_call_target="tpu_custom_call" | custom-call | flops 16911433728 | bytes 11010048 | tf_op jit(solution)/shard_map/vocabulary_stats/pallas_call | solution.py:233
  181.4 6.3 %all-to-all-start.2 = ((f32[8,2,1536]{2,1,0:T(2,128)}), f32[8,2,1536]{2,1,0:T(2,128)S(1)}, u32[]{:S(2)}, u32[]{:S(2)}) async-start(f32[8,2,1536]{2,1,0:T(2,128)} %vocabulary_stats.1), calls=%async_computation.2 | async-start | bytes 196608 | tf_op jit(solution)/shard_map/all_to_all | solution.py:323
  187.8 6.9 %all-to-all-done.2 = f32[8,2,1536]{2,1,0:T(2,128)S(1)} async-done(((f32[8,2,1536]{2,1,0:T(2,128)}), f32[8,2,1536]{2,1,0:T(2,128)S(1)}, u32[]{:S(2)}, u32[]{:S(2)}) %all-to-all-start.2) | async-done | bytes 98336 | tf_op jit(solution)/shard_map/all_to_all | solution.py:323
  194.6 0.1 slice_reduce_fusion.3
  194.9 0.7 broadcast_in_dim.19
  195.5 3.4 %all-to-all-start.3 = ((f32[8,2,1536]{2,1,0:T(2,128)}), f32[8,2,1536]{2,1,0:T(2,128)S(1)}, u32[]{:S(2)}, u32[]{:S(2)}) async-start(f32[8,2,1536]{2,1,0:T(2,128)} %broadcast_in_dim.19), calls=%async_computation.3 | async-start | bytes 196608 | tf_op jit(solution)/shard_map/all_to_all | solution.py:323
  199.0 0.2 convert_reduce_fusion.1
  199.2 5.0 %all-to-all-done.3 = f32[8,2,1536]{2,1,0:T(2,128)S(1)} async-done(((f32[8,2,1536]{2,1,0:T(2,128)}), f32[8,2,1536]{2,1,0:T(2,128)S(1)}, u32[]{:S(2)}, u32[]{:S(2)}) %all-to-all-start.3) | async-done | bytes 98336 | tf_op jit(solution)/shard_map/all_to_all | solution.py:323
  204.1 0.1 slice_reduce_fusion.2
  204.3 0.1 sub.46
  204.4 0.1 multiply_reduce_fusion.1
  204.7 3.2 %collective-permute-start.1 = (f32[8,2]{0,1:T(2,128)S(1)}, f32[8,2]{0,1:T(2,128)S(1)}, u32[]{:S(2)}, u32[]{:S(2)}) collective-permute-start(f32[8,2]{0,1:T(2,128)S(1)} %broadcast_divide_fusion), channel_id=1, source_target_pairs={{0,8},{8,0},{1,9},{9,1},{2,10},{10,2},{3,11},{11,3},{4,12},{12,4},... | collective-permute-start | bytes 200 | tf_op jit(solution)/shard_map/ppermute | solution.py:377
  207.9 0.8 collective-permute-done.1
  209.0 0.1 reduce_sum.92
  209.3 7.7 %update.1 = f32[148,3584]{1,0:T(8,128)} custom-call(f32[1,256]{1,0:T(1,128)S(1)} %reshape_tile.3.gap_ref, bf16[7,2368,512]{2,1,0:T(8,128)(2,1)} %regenerate.1.noise_hbm), custom_call_target="tpu_custom_call" | custom-call | flops 16973824 | bytes 16973824 | tf_op jit(solution)/shard_map/update/pallas_call | solution.py:298
  (53 shorter events, 1.3 us)
Async XLA Ops:
  7.2 19.9 %copy-start = (s32[1,128]{1,0:T(1,128)S(1)}, s32[1,128]{1,0:T(1,128)}, u32[]{:S(2)}) copy-start(s32[1,128]{1,0:T(1,128)} %param.14) | copy-start | bytes 1540
  8.6 0.7 copy-start.2
  9.2 17.8 %copy-start.7 = (s32[32]{0:T(128)S(1)}, s32[32]{0:T(128)}, u32[]{:S(2)}) copy-start(s32[32]{0:T(128)} %param.17) | copy-start | bytes 388
  9.2 18.1 %copy-start.3 = (s32[16]{0:T(128)S(1)}, s32[16]{0:T(128)}, u32[]{:S(2)}) copy-start(s32[16]{0:T(128)} %seeds_ref.3) | copy-start | bytes 196
  18.5 31.8 %all-to-all-start = ((f32[8,24,1792]{2,1,0:T(8,128)}), f32[8,24,1792]{2,1,0:T(8,128)S(1)}, u32[]{:S(2)}, u32[]{:S(2)}) async-start(f32[8,24,1792]{2,1,0:T(8,128)} %get-tuple-element.11), calls=%async_computation | async-start | bytes 2752512 | tf_op jit(solution)/shard_map/all_to_all | solution.py:316
  50.3 19.0 %copy-start.4 = (f32[3584]{0:T(1024)S(1)}, f32[3584]{0:T(1024)}, u32[]{:S(2)}) copy-start(f32[3584]{0:T(1024)} %param.12) | copy-start | bytes 43012
  50.3 22.5 %copy-start.5 = (s32[16]{0:T(128)S(1)}, s32[16]{0:T(128)}, u32[]{:S(2)}) copy-start(s32[16]{0:T(128)} %param.15) | copy-start | bytes 196
  50.5 18.5 %all-to-all-start.1 = ((bf16[8,24,1792]{2,1,0:T(8,128)(2,1)}), bf16[8,24,1792]{2,1,0:T(8,128)(2,1)S(1)}, u32[]{:S(2)}, u32[]{:S(2)}) async-start(bf16[8,24,1792]{2,1,0:T(8,128)(2,1)} %probe.1), calls=%async_computation.1 | async-start | bytes 1376256 | tf_op jit(solution)/shard_map/all_to_all | solution.py:316
  57.1 99.9 %all-gather.2.cloned.1.call-start = ((), (), s32[]{:S(2)}) async-start(), calls=%async_computation.4 | async-start | bytes 11581440 | tf_op jit(solution)/shard_map/all_gather | solution.py:364
  70.3 31.6 %collective-permute-start = (bf16[3584,768]{1,0:T(8,128)(2,1)}, bf16[3584,768]{1,0:T(8,128)(2,1)}, u32[]{:S(2)}, u32[]{:S(2)}) collective-permute-start(bf16[3584,768]{1,0:T(8,128)(2,1)} %own_hbm.1), channel_id=1, source_target_pairs={{0,8},{8,0},{1,9},{9,1},{2,10},{10,2},{3,11},{11,3},{4,12},{12,4},... | collective-permute-start | bytes 16515080 | tf_op jit(solution)/shard_map/ppermute | solution.py:343
  181.4 13.2 %all-to-all-start.2 = ((f32[8,2,1536]{2,1,0:T(2,128)}), f32[8,2,1536]{2,1,0:T(2,128)S(1)}, u32[]{:S(2)}, u32[]{:S(2)}) async-start(f32[8,2,1536]{2,1,0:T(2,128)} %vocabulary_stats.1), calls=%async_computation.2 | async-start | bytes 196608 | tf_op jit(solution)/shard_map/all_to_all | solution.py:323
  195.5 8.6 %all-to-all-start.3 = ((f32[8,2,1536]{2,1,0:T(2,128)}), f32[8,2,1536]{2,1,0:T(2,128)S(1)}, u32[]{:S(2)}, u32[]{:S(2)}) async-start(f32[8,2,1536]{2,1,0:T(2,128)} %broadcast_in_dim.19), calls=%async_computation.3 | async-start | bytes 196608 | tf_op jit(solution)/shard_map/all_to_all | solution.py:323
  204.7 4.1 %collective-permute-start.1 = (f32[8,2]{0,1:T(2,128)S(1)}, f32[8,2]{0,1:T(2,128)S(1)}, u32[]{:S(2)}, u32[]{:S(2)}) collective-permute-start(f32[8,2]{0,1:T(2,128)S(1)} %broadcast_divide_fusion), channel_id=1, source_target_pairs={{0,8},{8,0},{1,9},{9,1},{2,10},{10,2},{3,11},{11,3},{4,12},{12,4},... | collective-permute-start | bytes 200 | tf_op jit(solution)/shard_map/ppermute | solution.py:377
  208.9 8.1 %copy-start.6 = (f32[32]{0:T(128)}, f32[32]{0:T(128)S(1)}, u32[]{:S(2)}) copy-start(f32[32]{0:T(128)S(1)} %select_n.37) | copy-start | bytes 388
  209.2 7.8 %copy-start.1 = (s32[1,128]{1,0:T(1,128)S(1)}, s32[1,128]{1,0:T(1,128)}, u32[]{:S(2)}) copy-start(s32[1,128]{1,0:T(1,128)} %param.14) | copy-start | bytes 1540
Sparse Core Ops, SparseCore 0:
  70.4 86.5 all-gather.1

commit v7 on v6

--- a/solution.py
+++ b/solution.py
@@ -227,7 +227,7 @@
         out_ref[t] = both
 
 
-def vocabulary_stats(rows, own_head, other_head, firsts, copies, chunk=256, slots=4):
+def vocabulary_stats(rows, own_head, other_head, firsts, copies, chunk=512, slots=3):
     count = rows.shape[0]
     vocab = own_head.shape[1]
     return pl.pallas_call(

time: 224 us -> 225 us (level)
  no operation moved by 1% of the time
where the time goes in v7:
time: 225 us; the launch traced here: 224 us
  Pallas kernels  92.8 us (41%)
  waiting for transfers between devices  78.7 us (35%)
  starting transfers between devices  30.9 us (14%)
  between operations  14.3 us (6%)
  local copies, waits for them, and re-layouts  4.5 us (2%)
  other arithmetic  3.21 us (1%)
    all_gather x1, waiting for transfers between devices, local(): lax.all_gather(normed.reshape(2 * share, D + EXTRA), SAME_CORE, axis=0, t...  55.1 us
    pallas_call x1, Pallas kernels, regenerate(): pl.pallas_call(functools.partial(regenerate_kernel, out_rows=rows), grid=...  28.1 us
    pallas_call x1, Pallas kernels, vocabulary_stats(): pl.pallas_call(logits_kernel, in_specs=[pl.BlockSpec(memory_space=pltpu.S...  24.7 us
    pallas_call x1, Pallas kernels, products(): pl.pallas_call(functools.partial(rest_kernel, first_step=first_steps), gr...  23 us
    all_to_all x2, starting transfers between devices, scattered_sum(): pieces = lax.all_to_all(partial, axes, 0, 0)  15.2 us
    all_to_all x2, waiting for transfers between devices, joined(): everyone = lax.all_to_all(stats, axes, 0, 0)  11.9 us
    all_to_all x2, waiting for transfers between devices, scattered_sum(): pieces = lax.all_to_all(partial, axes, 0, 0)  10.8 us
    all_to_all x2, starting transfers between devices, joined(): everyone = lax.all_to_all(stats, axes, 0, 0)  9.92 us
  transfers between devices with their start and end apart: 7, of which 5 were waited for; matrix products, arithmetic and copies ran while one was open for 1% of the time, Pallas kernels for 23%

profile of v7, /device:TPU:1, one launch (start us, length us, event | category | flops | bytes accessed | tf_op | source)
XLA Modules:
  0.0 224.4 jit_solution(15849049920363732141)
XLA Ops:
  7.2 1.4 copy.25
  8.6 0.6 copy-done.2
  9.2 9.3 %base_and_probe.1 = (bf16[8,24,1792]{2,1,0:T(8,128)(2,1)}, f32[8,24,1792]{2,1,0:T(8,128)}) custom-call(s32[16]{0:T(128)S(1)} %copy-done.2, bf16[128,2368]{1,0:T(8,128)(2,1)S(1)} %bitcast.24, bf16[2368,3584]{1,0:T(8,128)(2,1)} %weight_hbm.1), custom_call_target="tpu_custom_call" | custom-call | flops 2424832000 | bytes 1212416 | tf_op jit(solution)/shard_map/base_and_probe/pallas_call | solution.py:106
  18.5 8.5 %all-to-all-start = ((f32[8,24,1792]{2,1,0:T(8,128)}), f32[8,24,1792]{2,1,0:T(8,128)S(1)}, u32[]{:S(2)}, u32[]{:S(2)}) async-start(f32[8,24,1792]{2,1,0:T(8,128)} %get-tuple-element.11), calls=%async_computation | async-start | bytes 2752512 | tf_op jit(solution)/shard_map/all_to_all | solution.py:316
  27.3 23.0 %probe.1 = bf16[8,24,1792]{2,1,0:T(8,128)(2,1)} custom-call(s32[16]{0:T(128)S(1)} %copy-done.3, bf16[128,2368]{1,0:T(8,128)(2,1)S(1)} %bitcast.25, bf16[8,24,1792]{2,1,0:T(8,128)(2,1)} %get-tuple-element.10._), custom_call_target="tpu_custom_call", output_to_operand_aliasing={{}: (2, {})} | custom-call | flops 14548992000 | bytes 7274496 | tf_op jit(solution)/shard_map/probe/pallas_call | solution.py:120
  50.5 6.7 %all-to-all-start.1 = ((bf16[8,24,1792]{2,1,0:T(8,128)(2,1)}), bf16[8,24,1792]{2,1,0:T(8,128)(2,1)S(1)}, u32[]{:S(2)}, u32[]{:S(2)}) async-start(bf16[8,24,1792]{2,1,0:T(8,128)(2,1)} %probe.1), calls=%async_computation.1 | async-start | bytes 1376256 | tf_op jit(solution)/shard_map/all_to_all | solution.py:316
  57.2 1.0 convert_add_fusion
  58.1 10.8 %all-to-all-done.1 = bf16[8,24,1792]{2,1,0:T(8,128)(2,1)S(1)} async-done(((bf16[8,24,1792]{2,1,0:T(8,128)(2,1)}), bf16[8,24,1792]{2,1,0:T(8,128)(2,1)S(1)}, u32[]{:S(2)}, u32[]{:S(2)}) %all-to-all-start.1) | async-done | bytes 688160 | tf_op jit(solution)/shard_map/all_to_all | solution.py:316
  69.0 0.1 convert_reduce_fusion
  69.1 0.2 multiply_reduce_fusion
  69.4 0.1 multiply_convert_fusion
  69.6 0.7 reshape.183
  70.3 2.5 %collective-permute-start = (bf16[3584,768]{1,0:T(8,128)(2,1)}, bf16[3584,768]{1,0:T(8,128)(2,1)}, u32[]{:S(2)}, u32[]{:S(2)}) collective-permute-start(bf16[3584,768]{1,0:T(8,128)(2,1)} %own_hbm.1), channel_id=1, source_target_pairs={{0,8},{8,0},{1,9},{9,1},{2,10},{10,2},{3,11},{11,3},{4,12},{12,4},... | collective-permute-start | bytes 16515080 | tf_op jit(solution)/shard_map/ppermute | solution.py:343
  72.9 0.2 dynamic-slice_reduce_fusion
  73.1 0.6 pad_add_fusion.first_ref
  73.8 28.1 %regenerate.1.noise_hbm = bf16[7,2368,512]{2,1,0:T(8,128)(2,1)} custom-call(s32[16,1]{1,0:T(8,128)S(1)} %copy.26.seeds_ref), custom_call_target="tpu_custom_call" | custom-call | flops 16973824000 | bytes 16973824 | tf_op jit(solution)/shard_map/regenerate/pallas_call | solution.py:147
  101.9 55.1 %all-gather.2.cloned.1.call-done.rows_hbm = bf16[1536,3712]{1,0:T(8,128)(2,1)} async-done(((bf16[24,3712]{1,0:T(8,128)(2,1)}), bf16[1536,3712]{1,0:T(8,128)(2,1)}) %all-gather.2.cloned.1.call-update) | async-done | bytes 11403280 | tf_op jit(solution)/shard_map/all_gather | solution.py:364
  157.0 24.7 %vocabulary_stats.1 = f32[8,2,1536]{2,1,0:T(2,128)} custom-call(s32[2]{0:T(128)} %pad_add_fusion.first_ref, bf16[1536,3712]{1,0:T(8,128)(2,1)} %all-gather.2.cloned.1.call-done.rows_hbm, bf16[3584,768]{1,0:T(8,128)(2,1)} %own_hbm.1, bf16[3584,768]{1,0:T(8,128)(2,1)} %collective-permute-done.other_hbm), custom_call_target="tpu_custom_call" | custom-call | flops 16911433728 | bytes 11010048 | tf_op jit(solution)/shard_map/vocabulary_stats/pallas_call | solution.py:233
  181.7 6.6 %all-to-all-start.2 = ((f32[8,2,1536]{2,1,0:T(2,128)}), f32[8,2,1536]{2,1,0:T(2,128)S(1)}, u32[]{:S(2)}, u32[]{:S(2)}) async-start(f32[8,2,1536]{2,1,0:T(2,128)} %vocabulary_stats.1), calls=%async_computation.2 | async-start | bytes 196608 | tf_op jit(solution)/shard_map/all_to_all | solution.py:323
  188.2 6.9 %all-to-all-done.2 = f32[8,2,1536]{2,1,0:T(2,128)S(1)} async-done(((f32[8,2,1536]{2,1,0:T(2,128)}), f32[8,2,1536]{2,1,0:T(2,128)S(1)}, u32[]{:S(2)}, u32[]{:S(2)}) %all-to-all-start.2) | async-done | bytes 98336 | tf_op jit(solution)/shard_map/all_to_all | solution.py:323
  195.1 0.1 slice_reduce_fusion.3
  195.4 0.7 broadcast_in_dim.19
  196.0 3.4 %all-to-all-start.3 = ((f32[8,2,1536]{2,1,0:T(2,128)}), f32[8,2,1536]{2,1,0:T(2,128)S(1)}, u32[]{:S(2)}, u32[]{:S(2)}) async-start(f32[8,2,1536]{2,1,0:T(2,128)} %broadcast_in_dim.19), calls=%async_computation.3 | async-start | bytes 196608 | tf_op jit(solution)/shard_map/all_to_all | solution.py:323
  199.5 0.2 convert_reduce_fusion.1
  199.7 5.0 %all-to-all-done.3 = f32[8,2,1536]{2,1,0:T(2,128)S(1)} async-done(((f32[8,2,1536]{2,1,0:T(2,128)}), f32[8,2,1536]{2,1,0:T(2,128)S(1)}, u32[]{:S(2)}, u32[]{:S(2)}) %all-to-all-start.3) | async-done | bytes 98336 | tf_op jit(solution)/shard_map/all_to_all | solution.py:323
  204.6 0.1 slice_reduce_fusion.2
  204.8 0.1 sub.46
  204.9 0.1 multiply_reduce_fusion.1
  205.2 3.3 %collective-permute-start.1 = (f32[8,2]{0,1:T(2,128)S(1)}, f32[8,2]{0,1:T(2,128)S(1)}, u32[]{:S(2)}, u32[]{:S(2)}) collective-permute-start(f32[8,2]{0,1:T(2,128)S(1)} %broadcast_divide_fusion), channel_id=1, source_target_pairs={{0,8},{8,0},{1,9},{9,1},{2,10},{10,2},{3,11},{11,3},{4,12},{12,4},... | collective-permute-start | bytes 200 | tf_op jit(solution)/shard_map/ppermute | solution.py:377
  208.4 0.8 collective-permute-done.1
  209.5 0.1 reduce_sum.92
  209.8 7.7 %update.1 = f32[148,3584]{1,0:T(8,128)} custom-call(f32[1,256]{1,0:T(1,128)S(1)} %reshape_tile.3.gap_ref, bf16[7,2368,512]{2,1,0:T(8,128)(2,1)} %regenerate.1.noise_hbm), custom_call_target="tpu_custom_call" | custom-call | flops 16973824 | bytes 16973824 | tf_op jit(solution)/shard_map/update/pallas_call | solution.py:298
  (53 shorter events, 1.3 us)
Async XLA Ops:
  7.2 19.9 %copy-start = (s32[1,128]{1,0:T(1,128)S(1)}, s32[1,128]{1,0:T(1,128)}, u32[]{:S(2)}) copy-start(s32[1,128]{1,0:T(1,128)} %param.14) | copy-start | bytes 1540
  8.6 0.7 copy-start.2
  9.2 17.8 %copy-start.7 = (s32[32]{0:T(128)S(1)}, s32[32]{0:T(128)}, u32[]{:S(2)}) copy-start(s32[32]{0:T(128)} %param.17) | copy-start | bytes 388
  9.2 18.1 %copy-start.3 = (s32[16]{0:T(128)S(1)}, s32[16]{0:T(128)}, u32[]{:S(2)}) copy-start(s32[16]{0:T(128)} %seeds_ref.3) | copy-start | bytes 196
  18.5 31.8 %all-to-all-start = ((f32[8,24,1792]{2,1,0:T(8,128)}), f32[8,24,1792]{2,1,0:T(8,128)S(1)}, u32[]{:S(2)}, u32[]{:S(2)}) async-start(f32[8,24,1792]{2,1,0:T(8,128)} %get-tuple-element.11), calls=%async_computation | async-start | bytes 2752512 | tf_op jit(solution)/shard_map/all_to_all | solution.py:316
  50.3 19.0 %copy-start.4 = (f32[3584]{0:T(1024)S(1)}, f32[3584]{0:T(1024)}, u32[]{:S(2)}) copy-start(f32[3584]{0:T(1024)} %param.12) | copy-start | bytes 43012
  50.3 22.5 %copy-start.5 = (s32[16]{0:T(128)S(1)}, s32[16]{0:T(128)}, u32[]{:S(2)}) copy-start(s32[16]{0:T(128)} %param.15) | copy-start | bytes 196
  50.5 18.5 %all-to-all-start.1 = ((bf16[8,24,1792]{2,1,0:T(8,128)(2,1)}), bf16[8,24,1792]{2,1,0:T(8,128)(2,1)S(1)}, u32[]{:S(2)}, u32[]{:S(2)}) async-start(bf16[8,24,1792]{2,1,0:T(8,128)(2,1)} %probe.1), calls=%async_computation.1 | async-start | bytes 1376256 | tf_op jit(solution)/shard_map/all_to_all | solution.py:316
  57.1 99.9 %all-gather.2.cloned.1.call-start = ((), (), s32[]{:S(2)}) async-start(), calls=%async_computation.4 | async-start | bytes 11581440 | tf_op jit(solution)/shard_map/all_gather | solution.py:364
  70.3 31.6 %collective-permute-start = (bf16[3584,768]{1,0:T(8,128)(2,1)}, bf16[3584,768]{1,0:T(8,128)(2,1)}, u32[]{:S(2)}, u32[]{:S(2)}) collective-permute-start(bf16[3584,768]{1,0:T(8,128)(2,1)} %own_hbm.1), channel_id=1, source_target_pairs={{0,8},{8,0},{1,9},{9,1},{2,10},{10,2},{3,11},{11,3},{4,12},{12,4},... | collective-permute-start | bytes 16515080 | tf_op jit(solution)/shard_map/ppermute | solution.py:343
  181.7 13.4 %all-to-all-start.2 = ((f32[8,2,1536]{2,1,0:T(2,128)}), f32[8,2,1536]{2,1,0:T(2,128)S(1)}, u32[]{:S(2)}, u32[]{:S(2)}) async-start(f32[8,2,1536]{2,1,0:T(2,128)} %vocabulary_stats.1), calls=%async_computation.2 | async-start | bytes 196608 | tf_op jit(solution)/shard_map/all_to_all | solution.py:323
  196.0 8.6 %all-to-all-start.3 = ((f32[8,2,1536]{2,1,0:T(2,128)}), f32[8,2,1536]{2,1,0:T(2,128)S(1)}, u32[]{:S(2)}, u32[]{:S(2)}) async-start(f32[8,2,1536]{2,1,0:T(2,128)} %broadcast_in_dim.19), calls=%async_computation.3 | async-start | bytes 196608 | tf_op jit(solution)/shard_map/all_to_all | solution.py:323
  205.2 4.1 %collective-permute-start.1 = (f32[8,2]{0,1:T(2,128)S(1)}, f32[8,2]{0,1:T(2,128)S(1)}, u32[]{:S(2)}, u32[]{:S(2)}) collective-permute-start(f32[8,2]{0,1:T(2,128)S(1)} %broadcast_divide_fusion), channel_id=1, source_target_pairs={{0,8},{8,0},{1,9},{9,1},{2,10},{10,2},{3,11},{11,3},{4,12},{12,4},... | collective-permute-start | bytes 200 | tf_op jit(solution)/shard_map/ppermute | solution.py:377
  209.4 8.1 %copy-start.6 = (f32[32]{0:T(128)}, f32[32]{0:T(128)S(1)}, u32[]{:S(2)}) copy-start(f32[32]{0:T(128)S(1)} %select_n.37) | copy-start | bytes 388
  209.7 7.8 %copy-start.1 = (s32[1,128]{1,0:T(1,128)S(1)}, s32[1,128]{1,0:T(1,128)}, u32[]{:S(2)}) copy-start(s32[1,128]{1,0:T(1,128)} %param.14) | copy-start | bytes 1540
Sparse Core Ops, SparseCore 0:
  70.4 86.5 all-gather.1
